TPU v7x, 128 devices: a whole 4x4x4 slice. The times are simulated.
128 devices in a mesh: dp: 8 (over y, x_lo), tm: 16 (over z, x_hi, core).
Axes of the slice: x: 4 (x_hi: 2, x_lo: 2; x = x_hi * 2 + x_lo), y: 4, z: 4, core: 2. Of those that a mesh axis runs over, the one named last changes fastest.
Arguments:
- queries: bfloat16 [8, 16, 256, 16, 128], P('dp', 'tm'), may hold values from -200 to 200
- keys: bfloat16 [8, 16, 256, 16, 128], P('dp', 'tm'), may hold values from -6.5 to 6.5
- values: bfloat16 [8, 16, 256, 16, 128], P('dp', 'tm'), may hold values from -6 to 6
- out_weight: bfloat16 [2048, 16, 128], replicated, may hold values from -0.125 to 0.125
- grad_out: bfloat16 [8, 16, 256, 2048], P('dp', 'tm'), may hold values from -6 to 6
Outputs:
- grad_queries: bfloat16 [8, 16, 256, 16, 128], P('dp', 'tm')
- grad_keys: bfloat16 [8, 16, 256, 16, 128], P('dp', 'tm')
- grad_values: bfloat16 [8, 16, 256, 16, 128], P('dp', 'tm')
- grad_weight: float32 [2048, 16, 128], P(('dp', 'tm'))
All inputs are finite; a program needn't handle non-finite values.
Results may differ from a plain program's by a relative error of at most 0.0058.
Values may be sent and summed in bfloat16 or wider, within the bound.
No kernel may reach another device: no remote copies, remote signals or barrier semaphores. Data moves between devices by JAX's collectives and lax.ppermute only.
A program may use at most 128 MiB of HBM per device.

v0:
```python
import jax
import jax.numpy as jnp
from jax import lax
from jax.sharding import PartitionSpec as P


def attend(queries, keys, values, grad_attended):
    scale = 1.0 / jnp.sqrt(jnp.float32(queries.shape[4]))
    frames = queries.shape[1]
    scores = (
        jnp.einsum("biphe,bjphe->bphij", queries, keys, preferred_element_type=jnp.float32) * scale
    )
    frame_ids = jnp.arange(frames)
    causal = frame_ids[None, :] <= frame_ids[:, None]
    masked = jnp.where(causal, scores, -jnp.inf)
    top = jnp.max(masked, axis=-1, keepdims=True)
    expd = jnp.where(causal, jnp.exp(masked - top), 0.0)
    probs = expd / jnp.sum(expd, axis=-1, keepdims=True)
    weights = probs.astype(jnp.bfloat16)
    attended = jnp.einsum(
        "bphij,bjphe->biphe", weights, values, preferred_element_type=jnp.float32
    ).astype(jnp.bfloat16)
    grad_values = jnp.einsum(
        "bphij,biphe->bjphe", weights, grad_attended, preferred_element_type=jnp.float32
    ).astype(jnp.bfloat16)
    grad_probs = jnp.einsum(
        "biphe,bjphe->bphij", grad_attended, values, preferred_element_type=jnp.float32
    )
    delta = jnp.sum(probs * grad_probs, axis=-1, keepdims=True)
    grad_scores = (probs * (grad_probs - delta)).astype(jnp.bfloat16)
    grad_queries = (
        jnp.einsum("bphij,bjphe->biphe", grad_scores, keys, preferred_element_type=jnp.float32)
        * scale
    ).astype(jnp.bfloat16)
    grad_keys = (
        jnp.einsum("bphij,biphe->bjphe", grad_scores, queries, preferred_element_type=jnp.float32)
        * scale
    ).astype(jnp.bfloat16)
    return (attended, grad_queries, grad_keys, grad_values)


def shards(queries, keys, values, out_weight, grad_out):
    q_tok, k_tok, v_tok = (
        lax.all_to_all(queries, "tm", split_axis=2, concat_axis=1, tiled=True),
        lax.all_to_all(keys, "tm", split_axis=2, concat_axis=1, tiled=True),
        lax.all_to_all(values, "tm", split_axis=2, concat_axis=1, tiled=True),
    )
    grad_attended = jnp.einsum(
        "bfpd,dhe->bfphe", grad_out, out_weight, preferred_element_type=jnp.float32
    ).astype(jnp.bfloat16)
    g_tok = lax.all_to_all(grad_attended, "tm", split_axis=2, concat_axis=1, tiled=True)
    results = attend(q_tok, k_tok, v_tok, g_tok)
    attended, grad_queries, grad_keys, grad_values = (
        lax.all_to_all(results[0], "tm", split_axis=1, concat_axis=2, tiled=True),
        lax.all_to_all(results[1], "tm", split_axis=1, concat_axis=2, tiled=True),
        lax.all_to_all(results[2], "tm", split_axis=1, concat_axis=2, tiled=True),
        lax.all_to_all(results[3], "tm", split_axis=1, concat_axis=2, tiled=True),
    )
    grad_weight = lax.psum_scatter(
        jnp.einsum("bfpd,bfphe->dhe", grad_out, attended, preferred_element_type=jnp.float32),
        ("dp", "tm"),
        scatter_dimension=0,
        tiled=True,
    )
    return (grad_queries, grad_keys, grad_values, grad_weight)


def solution(mesh):
    placed = (
        P("dp", "tm", None, None, None),
        P("dp", "tm", None, None, None),
        P("dp", "tm", None, None, None),
        P(),
        P("dp", "tm", None, None),
    )
    return jax.shard_map(
        shards,
        mesh=mesh,
        in_specs=placed,
        out_specs=(
            P("dp", "tm", None, None, None),
            P("dp", "tm", None, None, None),
            P("dp", "tm", None, None, None),
            P(("dp", "tm"), None, None),
        ),
        check_vma=False,
    )
```

profile of v0, /device:TPU:1, one launch (start us, length us, event | category | flops | bytes accessed | tf_op | source)
XLA Modules:
  0.0 832.3 jit_solution(17693138738484804999)
XLA Ops:
  7.2 0.0 copy-start
  7.2 0.0 copy-start.5
  7.2 26.3 %all_to_all.81 = bf16[1,1,256,16,128]{4,3,1,0,2:T(8,128)(2,1)S(1)} all-to-all(bf16[1,1,256,16,128]{4,3,1,0,2:T(8,128)(2,1)} %bitcast.52), channel_id=1, replica_groups=mesh['dp'=8,'tm'=16] {'tm'}, dimensions={2} | all-to-all | bytes 2097152 | tf_op jit(solution)/shard_map/all_to_all | solution.py:44
  33.5 0.0 copy-start.1
  33.5 0.0 copy-done.5
  33.5 20.6 %all_to_all.82 = bf16[1,1,256,16,128]{4,3,1,0,2:T(8,128)(2,1)S(1)} all-to-all(bf16[1,1,256,16,128]{4,3,1,0,2:T(8,128)(2,1)S(1)} %bitcast.53), channel_id=1, replica_groups=mesh['dp'=8,'tm'=16] {'tm'}, dimensions={2} | all-to-all | bytes 2097152 | tf_op jit(solution)/shard_map/all_to_all | solution.py:45
  54.1 5.2 all-to-all-start.3
  59.4 0.0 reduce-scatter.2.cloned.1.call-start
  59.4 0.0 copy-done.1
  59.4 3.3 fusion.34
  62.8 14.0 %all-to-all-done.3 = bf16[1,1,256,16,128]{4,3,1,0,2:T(8,128)(2,1)} async-done(((bf16[1,1,256,16,128]{4,3,1,0,2:T(8,128)(2,1)}), bf16[1,1,256,16,128]{4,3,1,0,2:T(8,128)(2,1)}, u32[]{:S(2)}, u32[]{:S(2)}) %all-to-all-start.3) | async-done | bytes 1048608 | tf_op jit(solution)/shard_map/all_to_all | solution.py:46
  76.8 2.7 fusion.10
  79.5 0.3 copy.69
  79.8 20.4 %all_to_all.83 = bf16[1,16,16,16,128]{4,3,2,0,1:T(8,128)(2,1)S(1)} all-to-all(bf16[1,16,16,16,128]{4,3,2,0,1:T(8,128)(2,1)S(1)} %copy.69), channel_id=1, replica_groups=mesh['dp'=8,'tm'=16] {'tm'}, dimensions={1} | all-to-all | bytes 2097152 | tf_op jit(solution)/shard_map/all_to_all | solution.py:54
  100.1 0.0 copy-done
  100.1 8.1 convolution_bitcast_fusion
  108.3 17.7 %copy.71 = f32[2048,16,128]{2,1,0:T(8,128)} copy(f32[2048,16,128]{0,2,1:T(8,128)} %convolution_bitcast_fusion) | data formatting | bytes 33554432 | tf_op jit(solution)/shard_map/bfpd,bfphe->dhe/dot_general | solution.py:60
  125.9 0.0 reduce-scatter.2.cloned.1.call-update
  126.0 5.7 fusion.7
  131.7 0.0 copy-start.3
  131.7 0.7 copy.56
  132.4 23.6 %all_to_all.84 = bf16[1,1,256,16,128]{4,3,1,0,2:T(8,128)(2,1)S(1)} all-to-all(bf16[1,1,256,16,128]{4,3,1,0,2:T(8,128)(2,1)S(1)} %copy.56), channel_id=1, replica_groups=mesh['dp'=8,'tm'=16] {'tm'}, dimensions={2} | all-to-all | bytes 2097152 | tf_op jit(solution)/shard_map/all_to_all | solution.py:51
  156.0 0.0 copy-done.3
  156.0 0.9 fusion.11
  156.9 1.3 copy.66
  158.2 6.6 all-to-all-start.6
  164.8 0.0 copy-start.4
  164.8 3.7 multiply_reduce_fusion
  168.4 0.0 copy-done.4
  168.5 0.0 copy-start.2
  168.5 0.6 multiply_convert_fusion.2
  169.1 0.6 copy-done.2
  169.7 0.9 fusion.13
  170.6 1.2 copy.64
  171.8 11.3 %all-to-all-done.6 = bf16[1,16,16,16,128]{4,3,2,0,1:T(8,128)(2,1)} async-done(((bf16[1,16,16,16,128]{4,3,2,0,1:T(8,128)(2,1)}), bf16[1,16,16,16,128]{4,3,2,0,1:T(8,128)(2,1)}, u32[]{:S(2)}, u32[]{:S(2)}) %all-to-all-start.6) | async-done | bytes 1048608 | tf_op jit(solution)/shard_map/all_to_all | solution.py:57
  183.2 8.0 all-to-all-start.5
  191.1 0.9 fusion.12
  192.0 1.2 copy.62
  193.3 16.4 %all-to-all-done.5 = bf16[1,16,16,16,128]{4,3,2,0,1:T(8,128)(2,1)} async-done(((bf16[1,16,16,16,128]{4,3,2,0,1:T(8,128)(2,1)}), bf16[1,16,16,16,128]{4,3,2,0,1:T(8,128)(2,1)}, u32[]{:S(2)}, u32[]{:S(2)}) %all-to-all-start.5) | async-done | bytes 1048608 | tf_op jit(solution)/shard_map/all_to_all | solution.py:56
  209.6 5.5 all-to-all-start.4
  215.1 18.1 %all-to-all-done.4 = bf16[1,16,16,16,128]{4,3,2,0,1:T(8,128)(2,1)S(1)} async-done(((bf16[1,16,16,16,128]{4,3,2,0,1:T(8,128)(2,1)}), bf16[1,16,16,16,128]{4,3,2,0,1:T(8,128)(2,1)S(1)}, u32[]{:S(2)}, u32[]{:S(2)}) %all-to-all-start.4) | async-done | bytes 1048608 | tf_op jit(solution)/shard_map/all_to_all | solution.py:55
  233.2 586.5 %reduce-scatter.2.cloned.1.call-done = f32[16,16,128]{2,1,0:T(8,128)} async-done(((f32[2048,16,128]{2,1,0:T(8,128)}), f32[16,16,128]{2,1,0:T(8,128)}) %reduce-scatter.2.cloned.1.call-update) | async-done | bytes 131088 | tf_op jit(solution)/shard_map/reduce_scatter | solution.py:59
  819.7 1.0 copy.113
  820.7 2.4 copy.114
  823.1 2.4 copy.115
  (1 shorter events, 0.0 us)
Async XLA Ops:
  7.2 93.0 %copy-start = (bf16[1,1,256,2048]{3,2,1,0:T(8,128)(2,1)S(1)}, bf16[1,1,256,2048]{3,2,1,0:T(8,128)(2,1)}, u32[]{:S(2)}) copy-start(bf16[1,1,256,2048]{3,2,1,0:T(8,128)(2,1)} %param.9) | copy-start | bytes 3145732
  7.2 26.4 %copy-start.5 = (bf16[1,1,256,16,128]{4,3,2,1,0:T(8,128)(2,1)S(1)}, bf16[1,1,256,16,128]{4,3,2,1,0:T(8,128)(2,1)}, u32[]{:S(2)}) copy-start(bf16[1,1,256,16,128]{4,3,2,1,0:T(8,128)(2,1)} %param.6) | copy-start | bytes 3145732
  33.5 25.9 %copy-start.1 = (bf16[1,1,256,16,128]{4,3,1,0,2:T(8,128)(2,1)}, bf16[1,1,256,16,128]{4,3,1,0,2:T(8,128)(2,1)S(1)}, u32[]{:S(2)}) copy-start(bf16[1,1,256,16,128]{4,3,1,0,2:T(8,128)(2,1)S(1)} %all_to_all.81) | copy-start | bytes 3145732
  54.1 22.6 %all-to-all-start.3 = ((bf16[1,1,256,16,128]{4,3,1,0,2:T(8,128)(2,1)}), bf16[1,1,256,16,128]{4,3,1,0,2:T(8,128)(2,1)}, u32[]{:S(2)}, u32[]{:S(2)}) async-start(bf16[1,1,256,16,128]{4,3,1,0,2:T(8,128)(2,1)} %bitcast.54), calls=%async_computation.3 | async-start | bytes 2097152 | tf_op jit(solution)/shard_map/all_to_all | solution.py:46
  59.4 760.4 %reduce-scatter.2.cloned.1.call-start = ((), (), s32[]{:S(2)}) async-start(), calls=%async_computation.9 | async-start | bytes 16908288 | tf_op jit(solution)/shard_map/reduce_scatter | solution.py:59
  131.7 24.3 %copy-start.3 = (f32[16,16,16,16]{2,3,1,0:T(8,128)S(1)}, f32[16,16,16,16]{2,3,1,0:T(8,128)}, u32[]{:S(2)}) copy-start(f32[16,16,16,16]{2,3,1,0:T(8,128)} %get-tuple-element.13) | copy-start | bytes 786436
  158.2 25.0 %all-to-all-start.6 = ((bf16[1,16,16,16,128]{4,3,2,0,1:T(8,128)(2,1)}), bf16[1,16,16,16,128]{4,3,2,0,1:T(8,128)(2,1)}, u32[]{:S(2)}, u32[]{:S(2)}) async-start(bf16[1,16,16,16,128]{4,3,2,0,1:T(8,128)(2,1)} %copy.66), calls=%async_computation.6 | async-start | bytes 2097152 | tf_op jit(solution)/shard_map/all_to_all | solution.py:57
  164.8 3.7 copy-start.4
  168.5 1.2 copy-start.2
  183.2 26.5 %all-to-all-start.5 = ((bf16[1,16,16,16,128]{4,3,2,0,1:T(8,128)(2,1)}), bf16[1,16,16,16,128]{4,3,2,0,1:T(8,128)(2,1)}, u32[]{:S(2)}, u32[]{:S(2)}) async-start(bf16[1,16,16,16,128]{4,3,2,0,1:T(8,128)(2,1)} %copy.64), calls=%async_computation.5 | async-start | bytes 2097152 | tf_op jit(solution)/shard_map/all_to_all | solution.py:56
  209.6 23.5 %all-to-all-start.4 = ((bf16[1,16,16,16,128]{4,3,2,0,1:T(8,128)(2,1)}), bf16[1,16,16,16,128]{4,3,2,0,1:T(8,128)(2,1)S(1)}, u32[]{:S(2)}, u32[]{:S(2)}) async-start(bf16[1,16,16,16,128]{4,3,2,0,1:T(8,128)(2,1)} %copy.62), calls=%async_computation.4 | async-start | bytes 2097152 | tf_op jit(solution)/shard_map/all_to_all | solution.py:55
Sparse Core Ops, SparseCore 0:
  126.1 693.5 reduce-scatter.1
where the time goes:
time: 840 us; the launch traced here: 832 us
  waiting for transfers between devices  646 us (77%)
  blocking collectives  90.9 us (11%)
  local copies, waits for them, and re-layouts  28.7 us (3%)
  matrix products  26.3 us (3%)
  starting transfers between devices  25.3 us (3%)
  between operations  14.2 us (2%)
    reduce_scatter x1, waiting for transfers between devices, shards(): lax.psum_scatter(jnp.einsum('bfpd,bfphe->dhe', grad_out, attended, prefer...  587 us
    all_to_all x1, blocking collectives, shards(): lax.all_to_all(queries, 'tm', split_axis=2, concat_axis=1, tiled=True)  26.3 us
    all_to_all x1, blocking collectives, shards(): lax.all_to_all(grad_attended, 'tm', split_axis=2, concat_axis=1, tiled=True)  23.6 us
    all_to_all x1, blocking collectives, shards(): lax.all_to_all(keys, 'tm', split_axis=2, concat_axis=1, tiled=True)  20.6 us
    all_to_all x1, blocking collectives, shards(): lax.all_to_all(results[0], 'tm', split_axis=1, concat_axis=2, tiled=True)  20.4 us
    all_to_all x1, waiting for transfers between devices, shards(): lax.all_to_all(results[1], 'tm', split_axis=1, concat_axis=2, tiled=True)  18.1 us
    dot_general x1, local copies, waits for them, and re-layouts, shards(): jnp.einsum('bfpd,bfphe->dhe', grad_out, attended, preferred_element_type=...  17.7 us
  transfers between devices with their start and end apart: 5, of which 5 were waited for; matrix products, arithmetic and copies ran while one was open for 2% of the time, Pallas kernels for 0%

commit v1 on v0

v1 whole, which is shorter than its diff:
```python
import jax
import jax.numpy as jnp
from jax import lax
from jax.experimental import pallas as pl
from jax.experimental.pallas import tpu as pltpu
from jax.sharding import PartitionSpec as P

FRAMES, TOK, HEADS, E, DM = 16, 16, 16, 128, 2048
PATCH = 256
ROWS = FRAMES * HEADS
AXES = ("dp", "tm")
SCALE = 1.0 / (E**0.5)
Y, CORES_IN_PLANE = 4, 32
YROWS = DM // Y


def y_shift(n):
    total = Y * CORES_IN_PLANE
    return [(i, (i + n * CORES_IN_PLANE) % total) for i in range(total)]


def planes():
    return [[y * CORES_IN_PLANE + i for i in range(CORES_IN_PLANE)] for y in range(Y)]


def dot_nt(a, b):
    return lax.dot_general(a, b, (((1,), (1,)), ((), ())), preferred_element_type=jnp.float32)


def dot_tn(a, b):
    return lax.dot_general(a, b, (((0,), (0,)), ((), ())), preferred_element_type=jnp.float32)


def dot_nn(a, b):
    return lax.dot_general(a, b, (((1,), (0,)), ((), ())), preferred_element_type=jnp.float32)


def attend_kernel(q_ref, k_ref, v_ref, g_ref, a_ref, grads_ref):
    q = q_ref[...].reshape(ROWS, E)
    k = k_ref[...].reshape(ROWS, E)
    v = v_ref[...].reshape(ROWS, E)
    g = g_ref[...].reshape(ROWS, E)
    row = lax.broadcasted_iota(jnp.int32, (ROWS, ROWS), 0)
    col = lax.broadcasted_iota(jnp.int32, (ROWS, ROWS), 1)
    keep = (row % HEADS == col % HEADS) & (col <= row)
    scores = jnp.where(keep, dot_nt(q, k) * SCALE, -jnp.inf)
    top = jnp.max(scores, axis=1, keepdims=True)
    expd = jnp.exp(scores - top)
    probs = expd / jnp.sum(expd, axis=1, keepdims=True)
    weights = probs.astype(jnp.bfloat16)
    a_ref[...] = dot_nn(weights, v).astype(jnp.bfloat16).reshape(a_ref.shape)
    gv = dot_tn(weights, g).astype(jnp.bfloat16)
    gp = dot_nt(g, v)
    pg = probs * gp
    delta = jnp.sum(pg, axis=1, keepdims=True)
    gs = (probs * (gp - delta)).astype(jnp.bfloat16)
    gq = (dot_nn(gs, k) * SCALE).astype(jnp.bfloat16)
    gk = (dot_tn(gs, q) * SCALE).astype(jnp.bfloat16)
    block = (FRAMES, 1, 1, HEADS, E)
    grads_ref[:, 0:1] = gq.reshape(block)
    grads_ref[:, 1:2] = gk.reshape(block)
    grads_ref[:, 2:3] = gv.reshape(block)


def attend(packed, grad_attended):
    def part(n):
        return pl.BlockSpec((FRAMES, 1, 1, HEADS, E), lambda t, n=n: (0, n, t, 0, 0))

    token = pl.BlockSpec((FRAMES, 1, HEADS, E), lambda t: (0, t, 0, 0))
    return pl.pallas_call(
        attend_kernel,
        grid=(TOK,),
        in_specs=[part(0), part(1), part(2), token],
        out_specs=[token, pl.BlockSpec((FRAMES, 3, 1, HEADS, E), lambda t: (0, 0, t, 0, 0))],
        out_shape=[
            jax.ShapeDtypeStruct((FRAMES, TOK, HEADS, E), jnp.bfloat16),
            jax.ShapeDtypeStruct((FRAMES, 3, TOK, HEADS, E), jnp.bfloat16),
        ],
        compiler_params=pltpu.CompilerParams(vmem_limit_bytes=32 * 1024 * 1024),
    )(packed, packed, packed, grad_attended)


def weight_kernel(*refs):
    out = refs[-1]
    total = dot_tn(refs[0][...], refs[4][...])
    for n in range(1, Y):
        total = total + dot_tn(refs[n][...], refs[Y + n][...])
    out[...] = total.astype(jnp.bfloat16)


def weight_block(gs, atts):
    width = 512
    tokens = FRAMES * TOK
    return pl.pallas_call(
        weight_kernel,
        grid=(DM // width,),
        in_specs=[pl.BlockSpec((tokens, YROWS), lambda c: (0, 0))] * Y
        + [pl.BlockSpec((tokens, width), lambda c: (0, c))] * Y,
        out_specs=pl.BlockSpec((YROWS, width), lambda c: (0, c)),
        out_shape=jax.ShapeDtypeStruct((YROWS, DM), jnp.bfloat16),
        compiler_params=pltpu.CompilerParams(vmem_limit_bytes=32 * 1024 * 1024),
    )(*gs, *atts)


def shards(queries, keys, values, out_weight, grad_out):
    y = lax.axis_index("dp") // 2
    tiles = TOK * 2
    pieces = [t.reshape(FRAMES, tiles, 8, E) for t in (queries, keys, values)]
    pieces.append(
        grad_out.reshape(FRAMES, 2, 8, HEADS, E).transpose(0, 1, 3, 2, 4).reshape(FRAMES, tiles, 8, E)
    )
    packed = jnp.concatenate(pieces, axis=1)
    packed = lax.all_to_all(packed, "tm", split_axis=0, concat_axis=0, tiled=True)
    g_tok = (
        packed[:, 3 * tiles :]
        .reshape(FRAMES, 2, HEADS, 8, E)
        .transpose(0, 1, 3, 2, 4)
        .reshape(FRAMES * TOK, DM)
    )
    grad_attended = jnp.einsum(
        "td,dhe->the", g_tok, out_weight, preferred_element_type=jnp.float32
    ).astype(jnp.bfloat16)
    attended, grads = attend(
        packed.reshape(FRAMES, 4, TOK, HEADS, E), grad_attended.reshape(FRAMES, TOK, HEADS, E)
    )
    att = attended.reshape(FRAMES * TOK, DM)

    gs, atts = [], []
    for n in range(Y):
        cut = lax.dynamic_slice_in_dim(g_tok, lax.rem(y + n, Y) * YROWS, YROWS, axis=1)
        gs.append(cut if n == 0 else lax.ppermute(cut, AXES, y_shift(n)))
        atts.append(att if n == 0 else lax.ppermute(att, AXES, y_shift(n)))

    back = lax.all_to_all(grads, "tm", split_axis=0, concat_axis=0, tiled=True)
    shape = (1, 1, PATCH, HEADS, E)
    outs = [back[:, n].reshape(shape) for n in range(3)]

    block = weight_block(gs, atts)
    block = lax.all_to_all(
        block, AXES, split_axis=0, concat_axis=0, tiled=True, axis_index_groups=planes()
    )
    grad_weight = jnp.sum(
        block.reshape(CORES_IN_PLANE, DM // 128, HEADS, E).astype(jnp.float32), axis=0
    )
    return (*outs, grad_weight)


def solution(mesh):
    clip = P("dp", "tm", None, None, None)
    return jax.shard_map(
        shards,
        mesh=mesh,
        in_specs=(clip, clip, clip, P(), P("dp", "tm", None, None)),
        out_specs=(clip, clip, clip, P(AXES, None, None)),
        check_vma=False,
    )
```

time: 840 us -> 198 us (0.24)
  waiting for transfers between devices: 646 us -> 83.8 us
  blocking collectives: 90.9 us -> 60 us
  matrix products: 26.3 us -> 2.38 us
  local copies, waits for them, and re-layouts: 28.7 us -> 6.98 us
  Pallas kernels: 0 us -> 19.3 us
  between operations: 14.2 us -> 0.74 us
    reduce_scatter x1 -> x0, waiting for transfers between devices: 587 us -> none  [shards(): lax.psum_scatter(jnp.einsum('bfpd,bfphe->dhe', grad_out, attended, prefer...]
    ppermute x0 -> x6, waiting for transfers between devices: none -> 59.2 us  [the longest x3 59.2 us: shards(): gs.append(cut if n == 0 else lax.ppermute(cut, AXES, y_shift(n)))]
    all_to_all x4 -> x2, waiting for transfers between devices: 59.7 us -> 24.6 us  [the longest x1 24.6 us: shards(): lax.all_to_all(block, AXES, split_axis=0, concat_axis=0, tiled=True, axis...]
    all_to_all x4 -> x1, blocking collectives: 90.9 us -> 60 us  [shards(): lax.all_to_all(packed, 'tm', split_axis=0, concat_axis=0, tiled=True)]
    dot_general x7 -> x1, matrix products: 22.9 us -> 2.38 us  [shards(): jnp.einsum('td,dhe->the', g_tok, out_weight, preferred_element_type=jnp.f...]
    pallas_call x0 -> x2, Pallas kernels: none -> 19.3 us  [the longest x1 14 us: attend(): pl.pallas_call(attend_kernel, grid=(TOK,), in_specs=[part(0), part(1), pa...]
    dot_general x1 -> x0, local copies, waits for them, and re-layouts: 17.7 us -> none  [shards(): jnp.einsum('bfpd,bfphe->dhe', grad_out, attended, preferred_element_type=...]
    all_to_all x4 -> x2, starting transfers between devices: 25.3 us -> 14.1 us  [the longest x1 8.68 us: shards(): lax.all_to_all(block, AXES, split_axis=0, concat_axis=0, tiled=True, axis...]
  transfers between devices with their start and end apart: 5 -> 8, of which waited for: 5 -> 3; matrix products, arithmetic and copies ran while one was open for 2% -> 3% of each run, Pallas kernels for 0% -> 3%
where the time goes in v1:
time: 198 us; the launch traced here: 197 us
  waiting for transfers between devices  83.8 us (42%)
  blocking collectives  60 us (30%)
  starting transfers between devices  21.4 us (11%)
  Pallas kernels  19.3 us (10%)
  local copies, waits for them, and re-layouts  6.98 us (4%)
  other arithmetic  2.9 us (1%)
  matrix products  2.38 us (1%)
    all_to_all x1, blocking collectives, shards(): lax.all_to_all(packed, 'tm', split_axis=0, concat_axis=0, tiled=True)  60 us
    ppermute x3, waiting for transfers between devices, shards(): gs.append(cut if n == 0 else lax.ppermute(cut, AXES, y_shift(n)))  59.2 us
    all_to_all x1, waiting for transfers between devices, shards(): lax.all_to_all(block, AXES, split_axis=0, concat_axis=0, tiled=True, axis...  24.6 us
    pallas_call x1, Pallas kernels, attend(): pl.pallas_call(attend_kernel, grid=(TOK,), in_specs=[part(0), part(1), pa...  14 us
    all_to_all x1, starting transfers between devices, shards(): lax.all_to_all(block, AXES, split_axis=0, concat_axis=0, tiled=True, axis...  8.68 us
    all_to_all x1, starting transfers between devices, shards(): back = lax.all_to_all(grads, 'tm', split_axis=0, concat_axis=0, tiled=True)  5.39 us
    pallas_call x1, Pallas kernels, weight_block(): pl.pallas_call(weight_kernel, grid=(DM // width,), in_specs=[pl.BlockSpec...  5.28 us
    slice x1, local copies, waits for them, and re-layouts, shards(): outs = [back[:, n].reshape(shape) for n in range(3)]  3.99 us
  transfers between devices with their start and end apart: 8, of which 3 were waited for; matrix products, arithmetic and copies ran while one was open for 3% of the time, Pallas kernels for 3%

profile of v1, /device:TPU:1, one launch (start us, length us, event | category | flops | bytes accessed | tf_op | source)
XLA Modules:
  0.0 197.5 jit_solution(8689863349324116362)
XLA Ops:
  0.6 0.0 slice-start
  0.6 2.6 %pad_maximum_fusion = bf16[16,128,8,128]{3,2,1,0:T(8,128)(2,1)S(1)} fusion(bf16[16,32,8,128]{3,2,1,0:T(8,128)(2,1)} %bitcast.43, bf16[16,32,8,128]{3,2,1,0:T(8,128)(2,1)} %bitcast.44, bf16[16,32,8,128]{3,2,1,0:T(8,128)(2,1)} %bitcast.45, bf16[16,32,8,128]{3,2,1,0:T(8,128)(2,1)} %bitcast.46), kind=kLoop, calls=%fused_computation.2 | loop fusion | flops 6291456 | bytes 8388608 | tf_op jit(solution)/shard_map/concatenate | solution.py:112
  3.2 0.0 slice-start.1
  3.2 60.0 %all_to_all.19 = bf16[16,128,8,128]{3,2,1,0:T(8,128)(2,1)S(1)} all-to-all(bf16[16,128,8,128]{3,2,1,0:T(8,128)(2,1)S(1)} %pad_maximum_fusion), channel_id=1, replica_groups=mesh['dp'=8,'tm'=16] {'tm'}, dimensions={0} | all-to-all | bytes 8388608 | tf_op jit(solution)/shard_map/all_to_all | solution.py:113
  63.2 0.1 slice.16
  63.3 0.0 copy-start
  63.3 0.0 slice-done
  63.3 0.0 slice-done.1
  63.3 2.4 %fusion.2 = bf16[256,16,128]{2,0,1:T(8,128)(2,1)S(1)} fusion(bf16[256,2048,1]{1,0,2:T(8,128)(2,1)S(1)} %bitcast.38, bf16[2048,16,128]{2,1,0:T(8,128)(2,1)S(1)} %bitcast.50), kind=kOutput, calls=%fused_computation.4 | convolution fusion | flops 2148007936 | bytes 10485760 | tf_op jit(solution)/shard_map/td,dhe->the/dot_general | solution.py:120
  65.7 0.0 copy-done
  65.7 0.7 copy.10
  66.4 14.0 %shard_map.84 = (bf16[16,16,16,128]{3,2,1,0:T(8,128)(2,1)S(1)}, bf16[16,3,16,16,128]{4,3,2,1,0:T(8,128)(2,1)}) custom-call(bf16[16,4,16,16,128]{4,3,2,1,0:T(8,128)(2,1)S(1)} %bitcast.29, bf16[16,4,16,16,128]{4,3,2,1,0:T(8,128)(2,1)S(1)} %bitcast.30, bf16[16,4,16,16,128]{4,3,2,1,0:T(8,128)(2,1)S(1)} %bitcast.31, bf16[16,16,16,128]{3,2,1,0:T(8,128)(2,1)S(1)} %bitcast.36), custom_call_target="tpu_custom_call" | custom-call | tf_op jit(solution)/shard_map/pallas_call | solution.py:70
  80.5 5.4 %all-to-all-start.1 = ((bf16[16,3,16,16,128]{4,3,2,1,0:T(8,128)(2,1)}), bf16[16,3,16,16,128]{4,3,2,1,0:T(8,128)(2,1)}, u32[]{:S(2)}, u32[]{:S(2)}) async-start(bf16[16,3,16,16,128]{4,3,2,1,0:T(8,128)(2,1)} %get-tuple-element.6), calls=%async_computation.1 | async-start | bytes 6291456 | tf_op jit(solution)/shard_map/all_to_all | solution.py:134
  85.9 0.3 copy.18
  86.1 2.8 %collective-permute-start.5 = (bf16[256,2048]{1,0:T(8,128)(2,1)S(1)}, bf16[256,2048]{1,0:T(8,128)(2,1)S(1)}, u32[]{:S(2)}, u32[]{:S(2)}) collective-permute-start(bf16[256,2048]{1,0:T(8,128)(2,1)S(1)} %bitcast.32), channel_id=1, source_target_pairs={{0,96},{1,97},{2,98},{3,99},{4,100},{5,101},{6,102},{7,103},{8,104... | collective-permute-start | bytes 3145736 | tf_op jit(solution)/shard_map/ppermute | solution.py:132
  88.9 0.3 collective-permute-start.4
  89.3 0.7 collective-permute-start.3
  90.0 1.3 constant_dynamic-slice_fusion
  91.2 2.1 %collective-permute-start.2 = (bf16[256,512]{1,0:T(8,128)(2,1)S(1)}, bf16[256,512]{1,0:T(8,128)(2,1)S(1)}, u32[]{:S(2)}, u32[]{:S(2)}) collective-permute-start(bf16[256,512]{1,0:T(8,128)(2,1)S(1)} %get-tuple-element.11), channel_id=1, source_target_pairs={{0,96},{1,97},{2,98},{3,99},{4,100},{5,101},{6,102},{7,103},{8,104... | collective-permute-start | bytes 786440 | tf_op jit(solution)/shard_map/ppermute | solution.py:131
  93.3 1.4 collective-permute-start.1
  94.7 50.1 %collective-permute-done.2.refs_3_ = bf16[256,512]{1,0:T(8,128)(2,1)S(1)} collective-permute-done((bf16[256,512]{1,0:T(8,128)(2,1)S(1)}, bf16[256,512]{1,0:T(8,128)(2,1)S(1)}, u32[]{:S(2)}, u32[]{:S(2)}) %collective-permute-start.2) | collective-permute-done | bytes 262176 | tf_op jit(solution)/shard_map/ppermute | solution.py:131
  144.8 0.0 collective-permute-start
  144.8 0.0 collective-permute-done.1.refs_2_
  144.8 9.1 %collective-permute-done.refs_1_ = bf16[256,512]{1,0:T(8,128)(2,1)S(1)} collective-permute-done((bf16[256,512]{1,0:T(8,128)(2,1)S(1)}, bf16[256,512]{1,0:T(8,128)(2,1)S(1)}, u32[]{:S(2)}, u32[]{:S(2)}) %collective-permute-start) | collective-permute-done | bytes 262176 | tf_op jit(solution)/shard_map/ppermute | solution.py:131
  153.9 0.0 collective-permute-done.5.refs_7_
  153.9 0.0 collective-permute-done.4.refs_6_
  153.9 0.0 collective-permute-done.3.refs_5_
  153.9 5.3 %shard_map.85 = bf16[512,2048]{1,0:T(8,128)(2,1)} custom-call(bf16[256,512]{1,0:T(8,128)(2,1)S(1)} %get-tuple-element.14.refs_0_, bf16[256,512]{1,0:T(8,128)(2,1)S(1)} %collective-permute-done.refs_1_, bf16[256,512]{1,0:T(8,128)(2,1)S(1)} %collective-permute-done.1.refs_2_, bf16[256,512]{1,0:T(8,128)(2,1)S(1)} %collective-permute-done.2.refs_3_, ...), custom_call_target="tpu_custom_call" | custom-call | tf_op jit(solution)/shard_map/pallas_call | solution.py:94
  159.2 0.0 all-to-all-done.1
  159.2 8.7 %all-to-all-start.2 = ((bf16[32,16,2048]{2,1,0:T(8,128)(2,1)}), bf16[32,16,2048]{2,1,0:T(8,128)(2,1)S(1)}, u32[]{:S(2)}, u32[]{:S(2)}) async-start(bf16[32,16,2048]{2,1,0:T(8,128)(2,1)} %bitcast.17), calls=%async_computation.2 | async-start | bytes 4194304 | tf_op jit(solution)/shard_map/all_to_all | solution.py:139
  167.9 4.0 %fusion.5 = (bf16[16,1,16,16,128]{4,3,2,1,0:T(8,128)(2,1)}, bf16[16,1,16,16,128]{4,3,2,1,0:T(8,128)(2,1)}, bf16[16,1,16,16,128]{4,3,2,1,0:T(8,128)(2,1)}) fusion(bf16[16,3,16,16,128]{4,3,2,1,0:T(8,128)(2,1)} %all-to-all-done.1), kind=kLoop, calls=%fused_computation.10 | loop fusion | bytes 6291456 | tf_op jit(solution)/shard_map/slice | solution.py:136
  171.8 24.6 %all-to-all-done.2 = bf16[32,16,2048]{2,1,0:T(8,128)(2,1)S(1)} async-done(((bf16[32,16,2048]{2,1,0:T(8,128)(2,1)}), bf16[32,16,2048]{2,1,0:T(8,128)(2,1)S(1)}, u32[]{:S(2)}, u32[]{:S(2)}) %all-to-all-start.2) | async-done | bytes 2097184 | tf_op jit(solution)/shard_map/all_to_all | solution.py:139
  196.5 0.3 convert_reduce_fusion
  196.8 0.7 copy.12
  (1 shorter events, 0.0 us)
Async XLA Ops:
  0.6 62.7 %slice-start = ((s8[8388608]{0:T(1024)(128)(4,1)}), s8[4194304]{0:T(1024)(128)(4,1)S(1)}, s32[]{:S(2)}) async-start(s8[8388608]{0:T(1024)(128)(4,1)} %bitcast.49), calls=%async_computation.3 | async-start | bytes 8388608
  3.2 60.1 %slice-start.1 = ((s8[8388608]{0:T(1024)(128)(4,1)}), s8[4194304]{0:T(1024)(128)(4,1)S(1)}, s32[]{:S(2)}) async-start(s8[8388608]{0:T(1024)(128)(4,1)} %bitcast.49), calls=%async_computation.4 | async-start | bytes 8388608
  63.3 2.4 %copy-start = (bf16[16,32,8,128]{3,2,1,0:T(8,128)(2,1)}, bf16[16,32,8,128]{3,2,1,0:T(8,128)(2,1)S(1)}, u32[]{:S(2)}) copy-start(bf16[16,32,8,128]{3,2,1,0:T(8,128)(2,1)S(1)} %slice.16) | copy-start | bytes 3145732
  80.5 78.7 %all-to-all-start.1 = ((bf16[16,3,16,16,128]{4,3,2,1,0:T(8,128)(2,1)}), bf16[16,3,16,16,128]{4,3,2,1,0:T(8,128)(2,1)}, u32[]{:S(2)}, u32[]{:S(2)}) async-start(bf16[16,3,16,16,128]{4,3,2,1,0:T(8,128)(2,1)} %get-tuple-element.6), calls=%async_computation.1 | async-start | bytes 6291456 | tf_op jit(solution)/shard_map/all_to_all | solution.py:134
  86.1 67.7 %collective-permute-start.5 = (bf16[256,2048]{1,0:T(8,128)(2,1)S(1)}, bf16[256,2048]{1,0:T(8,128)(2,1)S(1)}, u32[]{:S(2)}, u32[]{:S(2)}) collective-permute-start(bf16[256,2048]{1,0:T(8,128)(2,1)S(1)} %bitcast.32), channel_id=1, source_target_pairs={{0,96},{1,97},{2,98},{3,99},{4,100},{5,101},{6,102},{7,103},{8,104... | collective-permute-start | bytes 3145736 | tf_op jit(solution)/shard_map/ppermute | solution.py:132
  88.9 64.9 %collective-permute-start.4 = (bf16[256,2048]{1,0:T(8,128)(2,1)S(1)}, bf16[256,2048]{1,0:T(8,128)(2,1)S(1)}, u32[]{:S(2)}, u32[]{:S(2)}) collective-permute-start(bf16[256,2048]{1,0:T(8,128)(2,1)S(1)} %bitcast.33), channel_id=1, source_target_pairs={{0,64},{1,65},{2,66},{3,67},{4,68},{5,69},{6,70},{7,71},{8,72},{9,... | collective-permute-start | bytes 3145736 | tf_op jit(solution)/shard_map/ppermute | solution.py:132
  89.3 64.6 %collective-permute-start.3 = (bf16[256,2048]{1,0:T(8,128)(2,1)S(1)}, bf16[256,2048]{1,0:T(8,128)(2,1)}, u32[]{:S(2)}, u32[]{:S(2)}) collective-permute-start(bf16[256,2048]{1,0:T(8,128)(2,1)S(1)} %bitcast.34), channel_id=1, source_target_pairs={{0,32},{1,33},{2,34},{3,35},{4,36},{5,37},{6,38},{7,39},{8,40},{9,... | collective-permute-start | bytes 3145736 | tf_op jit(solution)/shard_map/ppermute | solution.py:132
  91.2 53.5 %collective-permute-start.2 = (bf16[256,512]{1,0:T(8,128)(2,1)S(1)}, bf16[256,512]{1,0:T(8,128)(2,1)S(1)}, u32[]{:S(2)}, u32[]{:S(2)}) collective-permute-start(bf16[256,512]{1,0:T(8,128)(2,1)S(1)} %get-tuple-element.11), channel_id=1, source_target_pairs={{0,96},{1,97},{2,98},{3,99},{4,100},{5,101},{6,102},{7,103},{8,104... | collective-permute-start | bytes 786440 | tf_op jit(solution)/shard_map/ppermute | solution.py:131
  93.3 51.5 %collective-permute-start.1 = (bf16[256,512]{1,0:T(8,128)(2,1)S(1)}, bf16[256,512]{1,0:T(8,128)(2,1)S(1)}, u32[]{:S(2)}, u32[]{:S(2)}) collective-permute-start(bf16[256,512]{1,0:T(8,128)(2,1)S(1)} %get-tuple-element.12), channel_id=1, source_target_pairs={{0,64},{1,65},{2,66},{3,67},{4,68},{5,69},{6,70},{7,71},{8,72},{9,... | collective-permute-start | bytes 786440 | tf_op jit(solution)/shard_map/ppermute | solution.py:131
  144.8 9.1 %collective-permute-start = (bf16[256,512]{1,0:T(8,128)(2,1)S(1)}, bf16[256,512]{1,0:T(8,128)(2,1)S(1)}, u32[]{:S(2)}, u32[]{:S(2)}) collective-permute-start(bf16[256,512]{1,0:T(8,128)(2,1)S(1)} %get-tuple-element.13), channel_id=1, source_target_pairs={{0,32},{1,33},{2,34},{3,35},{4,36},{5,37},{6,38},{7,39},{8,40},{9,... | collective-permute-start | bytes 786440 | tf_op jit(solution)/shard_map/ppermute | solution.py:131
  159.2 37.3 %all-to-all-start.2 = ((bf16[32,16,2048]{2,1,0:T(8,128)(2,1)}), bf16[32,16,2048]{2,1,0:T(8,128)(2,1)S(1)}, u32[]{:S(2)}, u32[]{:S(2)}) async-start(bf16[32,16,2048]{2,1,0:T(8,128)(2,1)} %bitcast.17), calls=%async_computation.2 | async-start | bytes 4194304 | tf_op jit(solution)/shard_map/all_to_all | solution.py:139

commit v2 on v1

v2 whole, which is shorter than its diff:
```python
import jax
import jax.numpy as jnp
from jax import lax
from jax.experimental import pallas as pl
from jax.experimental.pallas import tpu as pltpu
from jax.sharding import PartitionSpec as P

FRAMES, TOK, HEADS, E, DM = 16, 16, 16, 128, 2048
PATCH = 256
TOKENS = FRAMES * TOK
GROUPS, GROUP = 2, 8
ROWS = FRAMES * GROUP
STEP_TOK = 4
AXES = ("dp", "tm")
SCALE = 1.0 / (E**0.5)
EXP2_SCALE = SCALE * 1.4426950408889634
Y, PLANE = 4, 32
YROWS = DM // Y
HALF = DM // 2
VMEM = 16 * 1024 * 1024


def y_shift(n):
    total = Y * PLANE
    return [(i, (i + n * PLANE) % total) for i in range(total)]


def core_swap():
    return [(i, i ^ 1) for i in range(Y * PLANE)]


def planes():
    return [[y * PLANE + i for i in range(PLANE)] for y in range(Y)]


def dot_nt(a, b):
    return lax.dot_general(a, b, (((1,), (1,)), ((), ())), preferred_element_type=jnp.float32)


def dot_tn(a, b):
    return lax.dot_general(a, b, (((0,), (0,)), ((), ())), preferred_element_type=jnp.float32)


def dot_nn(a, b):
    return lax.dot_general(a, b, (((1,), (0,)), ((), ())), preferred_element_type=jnp.float32)


def attend_group(q, k, v, g, bias):
    scores = dot_nt(q, k) + bias
    expd = jnp.exp2((scores - jnp.max(scores, axis=1, keepdims=True)) * EXP2_SCALE)
    probs = expd * (1.0 / jnp.sum(expd, axis=1, keepdims=True))
    weights = probs.astype(jnp.bfloat16)
    attended = dot_nn(weights, v).astype(jnp.bfloat16)
    gv = dot_tn(weights, g).astype(jnp.bfloat16)
    gp = dot_nt(g, v)
    delta = jnp.sum(probs * gp, axis=1, keepdims=True)
    gs = (probs * (gp - delta)).astype(jnp.bfloat16)
    gq = (dot_nn(gs, k) * SCALE).astype(jnp.bfloat16)
    gk = (dot_tn(gs, q) * SCALE).astype(jnp.bfloat16)
    return attended, gq, gk, gv


def attend_kernel(core_ref, q_ref, k_ref, v_ref, g_ref, a_ref, grads_ref, bias_ref):
    @pl.when(pl.program_id(0) == 0)
    def _():
        row = lax.broadcasted_iota(jnp.int32, (ROWS, ROWS), 0)
        col = lax.broadcasted_iota(jnp.int32, (ROWS, ROWS), 1)
        keep = (row % GROUP == col % GROUP) & (col <= row)
        bias_ref[...] = jnp.where(keep, 0.0, -jnp.inf)

    bias = bias_ref[...]
    for t in range(STEP_TOK):
        for h in range(GROUPS):
            q, k, v = (ref[:, 0, t, h].reshape(ROWS, E) for ref in (q_ref, k_ref, v_ref))
            g = g_ref[:, t, h].reshape(ROWS, E)
            attended, *grads = attend_group(q, k, v, g, bias)
            a_ref[lax.rem(core_ref[0] + h, GROUPS), :, t] = attended.reshape(FRAMES, GROUP, E)
            for n, grad in enumerate(grads):
                grads_ref[:, n, t, h] = grad.reshape(FRAMES, GROUP, E)


def attend(core, packed, grad_attended):
    def part(n):
        block = (FRAMES, 1, STEP_TOK, GROUPS, GROUP, E)
        return pl.BlockSpec(block, lambda t, n=n: (0, n, t, 0, 0, 0))

    token = pl.BlockSpec((FRAMES, STEP_TOK, GROUPS, GROUP, E), lambda t: (0, t, 0, 0, 0))
    halves = pl.BlockSpec((GROUPS, FRAMES, STEP_TOK, GROUP, E), lambda t: (0, 0, t, 0, 0))
    grads = pl.BlockSpec((FRAMES, 3, STEP_TOK, GROUPS, GROUP, E), lambda t: (0, 0, t, 0, 0, 0))
    return pl.pallas_call(
        attend_kernel,
        grid=(TOK // STEP_TOK,),
        in_specs=[pl.BlockSpec(memory_space=pltpu.SMEM), part(0), part(1), part(2), token],
        out_specs=[halves, grads],
        out_shape=[
            jax.ShapeDtypeStruct((GROUPS, FRAMES, TOK, GROUP, E), jnp.bfloat16),
            jax.ShapeDtypeStruct((FRAMES, 3, TOK, GROUPS, GROUP, E), jnp.bfloat16),
        ],
        scratch_shapes=[pltpu.VMEM((ROWS, ROWS), jnp.float32)],
        compiler_params=pltpu.CompilerParams(vmem_limit_bytes=VMEM),
        cost_estimate=pl.CostEstimate(flops=7 * 10**9, bytes_accessed=8 * 2**20, transcendentals=0),
    )(core.reshape(1), packed, packed, packed, grad_attended)


def partial_product(g_ref, g_swapped_ref, a_ref, a_swapped_ref):
    return dot_tn(g_ref[...], a_ref[...]) + dot_tn(g_swapped_ref[...], a_swapped_ref[...])


def far_kernel(plane_ref, g_ref, gs_ref, a_ref, as_ref, left_ref, right_ref):
    total = partial_product(g_ref, gs_ref, a_ref, as_ref).astype(jnp.bfloat16)
    left_ref[...] = total[:, : HALF // 2]
    right_ref[...] = total[:, HALF // 2 :]


def near_kernel(plane_ref, g1, gs1, g3, gs3, a_ref, as_ref, left_ref, right_ref, up_ref, down_ref):
    up = partial_product(g1, gs1, a_ref, as_ref)
    up_ref[:, : HALF // 2] = (up[:, : HALF // 2] + left_ref[...]).astype(jnp.bfloat16)
    up_ref[:, HALF // 2 :] = up[:, HALF // 2 :].astype(jnp.bfloat16)
    down = partial_product(g3, gs3, a_ref, as_ref)
    down_ref[:, : HALF // 2] = down[:, : HALF // 2].astype(jnp.bfloat16)
    down_ref[:, HALF // 2 :] = (down[:, HALF // 2 :] + right_ref[...]).astype(jnp.bfloat16)


def own_kernel(plane_ref, g_ref, gs_ref, a_ref, as_ref, up_ref, down_ref, out_ref):
    total = partial_product(g_ref, gs_ref, a_ref, as_ref)
    out_ref[...] = (total + up_ref[...] + down_ref[...]).astype(jnp.bfloat16)


def weight_step(kernel, plane, offsets, g, g_swapped, rest, widths):
    def rows(n):
        return pl.BlockSpec((TOKENS, YROWS), lambda i, p, n=n: (0, lax.rem(p[0] + n, Y)))

    def whole(shape):
        return pl.BlockSpec(shape, lambda i, p: (0, 0))

    specs = [rows(n) for n in offsets for _ in range(2)] + [whole(r.shape) for r in rest]
    return pl.pallas_call(
        kernel,
        grid_spec=pltpu.PrefetchScalarGridSpec(
            num_scalar_prefetch=1,
            grid=(1,),
            in_specs=specs,
            out_specs=[whole((YROWS, w)) for w in widths],
        ),
        out_shape=[jax.ShapeDtypeStruct((YROWS, w), jnp.bfloat16) for w in widths],
        compiler_params=pltpu.CompilerParams(vmem_limit_bytes=24 * 1024 * 1024),
        cost_estimate=pl.CostEstimate(
            flops=10**9 * len(offsets), bytes_accessed=4 * 2**20, transcendentals=0
        ),
    )(plane, *([g, g_swapped] * len(offsets)), *rest)


def shards(queries, keys, values, out_weight, grad_out):
    y = lax.axis_index("dp") // 2
    core = lax.rem(lax.axis_index("tm"), 2)
    tiles = TOK * 2
    pieces = [t.reshape(FRAMES, tiles, 8, E) for t in (queries, keys, values)]
    pieces.append(
        grad_out.reshape(FRAMES, 2, 8, HEADS, E).transpose(0, 1, 3, 2, 4).reshape(FRAMES, tiles, 8, E)
    )
    packed = jnp.concatenate(pieces, axis=1)
    packed = lax.all_to_all(packed, "tm", split_axis=0, concat_axis=0, tiled=True)
    g_tok = (
        packed[:, 3 * tiles :]
        .reshape(FRAMES, 2, HEADS, 8, E)
        .transpose(0, 1, 3, 2, 4)
        .reshape(TOKENS, DM)
    )

    grad_attended = jnp.einsum(
        "td,dhe->the", g_tok, out_weight, preferred_element_type=jnp.float32
    ).astype(jnp.bfloat16)
    attended, grads = attend(
        core,
        packed.reshape(FRAMES, 4, TOK, GROUPS, GROUP, E),
        grad_attended.reshape(FRAMES, TOK, GROUPS, GROUP, E),
    )

    back = lax.all_to_all(grads, "tm", split_axis=0, concat_axis=0, tiled=True)

    own = attended[0].reshape(TOKENS, HALF)
    g_swapped = lax.ppermute(g_tok, AXES, core_swap())
    other = attended[1].reshape(TOKENS, HALF)
    swapped = lax.ppermute(other, AXES, core_swap())

    plane = y.reshape(1)
    left, right = weight_step(
        far_kernel, plane, [2], g_tok, g_swapped, [own, swapped], [HALF // 2, HALF // 2]
    )
    left = lax.ppermute(left, AXES, y_shift(1))
    right = lax.ppermute(right, AXES, y_shift(-1))
    up, down = weight_step(
        near_kernel, plane, [1, 3], g_tok, g_swapped, [own, swapped, left, right], [HALF, HALF]
    )
    up = lax.ppermute(up, AXES, y_shift(1))
    down = lax.ppermute(down, AXES, y_shift(-1))
    (block,) = weight_step(
        own_kernel, plane, [0], g_tok, g_swapped, [own, swapped, up, down], [HALF]
    )

    block, back = lax.optimization_barrier((block, back))
    block = lax.all_to_all(
        block, AXES, split_axis=0, concat_axis=0, tiled=True, axis_index_groups=planes()
    )
    shape = (1, 1, PATCH, HEADS, E)
    outs = [back[:, n].reshape(shape) for n in range(3)]
    rows = DM // (Y * PLANE)
    total = jnp.sum(block.reshape(PLANE // 2, 2, rows, HALF).astype(jnp.float32), axis=0)
    grad_weight = total.transpose(1, 0, 2).reshape(rows, HEADS, E)
    return (*outs, grad_weight)


def solution(mesh):
    clip = P("dp", "tm", None, None, None)
    return jax.shard_map(
        shards,
        mesh=mesh,
        in_specs=(clip, clip, clip, P(), P("dp", "tm", None, None)),
        out_specs=(clip, clip, clip, P(AXES, None, None)),
        check_vma=False,
    )
```

time: 198 us -> 161 us (0.81)
  blocking collectives: 60 us -> 0 us
  waiting for transfers between devices: 83.8 us -> 99.3 us
  Pallas kernels: 19.3 us -> 11 us
  starting transfers between devices: 21.4 us -> 28.9 us
  local copies, waits for them, and re-layouts: 6.98 us -> 10.6 us
  matrix products: 2.38 us -> 5.75 us
    all_to_all x1 -> x0, blocking collectives: 60 us -> none  [shards(): lax.all_to_all(packed, 'tm', split_axis=0, concat_axis=0, tiled=True)]
    all_to_all x0 -> x1, waiting for transfers between devices: none -> 51.1 us  [shards(): lax.all_to_all(packed, 'tm', split_axis=0, concat_axis=0, tiled=True)]
    ppermute x6, waiting for transfers between devices: 59.2 us -> 35.1 us  [the longest x1 22.4 us: shards(): up = lax.ppermute(up, AXES, y_shift(1))]
    all_to_all x1, waiting for transfers between devices: 24.6 us -> 13.1 us  [shards(): lax.all_to_all(block, AXES, split_axis=0, concat_axis=0, tiled=True, axis...]
    all_to_all x0 -> x1, starting transfers between devices: none -> 9.29 us  [shards(): lax.all_to_all(packed, 'tm', split_axis=0, concat_axis=0, tiled=True)]
    pallas_call x2 -> x4, Pallas kernels: 19.3 us -> 11 us  [the longest x1 7.14 us: attend(): pl.pallas_call(attend_kernel, grid=(TOK // STEP_TOK,), in_specs=[pl.Block...]
    dot_general x1, matrix products: 2.38 us -> 5.75 us  [shards(): jnp.einsum('td,dhe->the', g_tok, out_weight, preferred_element_type=jnp.f...]
  transfers between devices with their start and end apart: 8 -> 9, of which waited for: 3 -> 5; matrix products, arithmetic and copies ran while one was open for 3% -> 4% of each run, Pallas kernels for 3% -> 7%
where the time goes in v2:
time: 161 us; the launch traced here: 160 us
  waiting for transfers between devices  99.3 us (62%)
  starting transfers between devices  28.9 us (18%)
  Pallas kernels  11 us (7%)
  local copies, waits for them, and re-layouts  10.6 us (7%)
  matrix products  5.75 us (4%)
  other arithmetic  3.96 us (2%)
    all_to_all x1, waiting for transfers between devices, shards(): lax.all_to_all(packed, 'tm', split_axis=0, concat_axis=0, tiled=True)  51.1 us
    ppermute x1, waiting for transfers between devices, shards(): up = lax.ppermute(up, AXES, y_shift(1))  22.4 us
    all_to_all x1, waiting for transfers between devices, shards(): lax.all_to_all(block, AXES, split_axis=0, concat_axis=0, tiled=True, axis...  13.1 us
    ppermute x1, waiting for transfers between devices, shards(): left = lax.ppermute(left, AXES, y_shift(1))  12 us
    all_to_all x1, starting transfers between devices, shards(): lax.all_to_all(packed, 'tm', split_axis=0, concat_axis=0, tiled=True)  9.29 us
    all_to_all x1, starting transfers between devices, shards(): lax.all_to_all(block, AXES, split_axis=0, concat_axis=0, tiled=True, axis...  8.39 us
    pallas_call x1, Pallas kernels, attend(): pl.pallas_call(attend_kernel, grid=(TOK // STEP_TOK,), in_specs=[pl.Block...  7.14 us
    dot_general x1, matrix products, shards(): jnp.einsum('td,dhe->the', g_tok, out_weight, preferred_element_type=jnp.f...  5.75 us
  transfers between devices with their start and end apart: 9, of which 5 were waited for; matrix products, arithmetic and copies ran while one was open for 4% of the time, Pallas kernels for 7%

profile of v2, /device:TPU:1, one launch (start us, length us, event | category | flops | bytes accessed | tf_op | source)
XLA Modules:
  0.0 160.3 jit_solution(8370884540376087538)
XLA Ops:
  0.6 3.8 %pad_maximum_fusion = bf16[16,128,8,128]{3,2,1,0:T(8,128)(2,1)} fusion(bf16[16,32,8,128]{3,2,1,0:T(8,128)(2,1)} %bitcast.53, bf16[16,32,8,128]{3,2,1,0:T(8,128)(2,1)} %bitcast.54, bf16[16,32,8,128]{3,2,1,0:T(8,128)(2,1)} %bitcast.55, bf16[16,32,8,128]{3,2,1,0:T(8,128)(2,1)} %bitcast.56), kind=kLoop, calls=%fused_computation.2 | loop fusion | flops 6291456 | bytes 8388608 | tf_op jit(solution)/shard_map/concatenate | solution.py:161
  4.4 9.3 %all-to-all-start = ((bf16[16,128,8,128]{3,2,1,0:T(8,128)(2,1)}), bf16[16,128,8,128]{3,2,1,0:T(8,128)(2,1)}, u32[]{:S(2)}, u32[]{:S(2)}) async-start(bf16[16,128,8,128]{3,2,1,0:T(8,128)(2,1)} %pad_maximum_fusion), calls=%async_computation | async-start | bytes 8388608 | tf_op jit(solution)/shard_map/all_to_all | solution.py:162
  13.7 51.1 %all-to-all-done = bf16[16,128,8,128]{3,2,1,0:T(8,128)(2,1)} async-done(((bf16[16,128,8,128]{3,2,1,0:T(8,128)(2,1)}), bf16[16,128,8,128]{3,2,1,0:T(8,128)(2,1)}, u32[]{:S(2)}, u32[]{:S(2)}) %all-to-all-start) | async-done | bytes 4194336 | tf_op jit(solution)/shard_map/all_to_all | solution.py:162
  64.8 1.3 slice.24
  66.1 5.7 %fusion.2 = bf16[256,16,128]{2,0,1:T(8,128)(2,1)S(1)} fusion(bf16[256,2048,1]{1,0,2:T(8,128)(2,1)S(1)} %bitcast.37, bf16[2048,16,128]{2,1,0:T(8,128)(2,1)} %param.8), kind=kOutput, calls=%fused_computation.4 | convolution fusion | flops 2148007936 | bytes 10485760 | tf_op jit(solution)/shard_map/td,dhe->the/dot_general | solution.py:170
  71.9 0.7 copy.14
  72.6 1.0 collective-permute-start
  73.6 7.1 %shard_map.84 = (bf16[2,16,16,8,128]{4,3,2,1,0:T(8,128)(2,1)S(1)}, bf16[16,3,16,2,8,128]{5,4,3,2,1,0:T(8,128)(2,1)S(1)}) custom-call(s32[1]{0:T(128)} %bitcast.12.core_ref, bf16[16,4,16,2,8,128]{5,4,3,2,1,0:T(8,128)(2,1)} %bitcast.13.q_ref.k_ref.v_ref, bf16[16,4,16,2,8,128]{5,4,3,2,1,0:T(8,128)(2,1)} %bitcast.13.q_ref.k_ref.v_ref, ...), custom_call_target="tpu_custom_call" | custom-call | flops 7000000000 | bytes 8388608 | tf_op jit(solution)/shard_map/pallas_call | solution.py:90
  80.7 0.0 copy-start
  80.7 1.7 %copy-done = bf16[16,3,16,2,8,128]{5,4,3,2,1,0:T(8,128)(2,1)} copy-done((bf16[16,3,16,2,8,128]{5,4,3,2,1,0:T(8,128)(2,1)}, bf16[16,3,16,2,8,128]{5,4,3,2,1,0:T(8,128)(2,1)S(1)}, u32[]{:S(2)}) %copy-start) | copy-done | bytes 3145752
  82.4 4.4 %all-to-all-start.1 = ((bf16[16,3,16,2,8,128]{5,4,3,2,1,0:T(8,128)(2,1)}), bf16[16,3,16,2,8,128]{5,4,3,2,1,0:T(8,128)(2,1)}, u32[]{:S(2)}, u32[]{:S(2)}) async-start(bf16[16,3,16,2,8,128]{5,4,3,2,1,0:T(8,128)(2,1)} %copy-done), calls=%async_computation.1 | async-start | bytes 6291456 | tf_op jit(solution)/shard_map/all_to_all | solution.py:179
  86.8 0.9 fusion.6
  87.7 0.1 copy.24
  87.8 0.2 collective-permute-start.1
  88.0 1.1 copy.25
  89.1 0.6 collective-permute-done.1.as_ref
  89.8 0.0 collective-permute-done.gs_ref.gs1.gs3
  89.8 0.7 shard_map.85
  90.5 1.4 collective-permute-start.2
  91.9 1.5 collective-permute-start.3
  93.4 12.0 %collective-permute-done.2.left_ref = bf16[512,512]{1,0:T(8,128)(2,1)S(1)} collective-permute-done((bf16[512,512]{1,0:T(8,128)(2,1)S(1)}, bf16[512,512]{1,0:T(8,128)(2,1)S(1)}, u32[]{:S(2)}, u32[]{:S(2)}) %collective-permute-start.2) | collective-permute-done | bytes 524320 | tf_op jit(solution)/shard_map/ppermute | solution.py:190
  105.4 0.0 collective-permute-done.3.right_ref
  105.4 1.3 shard_map.86
  106.7 1.0 collective-permute-start.4
  107.7 1.8 %collective-permute-start.5 = (bf16[512,1024]{1,0:T(8,128)(2,1)S(1)}, bf16[512,1024]{1,0:T(8,128)(2,1)S(1)}, u32[]{:S(2)}, u32[]{:S(2)}) collective-permute-start(bf16[512,1024]{1,0:T(8,128)(2,1)S(1)} %get-tuple-element.16), channel_id=1, source_target_pairs={{0,96},{1,97},{2,98},{3,99},{4,100},{5,101},{6,102},{7,103},{8,104... | collective-permute-start | bytes 3145736 | tf_op jit(solution)/shard_map/ppermute | solution.py:196
  109.5 22.4 %collective-permute-done.4.up_ref = bf16[512,1024]{1,0:T(8,128)(2,1)S(1)} collective-permute-done((bf16[512,1024]{1,0:T(8,128)(2,1)S(1)}, bf16[512,1024]{1,0:T(8,128)(2,1)S(1)}, u32[]{:S(2)}, u32[]{:S(2)}) %collective-permute-start.4) | collective-permute-done | bytes 1048608 | tf_op jit(solution)/shard_map/ppermute | solution.py:195
  131.9 0.0 collective-permute-done.5.down_ref
  131.9 1.8 %shard_map.87 = bf16[512,1024]{1,0:T(8,128)(2,1)} custom-call(s32[1]{0:T(128)} %bitcast.plane_ref, bf16[256,2048]{1,0:T(8,128)(2,1)S(1)} %bitcast.42, bf16[256,2048]{1,0:T(8,128)(2,1)S(1)} %collective-permute-done.gs_ref.gs1.gs3, bf16[256,1024]{1,0:T(8,128)(2,1)S(1)} %bitcast.45, bf16[256,1024]{1,0:T(8,128)(2,1)S(1)} %collective-permute-done.1.as_ref, ...), custom_call_target="tpu_custom_call" | custom-call | flops 1000000000 | bytes 4194304 | tf_op jit(solution)/shard_map/pallas_call | solution.py:137
  133.8 0.0 all-to-all-done.1
  133.8 8.4 %all-to-all-start.2 = ((bf16[32,16,1024]{2,1,0:T(8,128)(2,1)}), bf16[32,16,1024]{2,1,0:T(8,128)(2,1)S(1)}, u32[]{:S(2)}, u32[]{:S(2)}) async-start(bf16[32,16,1024]{2,1,0:T(8,128)(2,1)} %bitcast.19), calls=%async_computation.2 | async-start | bytes 2097152 | tf_op jit(solution)/shard_map/all_to_all | solution.py:202
  142.2 4.0 %fusion.5 = (bf16[16,1,16,2,8,128]{5,4,3,2,1,0:T(8,128)(2,1)}, bf16[16,1,16,2,8,128]{5,4,3,2,1,0:T(8,128)(2,1)}, bf16[16,1,16,2,8,128]{5,4,3,2,1,0:T(8,128)(2,1)}) fusion(bf16[16,3,16,2,8,128]{5,4,3,2,1,0:T(8,128)(2,1)} %all-to-all-done.1), kind=kLoop, calls=%fused_computation.7 | loop fusion | bytes 6291456 | tf_op jit(solution)/shard_map/slice | solution.py:206
  146.2 13.1 %all-to-all-done.2 = bf16[32,16,1024]{2,1,0:T(8,128)(2,1)S(1)} async-done(((bf16[32,16,1024]{2,1,0:T(8,128)(2,1)}), bf16[32,16,1024]{2,1,0:T(8,128)(2,1)S(1)}, u32[]{:S(2)}, u32[]{:S(2)}) %all-to-all-start.2) | async-done | bytes 1048608 | tf_op jit(solution)/shard_map/all_to_all | solution.py:202
  159.2 0.2 convert_reduce_fusion
  159.4 0.1 copy.15
  159.5 0.8 reshape.61
Async XLA Ops:
  4.4 60.4 %all-to-all-start = ((bf16[16,128,8,128]{3,2,1,0:T(8,128)(2,1)}), bf16[16,128,8,128]{3,2,1,0:T(8,128)(2,1)}, u32[]{:S(2)}, u32[]{:S(2)}) async-start(bf16[16,128,8,128]{3,2,1,0:T(8,128)(2,1)} %pad_maximum_fusion), calls=%async_computation | async-start | bytes 8388608 | tf_op jit(solution)/shard_map/all_to_all | solution.py:162
  72.6 17.2 %collective-permute-start = (bf16[256,2048]{1,0:T(8,128)(2,1)S(1)}, bf16[256,2048]{1,0:T(8,128)(2,1)S(1)}, u32[]{:S(2)}, u32[]{:S(2)}) collective-permute-start(bf16[256,2048]{1,0:T(8,128)(2,1)S(1)} %bitcast.38), channel_id=1, source_target_pairs={{0,1},{1,0},{2,3},{3,2},{4,5},{5,4},{6,7},{7,6},{8,9},{9,8},{10,11... | collective-permute-start | bytes 3145736 | tf_op jit(solution)/shard_map/ppermute | solution.py:182
  80.7 1.7 %copy-start = (bf16[16,3,16,2,8,128]{5,4,3,2,1,0:T(8,128)(2,1)}, bf16[16,3,16,2,8,128]{5,4,3,2,1,0:T(8,128)(2,1)S(1)}, u32[]{:S(2)}) copy-start(bf16[16,3,16,2,8,128]{5,4,3,2,1,0:T(8,128)(2,1)S(1)} %get-tuple-element.17) | copy-start | bytes 9437188
  82.4 51.4 %all-to-all-start.1 = ((bf16[16,3,16,2,8,128]{5,4,3,2,1,0:T(8,128)(2,1)}), bf16[16,3,16,2,8,128]{5,4,3,2,1,0:T(8,128)(2,1)}, u32[]{:S(2)}, u32[]{:S(2)}) async-start(bf16[16,3,16,2,8,128]{5,4,3,2,1,0:T(8,128)(2,1)} %copy-done), calls=%async_computation.1 | async-start | bytes 6291456 | tf_op jit(solution)/shard_map/all_to_all | solution.py:179
  87.8 2.0 %collective-permute-start.1 = (bf16[256,1024]{1,0:T(8,128)(2,1)S(1)}, bf16[256,1024]{1,0:T(8,128)(2,1)S(1)}, u32[]{:S(2)}, u32[]{:S(2)}) collective-permute-start(bf16[256,1024]{1,0:T(8,128)(2,1)S(1)} %bitcast.58), channel_id=1, source_target_pairs={{0,1},{1,0},{2,3},{3,2},{4,5},{5,4},{6,7},{7,6},{8,9},{9,8},{10,11... | collective-permute-start | bytes 1572872 | tf_op jit(solution)/shard_map/ppermute | solution.py:184
  90.5 14.9 %collective-permute-start.2 = (bf16[512,512]{1,0:T(8,128)(2,1)S(1)}, bf16[512,512]{1,0:T(8,128)(2,1)S(1)}, u32[]{:S(2)}, u32[]{:S(2)}) collective-permute-start(bf16[512,512]{1,0:T(8,128)(2,1)S(1)} %get-tuple-element.13), channel_id=1, source_target_pairs={{0,32},{1,33},{2,34},{3,35},{4,36},{5,37},{6,38},{7,39},{8,40},{9,... | collective-permute-start | bytes 1572872 | tf_op jit(solution)/shard_map/ppermute | solution.py:190
  91.9 13.5 %collective-permute-start.3 = (bf16[512,512]{1,0:T(8,128)(2,1)S(1)}, bf16[512,512]{1,0:T(8,128)(2,1)S(1)}, u32[]{:S(2)}, u32[]{:S(2)}) collective-permute-start(bf16[512,512]{1,0:T(8,128)(2,1)S(1)} %get-tuple-element.14), channel_id=1, source_target_pairs={{0,96},{1,97},{2,98},{3,99},{4,100},{5,101},{6,102},{7,103},{8,104... | collective-permute-start | bytes 1572872 | tf_op jit(solution)/shard_map/ppermute | solution.py:191
  106.7 25.2 %collective-permute-start.4 = (bf16[512,1024]{1,0:T(8,128)(2,1)S(1)}, bf16[512,1024]{1,0:T(8,128)(2,1)S(1)}, u32[]{:S(2)}, u32[]{:S(2)}) collective-permute-start(bf16[512,1024]{1,0:T(8,128)(2,1)S(1)} %get-tuple-element.15), channel_id=1, source_target_pairs={{0,32},{1,33},{2,34},{3,35},{4,36},{5,37},{6,38},{7,39},{8,40},{9,... | collective-permute-start | bytes 3145736 | tf_op jit(solution)/shard_map/ppermute | solution.py:195
  107.7 24.2 %collective-permute-start.5 = (bf16[512,1024]{1,0:T(8,128)(2,1)S(1)}, bf16[512,1024]{1,0:T(8,128)(2,1)S(1)}, u32[]{:S(2)}, u32[]{:S(2)}) collective-permute-start(bf16[512,1024]{1,0:T(8,128)(2,1)S(1)} %get-tuple-element.16), channel_id=1, source_target_pairs={{0,96},{1,97},{2,98},{3,99},{4,100},{5,101},{6,102},{7,103},{8,104... | collective-permute-start | bytes 3145736 | tf_op jit(solution)/shard_map/ppermute | solution.py:196
  133.8 25.5 %all-to-all-start.2 = ((bf16[32,16,1024]{2,1,0:T(8,128)(2,1)}), bf16[32,16,1024]{2,1,0:T(8,128)(2,1)S(1)}, u32[]{:S(2)}, u32[]{:S(2)}) async-start(bf16[32,16,1024]{2,1,0:T(8,128)(2,1)} %bitcast.19), calls=%async_computation.2 | async-start | bytes 2097152 | tf_op jit(solution)/shard_map/all_to_all | solution.py:202

commit v3 on v2

v3 whole, which is shorter than its diff:
```python
import jax
import jax.numpy as jnp
from jax import lax
from jax.experimental import pallas as pl
from jax.experimental.pallas import tpu as pltpu
from jax.sharding import PartitionSpec as P

FRAMES, TOK, HEADS, E, DM = 16, 16, 16, 128, 2048
PATCH = 256
TOKENS = FRAMES * TOK
GROUPS, GROUP = 2, 8
ROWS = FRAMES * GROUP
STEP_TOK = 4
AXES = ("dp", "tm")
SCALE = 1.0 / (E**0.5)
EXP2_SCALE = SCALE * 1.4426950408889634
Y, PLANE = 4, 32
YROWS = DM // Y
HALF = DM // 2
VMEM = 16 * 1024 * 1024


def y_shift(n):
    total = Y * PLANE
    return [(i, (i + n * PLANE) % total) for i in range(total)]


def core_swap():
    return [(i, i ^ 1) for i in range(Y * PLANE)]


def planes():
    return [[y * PLANE + i for i in range(PLANE)] for y in range(Y)]


def dot_nt(a, b):
    return lax.dot_general(a, b, (((1,), (1,)), ((), ())), preferred_element_type=jnp.float32)


def dot_tn(a, b):
    return lax.dot_general(a, b, (((0,), (0,)), ((), ())), preferred_element_type=jnp.float32)


def dot_nn(a, b):
    return lax.dot_general(a, b, (((1,), (0,)), ((), ())), preferred_element_type=jnp.float32)


def attend_groups(units, bias):
    scores = [dot_nt(q, k) + bias for q, k, v, g in units]
    grad_probs = [dot_nt(g, v) for q, k, v, g in units]
    expd = [jnp.exp2((s - jnp.max(s, axis=1, keepdims=True)) * EXP2_SCALE) for s in scores]
    probs = [e * (1.0 / jnp.sum(e, axis=1, keepdims=True)) for e in expd]
    weights = [p.astype(jnp.bfloat16) for p in probs]
    grad_scores = [
        (p * (gp - jnp.sum(p * gp, axis=1, keepdims=True))).astype(jnp.bfloat16)
        for p, gp in zip(probs, grad_probs)
    ]
    attended = [dot_nn(w, u[2]).astype(jnp.bfloat16) for w, u in zip(weights, units)]
    gv = [dot_tn(w, u[3]).astype(jnp.bfloat16) for w, u in zip(weights, units)]
    gq = [(dot_nn(gs, u[1]) * SCALE).astype(jnp.bfloat16) for gs, u in zip(grad_scores, units)]
    gk = [(dot_tn(gs, u[0]) * SCALE).astype(jnp.bfloat16) for gs, u in zip(grad_scores, units)]
    return attended, zip(gq, gk, gv)


def attend_kernel(q_ref, k_ref, v_ref, g_ref, own_ref, other_ref, grads_ref, bias_ref):
    @pl.when(pl.program_id(0) == 0)
    def _():
        row = lax.broadcasted_iota(jnp.int32, (ROWS, ROWS), 0)
        col = lax.broadcasted_iota(jnp.int32, (ROWS, ROWS), 1)
        keep = (row % GROUP == col % GROUP) & (col <= row)
        bias_ref[...] = jnp.where(keep, 0.0, -jnp.inf)

    bias = bias_ref[...]
    first = lax.rem(lax.axis_index("tm"), 2) == 0
    ids = [(t, h) for t in range(STEP_TOK) for h in range(GROUPS)]
    units = []
    for t, h in ids:
        parts = [ref[:, 0, t, h] for ref in (q_ref, k_ref, v_ref)] + [g_ref[:, t, h]]
        units.append([part.reshape(ROWS, E) for part in parts])
    attended, grads = attend_groups(units, bias)
    for (t, h), three in zip(ids, grads):
        for n, grad in enumerate(three):
            grads_ref[:, n, t, h] = grad.reshape(FRAMES, GROUP, E)
    for t in range(STEP_TOK):
        low, high = (a.reshape(FRAMES, GROUP, E) for a in attended[GROUPS * t : GROUPS * (t + 1)])
        own_ref[:, t] = jnp.where(first, low, high)
        other_ref[:, t] = jnp.where(first, high, low)


def attend(packed, grad_attended):
    def part(n):
        block = (FRAMES, 1, STEP_TOK, GROUPS, GROUP, E)
        return pl.BlockSpec(block, lambda t, n=n: (0, n, t, 0, 0, 0))

    token = pl.BlockSpec((FRAMES, STEP_TOK, GROUPS, GROUP, E), lambda t: (0, t, 0, 0, 0))
    half = pl.BlockSpec((FRAMES, STEP_TOK, GROUP, E), lambda t: (0, t, 0, 0))
    grads = pl.BlockSpec((FRAMES, 3, STEP_TOK, GROUPS, GROUP, E), lambda t: (0, 0, t, 0, 0, 0))
    return pl.pallas_call(
        attend_kernel,
        grid=(TOK // STEP_TOK,),
        in_specs=[part(0), part(1), part(2), token],
        out_specs=[half, half, grads],
        out_shape=[
            jax.ShapeDtypeStruct((FRAMES, TOK, GROUP, E), jnp.bfloat16),
            jax.ShapeDtypeStruct((FRAMES, TOK, GROUP, E), jnp.bfloat16),
            pltpu.HBM((FRAMES, 3, TOK, GROUPS, GROUP, E), jnp.bfloat16),
        ],
        scratch_shapes=[pltpu.VMEM((ROWS, ROWS), jnp.float32)],
        compiler_params=pltpu.CompilerParams(vmem_limit_bytes=VMEM),
        cost_estimate=pl.CostEstimate(flops=7 * 10**9, bytes_accessed=8 * 2**20, transcendentals=0),
    )(packed, packed, packed, grad_attended)


QUARTER = HALF // 2


def cut(ref, part):
    return ref[:, part * QUARTER : (part + 1) * QUARTER]


def plane_rows(ref, n):
    y = lax.div(lax.axis_index("dp"), 2)
    start = pl.multiple_of(lax.rem(y + n, Y) * YROWS, YROWS)
    return ref[:, pl.ds(start, YROWS)]


def partial_sum(n, part, g_ref, gs_ref, a_ref, as_ref):
    near = dot_tn(plane_rows(g_ref, n), cut(a_ref, part))
    return near + dot_tn(plane_rows(gs_ref, n), cut(as_ref, part))


def first_kernel(*refs):
    ins, outs = refs[:4], refs[4:]
    for out, n, part in zip(outs, (2, 2, 1, 3), (0, 1, 1, 0)):
        out[...] = partial_sum(n, part, *ins).astype(jnp.bfloat16)


def second_kernel(*refs):
    ins, came, outs = refs[:4], refs[4:6], refs[6:]
    for out, n, part, add in zip(outs, (1, 3), (0, 1), came):
        out[...] = (partial_sum(n, part, *ins) + add[...]).astype(jnp.bfloat16)


def own_kernel(*refs):
    ins, came, out = refs[:4], refs[4:8], refs[8]
    for part in range(2):
        total = partial_sum(0, part, *ins) + came[part][...] + came[2 + part][...]
        out[:, part * QUARTER : (part + 1) * QUARTER] = total.astype(jnp.bfloat16)


def weight_step(kernel, args, widths):
    whole = pl.BlockSpec(memory_space=pltpu.VMEM)
    return pl.pallas_call(
        kernel,
        in_specs=[whole] * len(args),
        out_specs=[whole] * len(widths),
        out_shape=[jax.ShapeDtypeStruct((YROWS, w), jnp.bfloat16) for w in widths],
        compiler_params=pltpu.CompilerParams(vmem_limit_bytes=VMEM),
        cost_estimate=pl.CostEstimate(flops=10**9, bytes_accessed=4 * 2**20, transcendentals=0),
    )(*args)


def shards(queries, keys, values, out_weight, grad_out):
    tiles = TOK * 2
    pieces = [t.reshape(FRAMES, tiles, 8, E) for t in (queries, keys, values)]
    pieces.append(
        grad_out.reshape(FRAMES, 2, 8, HEADS, E).transpose(0, 1, 3, 2, 4).reshape(FRAMES, tiles, 8, E)
    )
    packed = jnp.concatenate(pieces, axis=1)
    packed = lax.all_to_all(packed, "tm", split_axis=0, concat_axis=0, tiled=True)
    g_tok = (
        packed[:, 3 * tiles :]
        .reshape(FRAMES, 2, HEADS, 8, E)
        .transpose(0, 1, 3, 2, 4)
        .reshape(TOKENS, DM)
    )
    grad_attended = jnp.einsum(
        "td,dhe->the", g_tok, out_weight, preferred_element_type=jnp.float32
    ).astype(jnp.bfloat16)
    own, other, grads = attend(
        packed.reshape(FRAMES, 4, TOK, GROUPS, GROUP, E),
        grad_attended.reshape(FRAMES, TOK, GROUPS, GROUP, E),
    )

    back = lax.all_to_all(grads, "tm", split_axis=0, concat_axis=0, tiled=True)

    own = own.reshape(TOKENS, HALF)
    g_swapped = lax.ppermute(g_tok, AXES, core_swap())
    swapped = lax.ppermute(other.reshape(TOKENS, HALF), AXES, core_swap())

    ins = [g_tok, g_swapped, own, swapped]
    left, right, up1, down0 = weight_step(first_kernel, ins, [QUARTER] * 4)
    left = lax.ppermute(left, AXES, y_shift(1))
    right = lax.ppermute(right, AXES, y_shift(-1))
    up1 = lax.ppermute(up1, AXES, y_shift(1))
    down0 = lax.ppermute(down0, AXES, y_shift(-1))
    up0, down1 = weight_step(second_kernel, [*ins, left, right], [QUARTER] * 2)
    up0 = lax.ppermute(up0, AXES, y_shift(1))
    down1 = lax.ppermute(down1, AXES, y_shift(-1))
    (block,) = weight_step(own_kernel, [*ins, up0, up1, down0, down1], [HALF])

    block, back = lax.optimization_barrier((block, back))
    block = lax.all_to_all(
        block, AXES, split_axis=0, concat_axis=0, tiled=True, axis_index_groups=planes()
    )
    shape = (1, 1, PATCH, HEADS, E)
    outs = [back[:, n].reshape(shape) for n in range(3)]
    rows = DM // (Y * PLANE)
    total = jnp.sum(block.reshape(PLANE // 2, 2, rows, HALF).astype(jnp.float32), axis=0)
    grad_weight = total.transpose(1, 0, 2).reshape(rows, HEADS, E)
    return (*outs, grad_weight)


def solution(mesh):
    clip = P("dp", "tm", None, None, None)
    return jax.shard_map(
        shards,
        mesh=mesh,
        in_specs=(clip, clip, clip, P(), P("dp", "tm", None, None)),
        out_specs=(clip, clip, clip, P(AXES, None, None)),
        check_vma=False,
    )
```

time: 161 us -> 148 us (0.919)
  blocking collectives: 0 us -> 60 us
  waiting for transfers between devices: 99.3 us -> 43.6 us
  starting transfers between devices: 28.9 us -> 22.6 us
  local copies, waits for them, and re-layouts: 10.6 us -> 5.82 us
  matrix products: 5.75 us -> 2.37 us
    all_to_all x0 -> x1, blocking collectives: none -> 60 us  [shards(): lax.all_to_all(packed, 'tm', split_axis=0, concat_axis=0, tiled=True)]
    all_to_all x1 -> x0, waiting for transfers between devices: 51.1 us -> none  [shards(): lax.all_to_all(packed, 'tm', split_axis=0, concat_axis=0, tiled=True)]
    all_to_all x1 -> x0, starting transfers between devices: 9.29 us -> none  [shards(): lax.all_to_all(packed, 'tm', split_axis=0, concat_axis=0, tiled=True)]
    dot_general x1, matrix products: 5.75 us -> 2.37 us  [shards(): jnp.einsum('td,dhe->the', g_tok, out_weight, preferred_element_type=jnp.f...]
    ppermute x1, waiting for transfers between devices: 12 us -> 9.09 us  [shards(): left = lax.ppermute(left, AXES, y_shift(1))]
    unnamed x4 -> x6, local copies, waits for them, and re-layouts: 2.89 us -> 0.2 us
    ppermute x3 -> x5, starting transfers between devices: 2.97 us -> 5.66 us  [the longest x1 2.67 us: shards(): down0 = lax.ppermute(down0, AXES, y_shift(-1))]
    ppermute x3 -> x5, waiting for transfers between devices: 23.1 us -> 21.5 us  [the longest x1 11.1 us: shards(): up0 = lax.ppermute(up0, AXES, y_shift(1))]
  transfers between devices with their start and end apart: 9 -> 10, of which waited for: 5 -> 5; matrix products, arithmetic and copies ran while one was open for 4% -> 3% of each run, Pallas kernels for 7% -> 3%
where the time goes in v3:
time: 148 us; the launch traced here: 147 us
  blocking collectives  60 us (41%)
  waiting for transfers between devices  43.6 us (29%)
  starting transfers between devices  22.6 us (15%)
  Pallas kernels  9.49 us (6%)
  local copies, waits for them, and re-layouts  5.82 us (4%)
  other arithmetic  2.77 us (2%)
  matrix products  2.37 us (2%)
    all_to_all x1, blocking collectives, shards(): lax.all_to_all(packed, 'tm', split_axis=0, concat_axis=0, tiled=True)  60 us
    all_to_all x1, waiting for transfers between devices, shards(): lax.all_to_all(block, AXES, split_axis=0, concat_axis=0, tiled=True, axis...  13.1 us
    ppermute x1, waiting for transfers between devices, shards(): up0 = lax.ppermute(up0, AXES, y_shift(1))  11.1 us
    ppermute x1, waiting for transfers between devices, shards(): left = lax.ppermute(left, AXES, y_shift(1))  9.09 us
    all_to_all x1, starting transfers between devices, shards(): lax.all_to_all(block, AXES, split_axis=0, concat_axis=0, tiled=True, axis...  8.36 us
    ppermute x1, waiting for transfers between devices, shards(): up1 = lax.ppermute(up1, AXES, y_shift(1))  7.71 us
    pallas_call x1, Pallas kernels, attend(): pl.pallas_call(attend_kernel, grid=(TOK // STEP_TOK,), in_specs=[part(0),...  5.57 us
    all_to_all x1, starting transfers between devices, shards(): back = lax.all_to_all(grads, 'tm', split_axis=0, concat_axis=0, tiled=True)  5.4 us
  transfers between devices with their start and end apart: 10, of which 5 were waited for; matrix products, arithmetic and copies ran while one was open for 3% of the time, Pallas kernels for 3%

profile of v3, /device:TPU:1, one launch (start us, length us, event | category | flops | bytes accessed | tf_op | source)
XLA Modules:
  0.0 147.5 jit_solution(2634393679681269000)
XLA Ops:
  0.6 0.0 slice-start
  0.6 2.6 %pad_maximum_fusion = bf16[16,128,8,128]{3,2,1,0:T(8,128)(2,1)S(1)} fusion(bf16[16,32,8,128]{3,2,1,0:T(8,128)(2,1)} %bitcast.53, bf16[16,32,8,128]{3,2,1,0:T(8,128)(2,1)} %bitcast.54, bf16[16,32,8,128]{3,2,1,0:T(8,128)(2,1)} %bitcast.55, bf16[16,32,8,128]{3,2,1,0:T(8,128)(2,1)} %bitcast.56), kind=kLoop, calls=%fused_computation.2 | loop fusion | flops 6291456 | bytes 8388608 | tf_op jit(solution)/shard_map/concatenate | solution.py:169
  3.2 0.0 slice-start.1
  3.3 60.0 %all_to_all.19 = bf16[16,128,8,128]{3,2,1,0:T(8,128)(2,1)S(1)} all-to-all(bf16[16,128,8,128]{3,2,1,0:T(8,128)(2,1)S(1)} %pad_maximum_fusion), channel_id=1, replica_groups=mesh['dp'=8,'tm'=16] {'tm'}, dimensions={0} | all-to-all | bytes 8388608 | tf_op jit(solution)/shard_map/all_to_all | solution.py:170
  63.2 0.1 slice.16
  63.3 0.0 slice-done
  63.3 0.0 slice-done.1
  63.3 2.4 %fusion.2 = bf16[256,16,128]{2,0,1:T(8,128)(2,1)S(1)} fusion(bf16[256,2048,1]{1,0,2:T(8,128)(2,1)S(1)} %bitcast.35, bf16[2048,16,128]{2,1,0:T(8,128)(2,1)S(1)} %bitcast.60), kind=kOutput, calls=%fused_computation.4 | convolution fusion | flops 2148007936 | bytes 10485760 | tf_op jit(solution)/shard_map/td,dhe->the/dot_general | solution.py:177
  65.7 0.7 copy.14
  66.4 5.6 %shard_map.84 = (bf16[16,16,8,128]{3,2,1,0:T(8,128)(2,1)S(1)}, bf16[16,16,8,128]{3,2,1,0:T(8,128)(2,1)S(1)}, bf16[16,3,16,2,8,128]{5,4,3,2,1,0:T(8,128)(2,1)}) custom-call(bf16[16,4,16,2,8,128]{5,4,3,2,1,0:T(8,128)(2,1)S(1)} %bitcast.40, bf16[16,4,16,2,8,128]{5,4,3,2,1,0:T(8,128)(2,1)S(1)} %bitcast.41, bf16[16,4,16,2,8,128]{5,4,3,2,1,0:T(8,128)(2,1)S(1)} %bitcast.42, ...), custom_call_target="tpu_custom_call" | custom-call | flops 7000000000 | bytes 8388608 | tf_op jit(solution)/shard_map/pallas_call | solution.py:98
  72.0 5.4 %all-to-all-start.1 = ((bf16[16,3,16,2,8,128]{5,4,3,2,1,0:T(8,128)(2,1)}), bf16[16,3,16,2,8,128]{5,4,3,2,1,0:T(8,128)(2,1)}, u32[]{:S(2)}, u32[]{:S(2)}) async-start(bf16[16,3,16,2,8,128]{5,4,3,2,1,0:T(8,128)(2,1)} %get-tuple-element.23), calls=%async_computation.1 | async-start | bytes 6291456 | tf_op jit(solution)/shard_map/all_to_all | solution.py:185
  77.4 0.4 collective-permute-start
  77.7 0.1 copy.24
  77.8 0.2 collective-permute-start.1
  78.1 0.1 copy.25
  78.2 2.6 %collective-permute-done.1.refs_3_ = bf16[256,1024]{1,0:T(8,128)(2,1)S(1)} collective-permute-done((bf16[256,1024]{1,0:T(8,128)(2,1)S(1)}, bf16[256,1024]{1,0:T(8,128)(2,1)S(1)}, u32[]{:S(2)}, u32[]{:S(2)}) %collective-permute-start.1) | collective-permute-done | bytes 524320 | tf_op jit(solution)/shard_map/ppermute | solution.py:189
  80.8 0.0 collective-permute-done.refs_1_
  80.8 1.3 shard_map.85
  82.1 1.4 collective-permute-start.2
  83.5 1.5 %collective-permute-start.3 = (bf16[512,512]{1,0:T(8,128)(2,1)S(1)}, bf16[512,512]{1,0:T(8,128)(2,1)S(1)}, u32[]{:S(2)}, u32[]{:S(2)}) collective-permute-start(bf16[512,512]{1,0:T(8,128)(2,1)S(1)} %get-tuple-element.18), channel_id=1, source_target_pairs={{0,96},{1,97},{2,98},{3,99},{4,100},{5,101},{6,102},{7,103},{8,104... | collective-permute-start | bytes 1572872 | tf_op jit(solution)/shard_map/ppermute | solution.py:194
  85.0 0.0 collective-permute-start.5
  85.0 2.7 %collective-permute-start.6 = (bf16[512,512]{1,0:T(8,128)(2,1)S(1)}, bf16[512,512]{1,0:T(8,128)(2,1)S(1)}, u32[]{:S(2)}, u32[]{:S(2)}) collective-permute-start(bf16[512,512]{1,0:T(8,128)(2,1)S(1)} %get-tuple-element.21), channel_id=1, source_target_pairs={{0,96},{1,97},{2,98},{3,99},{4,100},{5,101},{6,102},{7,103},{8,104... | collective-permute-start | bytes 1572872 | tf_op jit(solution)/shard_map/ppermute | solution.py:196
  87.7 9.1 %collective-permute-done.2.refs_4_ = bf16[512,512]{1,0:T(8,128)(2,1)S(1)} collective-permute-done((bf16[512,512]{1,0:T(8,128)(2,1)S(1)}, bf16[512,512]{1,0:T(8,128)(2,1)S(1)}, u32[]{:S(2)}, u32[]{:S(2)}) %collective-permute-start.2) | collective-permute-done | bytes 524320 | tf_op jit(solution)/shard_map/ppermute | solution.py:193
  96.7 0.0 collective-permute-done.3.refs_5_
  96.7 0.8 shard_map.86
  97.5 1.0 collective-permute-start.4
  98.5 1.7 %collective-permute-start.7 = (bf16[512,512]{1,0:T(8,128)(2,1)S(1)}, bf16[512,512]{1,0:T(8,128)(2,1)S(1)}, u32[]{:S(2)}, u32[]{:S(2)}) collective-permute-start(bf16[512,512]{1,0:T(8,128)(2,1)S(1)} %get-tuple-element.22), channel_id=1, source_target_pairs={{0,96},{1,97},{2,98},{3,99},{4,100},{5,101},{6,102},{7,103},{8,104... | collective-permute-start | bytes 1572872 | tf_op jit(solution)/shard_map/ppermute | solution.py:199
  100.3 7.7 %collective-permute-done.5.refs_5_ = bf16[512,512]{1,0:T(8,128)(2,1)S(1)} collective-permute-done((bf16[512,512]{1,0:T(8,128)(2,1)S(1)}, bf16[512,512]{1,0:T(8,128)(2,1)S(1)}, u32[]{:S(2)}, u32[]{:S(2)}) %collective-permute-start.5) | collective-permute-done | bytes 524320 | tf_op jit(solution)/shard_map/ppermute | solution.py:195
  108.0 0.0 collective-permute-done.6.refs_6_
  108.0 11.1 %collective-permute-done.4.refs_4_ = bf16[512,512]{1,0:T(8,128)(2,1)S(1)} collective-permute-done((bf16[512,512]{1,0:T(8,128)(2,1)S(1)}, bf16[512,512]{1,0:T(8,128)(2,1)S(1)}, u32[]{:S(2)}, u32[]{:S(2)}) %collective-permute-start.4) | collective-permute-done | bytes 524320 | tf_op jit(solution)/shard_map/ppermute | solution.py:198
  119.1 0.0 collective-permute-done.7.refs_7_
  119.1 1.8 %shard_map.87 = bf16[512,1024]{1,0:T(8,128)(2,1)} custom-call(bf16[256,2048]{1,0:T(8,128)(2,1)S(1)} %bitcast.39, bf16[256,2048]{1,0:T(8,128)(2,1)S(1)} %collective-permute-done.refs_1_, bf16[256,1024]{1,0:T(8,128)(2,1)S(1)} %bitcast.45, bf16[256,1024]{1,0:T(8,128)(2,1)S(1)} %collective-permute-done.1.refs_3_, ...), custom_call_target="tpu_custom_call" | custom-call | flops 1000000000 | bytes 4194304 | tf_op jit(solution)/shard_map/pallas_call | solution.py:153
  120.9 0.0 all-to-all-done.1
  121.0 8.4 %all-to-all-start.2 = ((bf16[32,16,1024]{2,1,0:T(8,128)(2,1)}), bf16[32,16,1024]{2,1,0:T(8,128)(2,1)S(1)}, u32[]{:S(2)}, u32[]{:S(2)}) async-start(bf16[32,16,1024]{2,1,0:T(8,128)(2,1)} %bitcast.17), calls=%async_computation.2 | async-start | bytes 2097152 | tf_op jit(solution)/shard_map/all_to_all | solution.py:203
  129.3 4.0 %fusion.5 = (bf16[16,1,16,2,8,128]{5,4,3,2,1,0:T(8,128)(2,1)}, bf16[16,1,16,2,8,128]{5,4,3,2,1,0:T(8,128)(2,1)}, bf16[16,1,16,2,8,128]{5,4,3,2,1,0:T(8,128)(2,1)}) fusion(bf16[16,3,16,2,8,128]{5,4,3,2,1,0:T(8,128)(2,1)} %all-to-all-done.1), kind=kLoop, calls=%fused_computation.7 | loop fusion | bytes 6291456 | tf_op jit(solution)/shard_map/slice | solution.py:207
  133.3 13.1 %all-to-all-done.2 = bf16[32,16,1024]{2,1,0:T(8,128)(2,1)S(1)} async-done(((bf16[32,16,1024]{2,1,0:T(8,128)(2,1)}), bf16[32,16,1024]{2,1,0:T(8,128)(2,1)S(1)}, u32[]{:S(2)}, u32[]{:S(2)}) %all-to-all-start.2) | async-done | bytes 1048608 | tf_op jit(solution)/shard_map/all_to_all | solution.py:203
  146.4 0.2 convert_reduce_fusion
  146.6 0.1 copy.15
  146.7 0.8 reshape.61
  (1 shorter events, 0.0 us)
Async XLA Ops:
  0.6 62.7 %slice-start = ((s8[8388608]{0:T(1024)(128)(4,1)}), s8[4194304]{0:T(1024)(128)(4,1)S(1)}, s32[]{:S(2)}) async-start(s8[8388608]{0:T(1024)(128)(4,1)} %bitcast.59), calls=%async_computation.3 | async-start | bytes 8388608
  3.2 60.1 %slice-start.1 = ((s8[8388608]{0:T(1024)(128)(4,1)}), s8[4194304]{0:T(1024)(128)(4,1)S(1)}, s32[]{:S(2)}) async-start(s8[8388608]{0:T(1024)(128)(4,1)} %bitcast.59), calls=%async_computation.4 | async-start | bytes 8388608
  72.0 49.0 %all-to-all-start.1 = ((bf16[16,3,16,2,8,128]{5,4,3,2,1,0:T(8,128)(2,1)}), bf16[16,3,16,2,8,128]{5,4,3,2,1,0:T(8,128)(2,1)}, u32[]{:S(2)}, u32[]{:S(2)}) async-start(bf16[16,3,16,2,8,128]{5,4,3,2,1,0:T(8,128)(2,1)} %get-tuple-element.23), calls=%async_computation.1 | async-start | bytes 6291456 | tf_op jit(solution)/shard_map/all_to_all | solution.py:185
  77.4 3.4 %collective-permute-start = (bf16[256,2048]{1,0:T(8,128)(2,1)S(1)}, bf16[256,2048]{1,0:T(8,128)(2,1)S(1)}, u32[]{:S(2)}, u32[]{:S(2)}) collective-permute-start(bf16[256,2048]{1,0:T(8,128)(2,1)S(1)} %bitcast.36), channel_id=1, source_target_pairs={{0,1},{1,0},{2,3},{3,2},{4,5},{5,4},{6,7},{7,6},{8,9},{9,8},{10,11... | collective-permute-start | bytes 3145736 | tf_op jit(solution)/shard_map/ppermute | solution.py:188
  77.8 3.0 %collective-permute-start.1 = (bf16[256,1024]{1,0:T(8,128)(2,1)S(1)}, bf16[256,1024]{1,0:T(8,128)(2,1)S(1)}, u32[]{:S(2)}, u32[]{:S(2)}) collective-permute-start(bf16[256,1024]{1,0:T(8,128)(2,1)S(1)} %bitcast.58), channel_id=1, source_target_pairs={{0,1},{1,0},{2,3},{3,2},{4,5},{5,4},{6,7},{7,6},{8,9},{9,8},{10,11... | collective-permute-start | bytes 1572872 | tf_op jit(solution)/shard_map/ppermute | solution.py:189
  82.1 14.6 %collective-permute-start.2 = (bf16[512,512]{1,0:T(8,128)(2,1)S(1)}, bf16[512,512]{1,0:T(8,128)(2,1)S(1)}, u32[]{:S(2)}, u32[]{:S(2)}) collective-permute-start(bf16[512,512]{1,0:T(8,128)(2,1)S(1)} %get-tuple-element.17), channel_id=1, source_target_pairs={{0,32},{1,33},{2,34},{3,35},{4,36},{5,37},{6,38},{7,39},{8,40},{9,... | collective-permute-start | bytes 1572872 | tf_op jit(solution)/shard_map/ppermute | solution.py:193
  83.5 13.3 %collective-permute-start.3 = (bf16[512,512]{1,0:T(8,128)(2,1)S(1)}, bf16[512,512]{1,0:T(8,128)(2,1)S(1)}, u32[]{:S(2)}, u32[]{:S(2)}) collective-permute-start(bf16[512,512]{1,0:T(8,128)(2,1)S(1)} %get-tuple-element.18), channel_id=1, source_target_pairs={{0,96},{1,97},{2,98},{3,99},{4,100},{5,101},{6,102},{7,103},{8,104... | collective-permute-start | bytes 1572872 | tf_op jit(solution)/shard_map/ppermute | solution.py:194
  85.0 23.0 %collective-permute-start.5 = (bf16[512,512]{1,0:T(8,128)(2,1)S(1)}, bf16[512,512]{1,0:T(8,128)(2,1)S(1)}, u32[]{:S(2)}, u32[]{:S(2)}) collective-permute-start(bf16[512,512]{1,0:T(8,128)(2,1)S(1)} %get-tuple-element.20), channel_id=1, source_target_pairs={{0,32},{1,33},{2,34},{3,35},{4,36},{5,37},{6,38},{7,39},{8,40},{9,... | collective-permute-start | bytes 1572872 | tf_op jit(solution)/shard_map/ppermute | solution.py:195
  85.0 23.0 %collective-permute-start.6 = (bf16[512,512]{1,0:T(8,128)(2,1)S(1)}, bf16[512,512]{1,0:T(8,128)(2,1)S(1)}, u32[]{:S(2)}, u32[]{:S(2)}) collective-permute-start(bf16[512,512]{1,0:T(8,128)(2,1)S(1)} %get-tuple-element.21), channel_id=1, source_target_pairs={{0,96},{1,97},{2,98},{3,99},{4,100},{5,101},{6,102},{7,103},{8,104... | collective-permute-start | bytes 1572872 | tf_op jit(solution)/shard_map/ppermute | solution.py:196
  97.5 21.6 %collective-permute-start.4 = (bf16[512,512]{1,0:T(8,128)(2,1)S(1)}, bf16[512,512]{1,0:T(8,128)(2,1)S(1)}, u32[]{:S(2)}, u32[]{:S(2)}) collective-permute-start(bf16[512,512]{1,0:T(8,128)(2,1)S(1)} %get-tuple-element.19), channel_id=1, source_target_pairs={{0,32},{1,33},{2,34},{3,35},{4,36},{5,37},{6,38},{7,39},{8,40},{9,... | collective-permute-start | bytes 1572872 | tf_op jit(solution)/shard_map/ppermute | solution.py:198
  98.5 20.6 %collective-permute-start.7 = (bf16[512,512]{1,0:T(8,128)(2,1)S(1)}, bf16[512,512]{1,0:T(8,128)(2,1)S(1)}, u32[]{:S(2)}, u32[]{:S(2)}) collective-permute-start(bf16[512,512]{1,0:T(8,128)(2,1)S(1)} %get-tuple-element.22), channel_id=1, source_target_pairs={{0,96},{1,97},{2,98},{3,99},{4,100},{5,101},{6,102},{7,103},{8,104... | collective-permute-start | bytes 1572872 | tf_op jit(solution)/shard_map/ppermute | solution.py:199
  121.0 25.4 %all-to-all-start.2 = ((bf16[32,16,1024]{2,1,0:T(8,128)(2,1)}), bf16[32,16,1024]{2,1,0:T(8,128)(2,1)S(1)}, u32[]{:S(2)}, u32[]{:S(2)}) async-start(bf16[32,16,1024]{2,1,0:T(8,128)(2,1)} %bitcast.17), calls=%async_computation.2 | async-start | bytes 2097152 | tf_op jit(solution)/shard_map/all_to_all | solution.py:203

commit v4 on v3

--- a/solution.py
+++ b/solution.py
@@ -129,10 +129,14 @@
     return near + dot_tn(plane_rows(gs_ref, n), cut(as_ref, part))
 
 
-def first_kernel(*refs):
-    ins, outs = refs[:4], refs[4:]
-    for out, n, part in zip(outs, (2, 2, 1, 3), (0, 1, 1, 0)):
-        out[...] = partial_sum(n, part, *ins).astype(jnp.bfloat16)
+def far_kernel(*refs):
+    for part, out in enumerate(refs[4:]):
+        out[...] = partial_sum(2, part, *refs[:4]).astype(jnp.bfloat16)
+
+
+def direct_kernel(*refs):
+    for out, n, part in zip(refs[4:], (1, 3), (1, 0)):
+        out[...] = partial_sum(n, part, *refs[:4]).astype(jnp.bfloat16)
 
 
 def second_kernel(*refs):
@@ -142,21 +146,25 @@
 
 
 def own_kernel(*refs):
-    ins, came, out = refs[:4], refs[4:8], refs[8]
-    for part in range(2):
-        total = partial_sum(0, part, *ins) + came[part][...] + came[2 + part][...]
-        out[:, part * QUARTER : (part + 1) * QUARTER] = total.astype(jnp.bfloat16)
-
-
-def weight_step(kernel, args, widths):
+    ins, came, outs = refs[:4], refs[4:6], refs[6:]
+    for part, (out, add) in enumerate(zip(outs, came)):
+        out[...] = partial_sum(0, part, *ins) + add[...]
+
+
+def last_kernel(own0, own1, came0, came1, out):
+    out[:, :QUARTER] = (own0[...] + came0[...]).astype(jnp.bfloat16)
+    out[:, QUARTER:] = (own1[...] + came1[...]).astype(jnp.bfloat16)
+
+
+def weight_step(kernel, args, widths, dtype=jnp.bfloat16):
     whole = pl.BlockSpec(memory_space=pltpu.VMEM)
     return pl.pallas_call(
         kernel,
         in_specs=[whole] * len(args),
         out_specs=[whole] * len(widths),
-        out_shape=[jax.ShapeDtypeStruct((YROWS, w), jnp.bfloat16) for w in widths],
+        out_shape=[jax.ShapeDtypeStruct((YROWS, w), dtype) for w in widths],
         compiler_params=pltpu.CompilerParams(vmem_limit_bytes=VMEM),
-        cost_estimate=pl.CostEstimate(flops=10**9, bytes_accessed=4 * 2**20, transcendentals=0),
+        cost_estimate=pl.CostEstimate(flops=2 * 10**10, bytes_accessed=4 * 2**20, transcendentals=0),
     )(*args)
 
 
@@ -189,15 +197,18 @@
     swapped = lax.ppermute(other.reshape(TOKENS, HALF), AXES, core_swap())
 
     ins = [g_tok, g_swapped, own, swapped]
-    left, right, up1, down0 = weight_step(first_kernel, ins, [QUARTER] * 4)
+    pair = [QUARTER] * 2
+    left, right = weight_step(far_kernel, ins, pair)
     left = lax.ppermute(left, AXES, y_shift(1))
     right = lax.ppermute(right, AXES, y_shift(-1))
+    up1, down0 = weight_step(direct_kernel, ins, pair)
     up1 = lax.ppermute(up1, AXES, y_shift(1))
     down0 = lax.ppermute(down0, AXES, y_shift(-1))
-    up0, down1 = weight_step(second_kernel, [*ins, left, right], [QUARTER] * 2)
+    up0, down1 = weight_step(second_kernel, [*ins, left, right], pair)
     up0 = lax.ppermute(up0, AXES, y_shift(1))
     down1 = lax.ppermute(down1, AXES, y_shift(-1))
-    (block,) = weight_step(own_kernel, [*ins, up0, up1, down0, down1], [HALF])
+    own0, own1 = weight_step(own_kernel, [*ins, down0, up1], pair, jnp.float32)
+    (block,) = weight_step(last_kernel, [own0, own1, up0, down1], [HALF])
 
     block, back = lax.optimization_barrier((block, back))
     block = lax.all_to_all(

time: 148 us -> 145 us (0.980)
  starting transfers between devices: 22.6 us -> 20.4 us
  waiting for transfers between devices: 43.6 us -> 41.6 us
    ppermute x1, waiting for transfers between devices: 7.71 us -> 0.38 us  [shards(): up1 = lax.ppermute(up1, AXES, y_shift(1))]
    ppermute x1, waiting for transfers between devices: 0.01 us -> 7.33 us  [shards(): down0 = lax.ppermute(down0, AXES, y_shift(-1))]
    ppermute x1, waiting for transfers between devices: 2.62 us -> 0.01 us  [shards(): swapped = lax.ppermute(other.reshape(TOKENS, HALF), AXES, core_swap())]
    pallas_call x3 -> x5, Pallas kernels: 3.91 us -> 4.19 us  [weight_step(): pl.pallas_call(kernel, in_specs=[whole] * len(args), out_specs=[whole] *...]
  transfers between devices with their start and end apart: 10 -> 10, of which waited for: 5 -> 6; matrix products, arithmetic and copies ran while one was open for 3% -> 3% of each run, Pallas kernels for 3% -> 7%
where the time goes in v4:
time: 145 us; the launch traced here: 144 us
  blocking collectives  60 us (41%)
  waiting for transfers between devices  41.6 us (29%)
  starting transfers between devices  20.4 us (14%)
  Pallas kernels  9.78 us (7%)
  local copies, waits for them, and re-layouts  6.62 us (5%)
  other arithmetic  2.77 us (2%)
  matrix products  2.37 us (2%)
    all_to_all x1, blocking collectives, shards(): lax.all_to_all(packed, 'tm', split_axis=0, concat_axis=0, tiled=True)  60 us
    all_to_all x1, waiting for transfers between devices, shards(): lax.all_to_all(block, AXES, split_axis=0, concat_axis=0, tiled=True, axis...  13.1 us
    ppermute x1, waiting for transfers between devices, shards(): up0 = lax.ppermute(up0, AXES, y_shift(1))  10.5 us
    ppermute x1, waiting for transfers between devices, shards(): left = lax.ppermute(left, AXES, y_shift(1))  9.59 us
    ppermute x1, waiting for transfers between devices, shards(): down0 = lax.ppermute(down0, AXES, y_shift(-1))  7.33 us
    all_to_all x1, starting transfers between devices, shards(): lax.all_to_all(block, AXES, split_axis=0, concat_axis=0, tiled=True, axis...  7.25 us
    pallas_call x1, Pallas kernels, attend(): pl.pallas_call(attend_kernel, grid=(TOK // STEP_TOK,), in_specs=[part(0),...  5.59 us
    all_to_all x1, starting transfers between devices, shards(): back = lax.all_to_all(grads, 'tm', split_axis=0, concat_axis=0, tiled=True)  4.68 us
  transfers between devices with their start and end apart: 10, of which 6 were waited for; matrix products, arithmetic and copies ran while one was open for 3% of the time, Pallas kernels for 7%

profile of v4, /device:TPU:1, one launch (start us, length us, event | category | flops | bytes accessed | tf_op | source)
XLA Modules:
  0.0 144.3 jit_solution(10948601575976797408)
XLA Ops:
  0.6 0.0 slice-start
  0.6 2.6 %pad_maximum_fusion = bf16[16,128,8,128]{3,2,1,0:T(8,128)(2,1)S(1)} fusion(bf16[16,32,8,128]{3,2,1,0:T(8,128)(2,1)} %bitcast.55, bf16[16,32,8,128]{3,2,1,0:T(8,128)(2,1)} %bitcast.56, bf16[16,32,8,128]{3,2,1,0:T(8,128)(2,1)} %bitcast.57, bf16[16,32,8,128]{3,2,1,0:T(8,128)(2,1)} %bitcast.58), kind=kLoop, calls=%fused_computation.2 | loop fusion | flops 6291456 | bytes 8388608 | tf_op jit(solution)/shard_map/concatenate | solution.py:177
  3.2 0.0 slice-start.1
  3.2 60.0 %all_to_all.19 = bf16[16,128,8,128]{3,2,1,0:T(8,128)(2,1)S(1)} all-to-all(bf16[16,128,8,128]{3,2,1,0:T(8,128)(2,1)S(1)} %pad_maximum_fusion), channel_id=1, replica_groups=mesh['dp'=8,'tm'=16] {'tm'}, dimensions={0} | all-to-all | bytes 8388608 | tf_op jit(solution)/shard_map/all_to_all | solution.py:178
  63.2 0.1 slice.16
  63.3 0.0 slice-done
  63.3 0.0 slice-done.1
  63.3 2.4 %fusion.2 = bf16[256,16,128]{2,0,1:T(8,128)(2,1)S(1)} fusion(bf16[256,2048,1]{1,0,2:T(8,128)(2,1)S(1)} %bitcast.38, bf16[2048,16,128]{2,1,0:T(8,128)(2,1)S(1)} %bitcast.61), kind=kOutput, calls=%fused_computation.4 | convolution fusion | flops 2148007936 | bytes 10485760 | tf_op jit(solution)/shard_map/td,dhe->the/dot_general | solution.py:185
  65.7 0.7 copy.14
  66.4 1.2 collective-permute-start
  67.7 5.6 %shard_map.84 = (bf16[16,16,8,128]{3,2,1,0:T(8,128)(2,1)S(1)}, bf16[16,16,8,128]{3,2,1,0:T(8,128)(2,1)S(1)}, bf16[16,3,16,2,8,128]{5,4,3,2,1,0:T(8,128)(2,1)}) custom-call(bf16[16,4,16,2,8,128]{5,4,3,2,1,0:T(8,128)(2,1)S(1)} %bitcast.35, bf16[16,4,16,2,8,128]{5,4,3,2,1,0:T(8,128)(2,1)S(1)} %bitcast.36, bf16[16,4,16,2,8,128]{5,4,3,2,1,0:T(8,128)(2,1)S(1)} %bitcast.37, ...), custom_call_target="tpu_custom_call" | custom-call | flops 7000000000 | bytes 8388608 | tf_op jit(solution)/shard_map/pallas_call | solution.py:98
  73.2 0.9 copy.24
  74.1 0.1 collective-permute-start.1
  74.2 0.1 copy.25
  74.3 4.7 %all-to-all-start.1 = ((bf16[16,3,16,2,8,128]{5,4,3,2,1,0:T(8,128)(2,1)}), bf16[16,3,16,2,8,128]{5,4,3,2,1,0:T(8,128)(2,1)}, u32[]{:S(2)}, u32[]{:S(2)}) async-start(bf16[16,3,16,2,8,128]{5,4,3,2,1,0:T(8,128)(2,1)} %get-tuple-element.27), calls=%async_computation.1 | async-start | bytes 6291456 | tf_op jit(solution)/shard_map/all_to_all | solution.py:193
  79.0 0.0 collective-permute-done.1.refs_3_
  79.0 0.0 collective-permute-done.refs_1_
  79.0 0.8 shard_map.87
  79.8 1.4 collective-permute-start.4
  81.1 1.5 %collective-permute-start.5 = (bf16[512,512]{1,0:T(8,128)(2,1)S(1)}, bf16[512,512]{1,0:T(8,128)(2,1)S(1)}, u32[]{:S(2)}, u32[]{:S(2)}) collective-permute-start(bf16[512,512]{1,0:T(8,128)(2,1)S(1)} %get-tuple-element.24), channel_id=1, source_target_pairs={{0,96},{1,97},{2,98},{3,99},{4,100},{5,101},{6,102},{7,103},{8,104... | collective-permute-start | bytes 1572872 | tf_op jit(solution)/shard_map/ppermute | solution.py:203
  82.7 0.8 shard_map.85
  83.4 1.5 %collective-permute-start.2 = (bf16[512,512]{1,0:T(8,128)(2,1)S(1)}, bf16[512,512]{1,0:T(8,128)(2,1)S(1)}, u32[]{:S(2)}, u32[]{:S(2)}) collective-permute-start(bf16[512,512]{1,0:T(8,128)(2,1)S(1)} %get-tuple-element.19), channel_id=1, source_target_pairs={{0,96},{1,97},{2,98},{3,99},{4,100},{5,101},{6,102},{7,103},{8,104... | collective-permute-start | bytes 1572872 | tf_op jit(solution)/shard_map/ppermute | solution.py:206
  84.9 0.1 collective-permute-start.3
  84.9 9.6 %collective-permute-done.4.refs_4_ = bf16[512,512]{1,0:T(8,128)(2,1)S(1)} collective-permute-done((bf16[512,512]{1,0:T(8,128)(2,1)S(1)}, bf16[512,512]{1,0:T(8,128)(2,1)S(1)}, u32[]{:S(2)}, u32[]{:S(2)}) %collective-permute-start.4) | collective-permute-done | bytes 524320 | tf_op jit(solution)/shard_map/ppermute | solution.py:202
  94.5 0.0 collective-permute-done.5.refs_5_
  94.5 0.8 shard_map.88
  95.3 1.0 collective-permute-start.6
  96.3 1.8 %collective-permute-start.7 = (bf16[512,512]{1,0:T(8,128)(2,1)S(1)}, bf16[512,512]{1,0:T(8,128)(2,1)S(1)}, u32[]{:S(2)}, u32[]{:S(2)}) collective-permute-start(bf16[512,512]{1,0:T(8,128)(2,1)S(1)} %get-tuple-element.26), channel_id=1, source_target_pairs={{0,96},{1,97},{2,98},{3,99},{4,100},{5,101},{6,102},{7,103},{8,104... | collective-permute-start | bytes 1572872 | tf_op jit(solution)/shard_map/ppermute | solution.py:209
  98.1 7.3 %collective-permute-done.2.refs_4_ = bf16[512,512]{1,0:T(8,128)(2,1)S(1)} collective-permute-done((bf16[512,512]{1,0:T(8,128)(2,1)S(1)}, bf16[512,512]{1,0:T(8,128)(2,1)S(1)}, u32[]{:S(2)}, u32[]{:S(2)}) %collective-permute-start.2) | collective-permute-done | bytes 524320 | tf_op jit(solution)/shard_map/ppermute | solution.py:206
  105.4 0.4 collective-permute-done.3.refs_5_
  105.8 0.8 shard_map.86
  106.5 10.5 %collective-permute-done.6.came0 = bf16[512,512]{1,0:T(8,128)(2,1)S(1)} collective-permute-done((bf16[512,512]{1,0:T(8,128)(2,1)S(1)}, bf16[512,512]{1,0:T(8,128)(2,1)S(1)}, u32[]{:S(2)}, u32[]{:S(2)}) %collective-permute-start.6) | collective-permute-done | bytes 524320 | tf_op jit(solution)/shard_map/ppermute | solution.py:208
  117.0 0.0 collective-permute-done.7.came1
  117.0 1.2 shard_map.89
  118.2 0.7 all-to-all-done.1
  118.9 7.2 %all-to-all-start.2 = ((bf16[32,16,1024]{2,1,0:T(8,128)(2,1)}), bf16[32,16,1024]{2,1,0:T(8,128)(2,1)S(1)}, u32[]{:S(2)}, u32[]{:S(2)}) async-start(bf16[32,16,1024]{2,1,0:T(8,128)(2,1)} %bitcast.17), calls=%async_computation.2 | async-start | bytes 2097152 | tf_op jit(solution)/shard_map/all_to_all | solution.py:214
  126.2 4.0 %fusion.5 = (bf16[16,1,16,2,8,128]{5,4,3,2,1,0:T(8,128)(2,1)}, bf16[16,1,16,2,8,128]{5,4,3,2,1,0:T(8,128)(2,1)}, bf16[16,1,16,2,8,128]{5,4,3,2,1,0:T(8,128)(2,1)}) fusion(bf16[16,3,16,2,8,128]{5,4,3,2,1,0:T(8,128)(2,1)} %all-to-all-done.1), kind=kLoop, calls=%fused_computation.7 | loop fusion | bytes 6291456 | tf_op jit(solution)/shard_map/slice | solution.py:218
  130.2 13.1 %all-to-all-done.2 = bf16[32,16,1024]{2,1,0:T(8,128)(2,1)S(1)} async-done(((bf16[32,16,1024]{2,1,0:T(8,128)(2,1)}), bf16[32,16,1024]{2,1,0:T(8,128)(2,1)S(1)}, u32[]{:S(2)}, u32[]{:S(2)}) %all-to-all-start.2) | async-done | bytes 1048608 | tf_op jit(solution)/shard_map/all_to_all | solution.py:214
  143.2 0.2 convert_reduce_fusion
  143.4 0.1 copy.15
  143.5 0.8 reshape.61
  (1 shorter events, 0.0 us)
Async XLA Ops:
  0.6 62.7 %slice-start = ((s8[8388608]{0:T(1024)(128)(4,1)}), s8[4194304]{0:T(1024)(128)(4,1)S(1)}, s32[]{:S(2)}) async-start(s8[8388608]{0:T(1024)(128)(4,1)} %bitcast.60), calls=%async_computation.3 | async-start | bytes 8388608
  3.2 60.1 %slice-start.1 = ((s8[8388608]{0:T(1024)(128)(4,1)}), s8[4194304]{0:T(1024)(128)(4,1)S(1)}, s32[]{:S(2)}) async-start(s8[8388608]{0:T(1024)(128)(4,1)} %bitcast.60), calls=%async_computation.4 | async-start | bytes 8388608
  66.4 12.6 %collective-permute-start = (bf16[256,2048]{1,0:T(8,128)(2,1)S(1)}, bf16[256,2048]{1,0:T(8,128)(2,1)S(1)}, u32[]{:S(2)}, u32[]{:S(2)}) collective-permute-start(bf16[256,2048]{1,0:T(8,128)(2,1)S(1)} %bitcast.39), channel_id=1, source_target_pairs={{0,1},{1,0},{2,3},{3,2},{4,5},{5,4},{6,7},{7,6},{8,9},{9,8},{10,11... | collective-permute-start | bytes 3145736 | tf_op jit(solution)/shard_map/ppermute | solution.py:196
  74.1 4.8 %collective-permute-start.1 = (bf16[256,1024]{1,0:T(8,128)(2,1)}, bf16[256,1024]{1,0:T(8,128)(2,1)S(1)}, u32[]{:S(2)}, u32[]{:S(2)}) collective-permute-start(bf16[256,1024]{1,0:T(8,128)(2,1)} %bitcast.33), channel_id=1, source_target_pairs={{0,1},{1,0},{2,3},{3,2},{4,5},{5,4},{6,7},{7,6},{8,9},{9,8},{10,11... | collective-permute-start | bytes 1572872 | tf_op jit(solution)/shard_map/ppermute | solution.py:197
  74.3 44.6 %all-to-all-start.1 = ((bf16[16,3,16,2,8,128]{5,4,3,2,1,0:T(8,128)(2,1)}), bf16[16,3,16,2,8,128]{5,4,3,2,1,0:T(8,128)(2,1)}, u32[]{:S(2)}, u32[]{:S(2)}) async-start(bf16[16,3,16,2,8,128]{5,4,3,2,1,0:T(8,128)(2,1)} %get-tuple-element.27), calls=%async_computation.1 | async-start | bytes 6291456 | tf_op jit(solution)/shard_map/all_to_all | solution.py:193
  79.8 14.8 %collective-permute-start.4 = (bf16[512,512]{1,0:T(8,128)(2,1)S(1)}, bf16[512,512]{1,0:T(8,128)(2,1)S(1)}, u32[]{:S(2)}, u32[]{:S(2)}) collective-permute-start(bf16[512,512]{1,0:T(8,128)(2,1)S(1)} %get-tuple-element.23), channel_id=1, source_target_pairs={{0,32},{1,33},{2,34},{3,35},{4,36},{5,37},{6,38},{7,39},{8,40},{9,... | collective-permute-start | bytes 1572872 | tf_op jit(solution)/shard_map/ppermute | solution.py:202
  81.1 13.4 %collective-permute-start.5 = (bf16[512,512]{1,0:T(8,128)(2,1)S(1)}, bf16[512,512]{1,0:T(8,128)(2,1)S(1)}, u32[]{:S(2)}, u32[]{:S(2)}) collective-permute-start(bf16[512,512]{1,0:T(8,128)(2,1)S(1)} %get-tuple-element.24), channel_id=1, source_target_pairs={{0,96},{1,97},{2,98},{3,99},{4,100},{5,101},{6,102},{7,103},{8,104... | collective-permute-start | bytes 1572872 | tf_op jit(solution)/shard_map/ppermute | solution.py:203
  83.4 22.0 %collective-permute-start.2 = (bf16[512,512]{1,0:T(8,128)(2,1)S(1)}, bf16[512,512]{1,0:T(8,128)(2,1)S(1)}, u32[]{:S(2)}, u32[]{:S(2)}) collective-permute-start(bf16[512,512]{1,0:T(8,128)(2,1)S(1)} %get-tuple-element.19), channel_id=1, source_target_pairs={{0,96},{1,97},{2,98},{3,99},{4,100},{5,101},{6,102},{7,103},{8,104... | collective-permute-start | bytes 1572872 | tf_op jit(solution)/shard_map/ppermute | solution.py:206
  84.9 20.9 %collective-permute-start.3 = (bf16[512,512]{1,0:T(8,128)(2,1)S(1)}, bf16[512,512]{1,0:T(8,128)(2,1)S(1)}, u32[]{:S(2)}, u32[]{:S(2)}) collective-permute-start(bf16[512,512]{1,0:T(8,128)(2,1)S(1)} %get-tuple-element.20), channel_id=1, source_target_pairs={{0,32},{1,33},{2,34},{3,35},{4,36},{5,37},{6,38},{7,39},{8,40},{9,... | collective-permute-start | bytes 1572872 | tf_op jit(solution)/shard_map/ppermute | solution.py:205
  95.3 21.7 %collective-permute-start.6 = (bf16[512,512]{1,0:T(8,128)(2,1)S(1)}, bf16[512,512]{1,0:T(8,128)(2,1)S(1)}, u32[]{:S(2)}, u32[]{:S(2)}) collective-permute-start(bf16[512,512]{1,0:T(8,128)(2,1)S(1)} %get-tuple-element.25), channel_id=1, source_target_pairs={{0,32},{1,33},{2,34},{3,35},{4,36},{5,37},{6,38},{7,39},{8,40},{9,... | collective-permute-start | bytes 1572872 | tf_op jit(solution)/shard_map/ppermute | solution.py:208
  96.3 20.7 %collective-permute-start.7 = (bf16[512,512]{1,0:T(8,128)(2,1)S(1)}, bf16[512,512]{1,0:T(8,128)(2,1)S(1)}, u32[]{:S(2)}, u32[]{:S(2)}) collective-permute-start(bf16[512,512]{1,0:T(8,128)(2,1)S(1)} %get-tuple-element.26), channel_id=1, source_target_pairs={{0,96},{1,97},{2,98},{3,99},{4,100},{5,101},{6,102},{7,103},{8,104... | collective-permute-start | bytes 1572872 | tf_op jit(solution)/shard_map/ppermute | solution.py:209
  118.9 24.3 %all-to-all-start.2 = ((bf16[32,16,1024]{2,1,0:T(8,128)(2,1)}), bf16[32,16,1024]{2,1,0:T(8,128)(2,1)S(1)}, u32[]{:S(2)}, u32[]{:S(2)}) async-start(bf16[32,16,1024]{2,1,0:T(8,128)(2,1)} %bitcast.17), calls=%async_computation.2 | async-start | bytes 2097152 | tf_op jit(solution)/shard_map/all_to_all | solution.py:214

commit v5 on v4

--- a/solution.py
+++ b/solution.py
@@ -11,6 +11,7 @@
 GROUPS, GROUP = 2, 8
 ROWS = FRAMES * GROUP
 STEP_TOK = 4
+STEPS = TOK // STEP_TOK
 AXES = ("dp", "tm")
 SCALE = 1.0 / (E**0.5)
 EXP2_SCALE = SCALE * 1.4426950408889634
@@ -46,69 +47,73 @@
 
 
 def attend_groups(units, bias):
-    scores = [dot_nt(q, k) + bias for q, k, v, g in units]
-    grad_probs = [dot_nt(g, v) for q, k, v, g in units]
-    expd = [jnp.exp2((s - jnp.max(s, axis=1, keepdims=True)) * EXP2_SCALE) for s in scores]
-    probs = [e * (1.0 / jnp.sum(e, axis=1, keepdims=True)) for e in expd]
+    scores = [dot_nt(k, q) + bias for q, k, v, g in units]
+    grad_probs = [dot_nt(v, g) for q, k, v, g in units]
+    expd = [jnp.exp2((s - jnp.max(s, axis=0, keepdims=True)) * EXP2_SCALE) for s in scores]
+    probs = [e * (1.0 / jnp.sum(e, axis=0, keepdims=True)) for e in expd]
     weights = [p.astype(jnp.bfloat16) for p in probs]
     grad_scores = [
-        (p * (gp - jnp.sum(p * gp, axis=1, keepdims=True))).astype(jnp.bfloat16)
+        (p * (gp - jnp.sum(p * gp, axis=0, keepdims=True))).astype(jnp.bfloat16)
         for p, gp in zip(probs, grad_probs)
     ]
-    attended = [dot_nn(w, u[2]).astype(jnp.bfloat16) for w, u in zip(weights, units)]
-    gv = [dot_tn(w, u[3]).astype(jnp.bfloat16) for w, u in zip(weights, units)]
-    gq = [(dot_nn(gs, u[1]) * SCALE).astype(jnp.bfloat16) for gs, u in zip(grad_scores, units)]
-    gk = [(dot_tn(gs, u[0]) * SCALE).astype(jnp.bfloat16) for gs, u in zip(grad_scores, units)]
+    gv = [dot_nn(w, u[3]).astype(jnp.bfloat16) for w, u in zip(weights, units)]
+    gk = [(dot_nn(gs, u[0]) * SCALE).astype(jnp.bfloat16) for gs, u in zip(grad_scores, units)]
+    attended = [dot_tn(w, u[2]).astype(jnp.bfloat16) for w, u in zip(weights, units)]
+    gq = [(dot_tn(gs, u[1]) * SCALE).astype(jnp.bfloat16) for gs, u in zip(grad_scores, units)]
     return attended, zip(gq, gk, gv)
 
 
-def attend_kernel(q_ref, k_ref, v_ref, g_ref, own_ref, other_ref, grads_ref, bias_ref):
-    @pl.when(pl.program_id(0) == 0)
-    def _():
-        row = lax.broadcasted_iota(jnp.int32, (ROWS, ROWS), 0)
-        col = lax.broadcasted_iota(jnp.int32, (ROWS, ROWS), 1)
-        keep = (row % GROUP == col % GROUP) & (col <= row)
-        bias_ref[...] = jnp.where(keep, 0.0, -jnp.inf)
-
-    bias = bias_ref[...]
+def attend_kernel(packed_ref, g_ref, own_ref, other_ref, grads_ref, bias_ref, out_ref, sems):
+    row = lax.broadcasted_iota(jnp.int32, (ROWS, ROWS), 0)
+    col = lax.broadcasted_iota(jnp.int32, (ROWS, ROWS), 1)
+    keep = (row % GROUP == col % GROUP) & (row <= col)
+    bias_ref[...] = jnp.where(keep, 0.0, -jnp.inf)
     first = lax.rem(lax.axis_index("tm"), 2) == 0
     ids = [(t, h) for t in range(STEP_TOK) for h in range(GROUPS)]
-    units = []
-    for t, h in ids:
-        parts = [ref[:, 0, t, h] for ref in (q_ref, k_ref, v_ref)] + [g_ref[:, t, h]]
-        units.append([part.reshape(ROWS, E) for part in parts])
-    attended, grads = attend_groups(units, bias)
-    for (t, h), three in zip(ids, grads):
-        for n, grad in enumerate(three):
-            grads_ref[:, n, t, h] = grad.reshape(FRAMES, GROUP, E)
-    for t in range(STEP_TOK):
-        low, high = (a.reshape(FRAMES, GROUP, E) for a in attended[GROUPS * t : GROUPS * (t + 1)])
-        own_ref[:, t] = jnp.where(first, low, high)
-        other_ref[:, t] = jnp.where(first, high, low)
+
+    def out_copy(step):
+        slot = step % 2
+        there = grads_ref.at[:, :, pl.ds(step * STEP_TOK, STEP_TOK)]
+        return pltpu.make_async_copy(out_ref.at[slot], there, sems.at[slot])
+
+    for step in range(STEPS):
+        start = step * STEP_TOK
+        units = []
+        for t, h in ids:
+            parts = [packed_ref[:, n, start + t, h] for n in range(3)] + [g_ref[:, start + t, h]]
+            units.append([part.reshape(ROWS, E) for part in parts])
+        attended, grads = attend_groups(units, bias_ref[...])
+        if step >= 2:
+            out_copy(step - 2).wait()
+        for (t, h), three in zip(ids, grads):
+            for n, grad in enumerate(three):
+                out_ref[step % 2, :, n, t, h] = grad.reshape(FRAMES, GROUP, E)
+        out_copy(step).start()
+        for t in range(STEP_TOK):
+            pair = attended[GROUPS * t : GROUPS * (t + 1)]
+            low, high = (a.reshape(FRAMES, GROUP, E) for a in pair)
+            own_ref[:, start + t] = jnp.where(first, low, high)
+            other_ref[:, start + t] = jnp.where(first, high, low)
+    for step in range(max(STEPS - 2, 0), STEPS):
+        out_copy(step).wait()
 
 
 def attend(packed, grad_attended):
-    def part(n):
-        block = (FRAMES, 1, STEP_TOK, GROUPS, GROUP, E)
-        return pl.BlockSpec(block, lambda t, n=n: (0, n, t, 0, 0, 0))
-
-    token = pl.BlockSpec((FRAMES, STEP_TOK, GROUPS, GROUP, E), lambda t: (0, t, 0, 0, 0))
-    half = pl.BlockSpec((FRAMES, STEP_TOK, GROUP, E), lambda t: (0, t, 0, 0))
-    grads = pl.BlockSpec((FRAMES, 3, STEP_TOK, GROUPS, GROUP, E), lambda t: (0, 0, t, 0, 0, 0))
+    whole = pl.BlockSpec(memory_space=pltpu.VMEM)
+    half = jax.ShapeDtypeStruct((FRAMES, TOK, GROUP, E), jnp.bfloat16)
     return pl.pallas_call(
         attend_kernel,
-        grid=(TOK // STEP_TOK,),
-        in_specs=[part(0), part(1), part(2), token],
-        out_specs=[half, half, grads],
-        out_shape=[
-            jax.ShapeDtypeStruct((FRAMES, TOK, GROUP, E), jnp.bfloat16),
-            jax.ShapeDtypeStruct((FRAMES, TOK, GROUP, E), jnp.bfloat16),
-            pltpu.HBM((FRAMES, 3, TOK, GROUPS, GROUP, E), jnp.bfloat16),
+        in_specs=[whole, whole],
+        out_specs=[whole, whole, pl.BlockSpec(memory_space=pltpu.HBM)],
+        out_shape=[half, half, pltpu.HBM((FRAMES, 3, TOK, GROUPS, GROUP, E), jnp.bfloat16)],
+        scratch_shapes=[
+            pltpu.VMEM((ROWS, ROWS), jnp.float32),
+            pltpu.VMEM((2, FRAMES, 3, STEP_TOK, GROUPS, GROUP, E), jnp.bfloat16),
+            pltpu.SemaphoreType.DMA((2,)),
         ],
-        scratch_shapes=[pltpu.VMEM((ROWS, ROWS), jnp.float32)],
         compiler_params=pltpu.CompilerParams(vmem_limit_bytes=VMEM),
         cost_estimate=pl.CostEstimate(flops=7 * 10**9, bytes_accessed=8 * 2**20, transcendentals=0),
-    )(packed, packed, packed, grad_attended)
+    )(packed, grad_attended)
 
 
 QUARTER = HALF // 2
@@ -166,6 +171,27 @@
         compiler_params=pltpu.CompilerParams(vmem_limit_bytes=VMEM),
         cost_estimate=pl.CostEstimate(flops=2 * 10**10, bytes_accessed=4 * 2**20, transcendentals=0),
     )(*args)
+
+
+def sum_kernel(in_ref, out_ref):
+    total = in_ref[0].astype(jnp.float32)
+    for n in range(1, in_ref.shape[0]):
+        total = total + in_ref[n].astype(jnp.float32)
+    for h in range(HEADS):
+        c, k = divmod(h, GROUP)
+        out_ref[:, h, :] = total[c, :, k * E : (k + 1) * E]
+
+
+def sum_blocks(block):
+    rows = DM // (Y * PLANE)
+    whole = pl.BlockSpec(memory_space=pltpu.VMEM)
+    return pl.pallas_call(
+        sum_kernel,
+        in_specs=[whole],
+        out_specs=whole,
+        out_shape=jax.ShapeDtypeStruct((rows, HEADS, E), jnp.float32),
+        compiler_params=pltpu.CompilerParams(vmem_limit_bytes=VMEM),
+    )(block.reshape(PLANE // 2, 2, rows, HALF))
 
 
 def shards(queries, keys, values, out_weight, grad_out):
@@ -216,9 +242,7 @@
     )
     shape = (1, 1, PATCH, HEADS, E)
     outs = [back[:, n].reshape(shape) for n in range(3)]
-    rows = DM // (Y * PLANE)
-    total = jnp.sum(block.reshape(PLANE // 2, 2, rows, HALF).astype(jnp.float32), axis=0)
-    grad_weight = total.transpose(1, 0, 2).reshape(rows, HEADS, E)
+    grad_weight = sum_blocks(block)
     return (*outs, grad_weight)
 
 

time: 145 us -> 143 us (0.986)
    pallas_call x1 -> x2, Pallas kernels: 5.59 us -> 5.35 us  [the longest x1 4.49 us: attend(): pl.pallas_call(attend_kernel, in_specs=[whole, whole], out_specs=[whole,...]
  transfers between devices with their start and end apart: 10 -> 10, of which waited for: 6 -> 6; matrix products, arithmetic and copies ran while one was open for 3% -> 3% of each run, Pallas kernels for 7% -> 6%
where the time goes in v5:
time: 143 us
  blocking collectives  60 us (42%)
  waiting for transfers between devices  41.6 us (29%)
  starting transfers between devices  20.4 us (14%)
  Pallas kernels  9.55 us (7%)
  local copies, waits for them, and re-layouts  5.74 us (4%)
  other arithmetic  2.58 us (2%)
  matrix products  2.37 us (2%)
    all_to_all x1, blocking collectives, shards(): lax.all_to_all(packed, 'tm', split_axis=0, concat_axis=0, tiled=True)  60 us
    all_to_all x1, waiting for transfers between devices, shards(): lax.all_to_all(block, AXES, split_axis=0, concat_axis=0, tiled=True, axis...  13.1 us
    ppermute x1, waiting for transfers between devices, shards(): up0 = lax.ppermute(up0, AXES, y_shift(1))  10.5 us
    ppermute x1, waiting for transfers between devices, shards(): left = lax.ppermute(left, AXES, y_shift(1))  9.59 us
    ppermute x1, waiting for transfers between devices, shards(): down0 = lax.ppermute(down0, AXES, y_shift(-1))  7.34 us
    all_to_all x1, starting transfers between devices, shards(): lax.all_to_all(block, AXES, split_axis=0, concat_axis=0, tiled=True, axis...  7.25 us
    all_to_all x1, starting transfers between devices, shards(): back = lax.all_to_all(grads, 'tm', split_axis=0, concat_axis=0, tiled=True)  4.71 us
    pallas_call x1, Pallas kernels, attend(): pl.pallas_call(attend_kernel, in_specs=[whole, whole], out_specs=[whole,...  4.49 us
  transfers between devices with their start and end apart: 10, of which 6 were waited for; matrix products, arithmetic and copies ran while one was open for 3% of the time, Pallas kernels for 6%

profile of v5, /device:TPU:1, one launch (start us, length us, event | category | flops | bytes accessed | tf_op | source)
XLA Modules:
  0.0 143.0 jit_solution(5993081996701964917)
XLA Ops:
  0.6 0.0 slice-start
  0.6 2.6 %pad_maximum_fusion = bf16[16,128,8,128]{3,2,1,0:T(8,128)(2,1)S(1)} fusion(bf16[16,32,8,128]{3,2,1,0:T(8,128)(2,1)} %bitcast.51, bf16[16,32,8,128]{3,2,1,0:T(8,128)(2,1)} %bitcast.52, bf16[16,32,8,128]{3,2,1,0:T(8,128)(2,1)} %bitcast.53, bf16[16,32,8,128]{3,2,1,0:T(8,128)(2,1)} %bitcast.54), kind=kLoop, calls=%fused_computation.2 | loop fusion | flops 6291456 | bytes 8388608 | tf_op jit(solution)/shard_map/concatenate | solution.py:203
  3.2 0.0 slice-start.1
  3.2 60.0 %all_to_all.19 = bf16[16,128,8,128]{3,2,1,0:T(8,128)(2,1)S(1)} all-to-all(bf16[16,128,8,128]{3,2,1,0:T(8,128)(2,1)S(1)} %pad_maximum_fusion), channel_id=1, replica_groups=mesh['dp'=8,'tm'=16] {'tm'}, dimensions={0} | all-to-all | bytes 8388608 | tf_op jit(solution)/shard_map/all_to_all | solution.py:204
  63.2 0.1 slice.16
  63.3 0.0 slice-done
  63.3 0.0 slice-done.1
  63.3 2.4 %fusion.2 = bf16[256,16,128]{2,0,1:T(8,128)(2,1)S(1)} fusion(bf16[256,2048,1]{1,0,2:T(8,128)(2,1)S(1)} %bitcast.35, bf16[2048,16,128]{2,1,0:T(8,128)(2,1)S(1)} %bitcast.56), kind=kOutput, calls=%fused_computation.3 | convolution fusion | flops 2148007936 | bytes 10485760 | tf_op jit(solution)/shard_map/td,dhe->the/dot_general | solution.py:211
  65.7 0.7 copy.10
  66.4 1.2 collective-permute-start
  67.6 4.5 %shard_map.84 = (bf16[16,16,8,128]{3,2,1,0:T(8,128)(2,1)S(1)}, bf16[16,16,8,128]{3,2,1,0:T(8,128)(2,1)S(1)}, bf16[16,3,16,2,8,128]{5,4,3,2,1,0:T(8,128)(2,1)}) custom-call(bf16[16,4,16,2,8,128]{5,4,3,2,1,0:T(8,128)(2,1)S(1)} %bitcast.33, bf16[16,16,2,8,128]{4,3,2,1,0:T(8,128)(2,1)S(1)} %bitcast.41), custom_call_target="tpu_custom_call" | custom-call | flops 7000000000 | bytes 8388608 | tf_op jit(solution)/shard_map/pallas_call | solution.py:104
  72.1 0.9 copy.19
  73.0 0.0 collective-permute-start.1
  73.0 0.1 copy.20
  73.1 4.7 %all-to-all-start.1 = ((bf16[16,3,16,2,8,128]{5,4,3,2,1,0:T(8,128)(2,1)}), bf16[16,3,16,2,8,128]{5,4,3,2,1,0:T(8,128)(2,1)}, u32[]{:S(2)}, u32[]{:S(2)}) async-start(bf16[16,3,16,2,8,128]{5,4,3,2,1,0:T(8,128)(2,1)} %get-tuple-element.27), calls=%async_computation.1 | async-start | bytes 6291456 | tf_op jit(solution)/shard_map/all_to_all | solution.py:219
  77.9 0.0 collective-permute-done.1.refs_3_
  77.9 0.0 collective-permute-done.refs_1_
  77.9 0.8 shard_map.87
  78.6 1.4 collective-permute-start.4
  80.0 1.5 %collective-permute-start.5 = (bf16[512,512]{1,0:T(8,128)(2,1)S(1)}, bf16[512,512]{1,0:T(8,128)(2,1)S(1)}, u32[]{:S(2)}, u32[]{:S(2)}) collective-permute-start(bf16[512,512]{1,0:T(8,128)(2,1)S(1)} %get-tuple-element.24), channel_id=1, source_target_pairs={{0,96},{1,97},{2,98},{3,99},{4,100},{5,101},{6,102},{7,103},{8,104... | collective-permute-start | bytes 1572872 | tf_op jit(solution)/shard_map/ppermute | solution.py:229
  81.5 0.8 shard_map.85
  82.3 1.5 %collective-permute-start.2 = (bf16[512,512]{1,0:T(8,128)(2,1)S(1)}, bf16[512,512]{1,0:T(8,128)(2,1)S(1)}, u32[]{:S(2)}, u32[]{:S(2)}) collective-permute-start(bf16[512,512]{1,0:T(8,128)(2,1)S(1)} %get-tuple-element.19), channel_id=1, source_target_pairs={{0,96},{1,97},{2,98},{3,99},{4,100},{5,101},{6,102},{7,103},{8,104... | collective-permute-start | bytes 1572872 | tf_op jit(solution)/shard_map/ppermute | solution.py:232
  83.8 0.1 collective-permute-start.3
  83.8 9.6 %collective-permute-done.4.refs_4_ = bf16[512,512]{1,0:T(8,128)(2,1)S(1)} collective-permute-done((bf16[512,512]{1,0:T(8,128)(2,1)S(1)}, bf16[512,512]{1,0:T(8,128)(2,1)S(1)}, u32[]{:S(2)}, u32[]{:S(2)}) %collective-permute-start.4) | collective-permute-done | bytes 524320 | tf_op jit(solution)/shard_map/ppermute | solution.py:228
  93.4 0.0 collective-permute-done.5.refs_5_
  93.4 0.8 shard_map.88
  94.2 1.0 collective-permute-start.6
  95.2 1.8 %collective-permute-start.7 = (bf16[512,512]{1,0:T(8,128)(2,1)S(1)}, bf16[512,512]{1,0:T(8,128)(2,1)S(1)}, u32[]{:S(2)}, u32[]{:S(2)}) collective-permute-start(bf16[512,512]{1,0:T(8,128)(2,1)S(1)} %get-tuple-element.26), channel_id=1, source_target_pairs={{0,96},{1,97},{2,98},{3,99},{4,100},{5,101},{6,102},{7,103},{8,104... | collective-permute-start | bytes 1572872 | tf_op jit(solution)/shard_map/ppermute | solution.py:235
  96.9 7.3 %collective-permute-done.2.refs_4_ = bf16[512,512]{1,0:T(8,128)(2,1)S(1)} collective-permute-done((bf16[512,512]{1,0:T(8,128)(2,1)S(1)}, bf16[512,512]{1,0:T(8,128)(2,1)S(1)}, u32[]{:S(2)}, u32[]{:S(2)}) %collective-permute-start.2) | collective-permute-done | bytes 524320 | tf_op jit(solution)/shard_map/ppermute | solution.py:232
  104.3 0.4 collective-permute-done.3.refs_5_
  104.7 0.8 shard_map.86
  105.4 10.5 %collective-permute-done.6.came0 = bf16[512,512]{1,0:T(8,128)(2,1)S(1)} collective-permute-done((bf16[512,512]{1,0:T(8,128)(2,1)S(1)}, bf16[512,512]{1,0:T(8,128)(2,1)S(1)}, u32[]{:S(2)}, u32[]{:S(2)}) %collective-permute-start.6) | collective-permute-done | bytes 524320 | tf_op jit(solution)/shard_map/ppermute | solution.py:234
  115.9 0.0 collective-permute-done.7.came1
  115.9 1.2 shard_map.89
  117.0 0.8 all-to-all-done.1
  117.8 7.2 %all-to-all-start.2 = ((bf16[32,16,1024]{2,1,0:T(8,128)(2,1)}), bf16[32,16,1024]{2,1,0:T(8,128)(2,1)S(1)}, u32[]{:S(2)}, u32[]{:S(2)}) async-start(bf16[32,16,1024]{2,1,0:T(8,128)(2,1)} %bitcast.17), calls=%async_computation.2 | async-start | bytes 2097152 | tf_op jit(solution)/shard_map/all_to_all | solution.py:240
  125.1 4.0 %fusion.5 = (bf16[16,1,16,2,8,128]{5,4,3,2,1,0:T(8,128)(2,1)}, bf16[16,1,16,2,8,128]{5,4,3,2,1,0:T(8,128)(2,1)}, bf16[16,1,16,2,8,128]{5,4,3,2,1,0:T(8,128)(2,1)}) fusion(bf16[16,3,16,2,8,128]{5,4,3,2,1,0:T(8,128)(2,1)} %all-to-all-done.1), kind=kLoop, calls=%fused_computation.6 | loop fusion | bytes 6291456 | tf_op jit(solution)/shard_map/slice | solution.py:244
  129.0 13.1 %all-to-all-done.2 = bf16[32,16,1024]{2,1,0:T(8,128)(2,1)S(1)} async-done(((bf16[32,16,1024]{2,1,0:T(8,128)(2,1)}), bf16[32,16,1024]{2,1,0:T(8,128)(2,1)S(1)}, u32[]{:S(2)}, u32[]{:S(2)}) %all-to-all-start.2) | async-done | bytes 1048608 | tf_op jit(solution)/shard_map/all_to_all | solution.py:240
  142.1 0.9 shard_map.90
  (1 shorter events, 0.0 us)
Async XLA Ops:
  0.6 62.7 %slice-start = ((s8[8388608]{0:T(1024)(128)(4,1)}), s8[4194304]{0:T(1024)(128)(4,1)S(1)}, s32[]{:S(2)}) async-start(s8[8388608]{0:T(1024)(128)(4,1)} %bitcast.55), calls=%async_computation.3 | async-start | bytes 8388608
  3.2 60.1 %slice-start.1 = ((s8[8388608]{0:T(1024)(128)(4,1)}), s8[4194304]{0:T(1024)(128)(4,1)S(1)}, s32[]{:S(2)}) async-start(s8[8388608]{0:T(1024)(128)(4,1)} %bitcast.55), calls=%async_computation.4 | async-start | bytes 8388608
  66.4 11.5 %collective-permute-start = (bf16[256,2048]{1,0:T(8,128)(2,1)S(1)}, bf16[256,2048]{1,0:T(8,128)(2,1)S(1)}, u32[]{:S(2)}, u32[]{:S(2)}) collective-permute-start(bf16[256,2048]{1,0:T(8,128)(2,1)S(1)} %bitcast.36), channel_id=1, source_target_pairs={{0,1},{1,0},{2,3},{3,2},{4,5},{5,4},{6,7},{7,6},{8,9},{9,8},{10,11... | collective-permute-start | bytes 3145736 | tf_op jit(solution)/shard_map/ppermute | solution.py:222
  73.0 4.8 %collective-permute-start.1 = (bf16[256,1024]{1,0:T(8,128)(2,1)}, bf16[256,1024]{1,0:T(8,128)(2,1)S(1)}, u32[]{:S(2)}, u32[]{:S(2)}) collective-permute-start(bf16[256,1024]{1,0:T(8,128)(2,1)} %bitcast.31), channel_id=1, source_target_pairs={{0,1},{1,0},{2,3},{3,2},{4,5},{5,4},{6,7},{7,6},{8,9},{9,8},{10,11... | collective-permute-start | bytes 1572872 | tf_op jit(solution)/shard_map/ppermute | solution.py:223
  73.1 44.7 %all-to-all-start.1 = ((bf16[16,3,16,2,8,128]{5,4,3,2,1,0:T(8,128)(2,1)}), bf16[16,3,16,2,8,128]{5,4,3,2,1,0:T(8,128)(2,1)}, u32[]{:S(2)}, u32[]{:S(2)}) async-start(bf16[16,3,16,2,8,128]{5,4,3,2,1,0:T(8,128)(2,1)} %get-tuple-element.27), calls=%async_computation.1 | async-start | bytes 6291456 | tf_op jit(solution)/shard_map/all_to_all | solution.py:219
  78.6 14.8 %collective-permute-start.4 = (bf16[512,512]{1,0:T(8,128)(2,1)S(1)}, bf16[512,512]{1,0:T(8,128)(2,1)S(1)}, u32[]{:S(2)}, u32[]{:S(2)}) collective-permute-start(bf16[512,512]{1,0:T(8,128)(2,1)S(1)} %get-tuple-element.23), channel_id=1, source_target_pairs={{0,32},{1,33},{2,34},{3,35},{4,36},{5,37},{6,38},{7,39},{8,40},{9,... | collective-permute-start | bytes 1572872 | tf_op jit(solution)/shard_map/ppermute | solution.py:228
  80.0 13.4 %collective-permute-start.5 = (bf16[512,512]{1,0:T(8,128)(2,1)S(1)}, bf16[512,512]{1,0:T(8,128)(2,1)S(1)}, u32[]{:S(2)}, u32[]{:S(2)}) collective-permute-start(bf16[512,512]{1,0:T(8,128)(2,1)S(1)} %get-tuple-element.24), channel_id=1, source_target_pairs={{0,96},{1,97},{2,98},{3,99},{4,100},{5,101},{6,102},{7,103},{8,104... | collective-permute-start | bytes 1572872 | tf_op jit(solution)/shard_map/ppermute | solution.py:229
  82.3 22.0 %collective-permute-start.2 = (bf16[512,512]{1,0:T(8,128)(2,1)S(1)}, bf16[512,512]{1,0:T(8,128)(2,1)S(1)}, u32[]{:S(2)}, u32[]{:S(2)}) collective-permute-start(bf16[512,512]{1,0:T(8,128)(2,1)S(1)} %get-tuple-element.19), channel_id=1, source_target_pairs={{0,96},{1,97},{2,98},{3,99},{4,100},{5,101},{6,102},{7,103},{8,104... | collective-permute-start | bytes 1572872 | tf_op jit(solution)/shard_map/ppermute | solution.py:232
  83.8 20.9 %collective-permute-start.3 = (bf16[512,512]{1,0:T(8,128)(2,1)S(1)}, bf16[512,512]{1,0:T(8,128)(2,1)S(1)}, u32[]{:S(2)}, u32[]{:S(2)}) collective-permute-start(bf16[512,512]{1,0:T(8,128)(2,1)S(1)} %get-tuple-element.20), channel_id=1, source_target_pairs={{0,32},{1,33},{2,34},{3,35},{4,36},{5,37},{6,38},{7,39},{8,40},{9,... | collective-permute-start | bytes 1572872 | tf_op jit(solution)/shard_map/ppermute | solution.py:231
  94.2 21.7 %collective-permute-start.6 = (bf16[512,512]{1,0:T(8,128)(2,1)S(1)}, bf16[512,512]{1,0:T(8,128)(2,1)S(1)}, u32[]{:S(2)}, u32[]{:S(2)}) collective-permute-start(bf16[512,512]{1,0:T(8,128)(2,1)S(1)} %get-tuple-element.25), channel_id=1, source_target_pairs={{0,32},{1,33},{2,34},{3,35},{4,36},{5,37},{6,38},{7,39},{8,40},{9,... | collective-permute-start | bytes 1572872 | tf_op jit(solution)/shard_map/ppermute | solution.py:234
  95.2 20.7 %collective-permute-start.7 = (bf16[512,512]{1,0:T(8,128)(2,1)S(1)}, bf16[512,512]{1,0:T(8,128)(2,1)S(1)}, u32[]{:S(2)}, u32[]{:S(2)}) collective-permute-start(bf16[512,512]{1,0:T(8,128)(2,1)S(1)} %get-tuple-element.26), channel_id=1, source_target_pairs={{0,96},{1,97},{2,98},{3,99},{4,100},{5,101},{6,102},{7,103},{8,104... | collective-permute-start | bytes 1572872 | tf_op jit(solution)/shard_map/ppermute | solution.py:235
  117.8 24.3 %all-to-all-start.2 = ((bf16[32,16,1024]{2,1,0:T(8,128)(2,1)}), bf16[32,16,1024]{2,1,0:T(8,128)(2,1)S(1)}, u32[]{:S(2)}, u32[]{:S(2)}) async-start(bf16[32,16,1024]{2,1,0:T(8,128)(2,1)} %bitcast.17), calls=%async_computation.2 | async-start | bytes 2097152 | tf_op jit(solution)/shard_map/all_to_all | solution.py:240

commit v6 on v5

--- a/solution.py
+++ b/solution.py
@@ -63,18 +63,22 @@
     return attended, zip(gq, gk, gv)
 
 
-def attend_kernel(packed_ref, g_ref, own_ref, other_ref, grads_ref, bias_ref, out_ref, sems):
+def attend_kernel(packed_ref, mat_ref, own_ref, other_ref, grads_ref, bias_ref, out_ref, half_ref, g_ref, sems):
     row = lax.broadcasted_iota(jnp.int32, (ROWS, ROWS), 0)
     col = lax.broadcasted_iota(jnp.int32, (ROWS, ROWS), 1)
     keep = (row % GROUP == col % GROUP) & (row <= col)
     bias_ref[...] = jnp.where(keep, 0.0, -jnp.inf)
+    mat = jnp.concatenate([mat_ref[h] for h in range(HEADS)], axis=1)
+    g_ref[...] = mat.reshape(g_ref.shape)
     first = lax.rem(lax.axis_index("tm"), 2) == 0
     ids = [(t, h) for t in range(STEP_TOK) for h in range(GROUPS)]
 
-    def out_copy(step):
-        slot = step % 2
-        there = grads_ref.at[:, :, pl.ds(step * STEP_TOK, STEP_TOK)]
-        return pltpu.make_async_copy(out_ref.at[slot], there, sems.at[slot])
+    def out_copies(step):
+        slot, tokens = step % 2, pl.ds(step * STEP_TOK, STEP_TOK)
+        return (
+            pltpu.make_async_copy(half_ref.at[slot], other_ref.at[:, tokens], sems.at[0, slot]),
+            pltpu.make_async_copy(out_ref.at[slot], grads_ref.at[:, :, tokens], sems.at[1, slot]),
+        )
 
     for step in range(STEPS):
         start = step * STEP_TOK
@@ -84,18 +88,21 @@
             units.append([part.reshape(ROWS, E) for part in parts])
         attended, grads = attend_groups(units, bias_ref[...])
         if step >= 2:
-            out_copy(step - 2).wait()
+            for copy in out_copies(step - 2):
+                copy.wait()
         for (t, h), three in zip(ids, grads):
             for n, grad in enumerate(three):
                 out_ref[step % 2, :, n, t, h] = grad.reshape(FRAMES, GROUP, E)
-        out_copy(step).start()
         for t in range(STEP_TOK):
             pair = attended[GROUPS * t : GROUPS * (t + 1)]
             low, high = (a.reshape(FRAMES, GROUP, E) for a in pair)
             own_ref[:, start + t] = jnp.where(first, low, high)
-            other_ref[:, start + t] = jnp.where(first, high, low)
+            half_ref[step % 2, :, t] = jnp.where(first, high, low)
+        for copy in out_copies(step):
+            copy.start()
     for step in range(max(STEPS - 2, 0), STEPS):
-        out_copy(step).wait()
+        for copy in out_copies(step):
+            copy.wait()
 
 
 def attend(packed, grad_attended):
@@ -104,12 +111,18 @@
     return pl.pallas_call(
         attend_kernel,
         in_specs=[whole, whole],
-        out_specs=[whole, whole, pl.BlockSpec(memory_space=pltpu.HBM)],
-        out_shape=[half, half, pltpu.HBM((FRAMES, 3, TOK, GROUPS, GROUP, E), jnp.bfloat16)],
+        out_specs=[whole] + [pl.BlockSpec(memory_space=pltpu.HBM)] * 2,
+        out_shape=[
+            half,
+            pltpu.HBM(half.shape, half.dtype),
+            pltpu.HBM((FRAMES, 3, TOK, GROUPS, GROUP, E), jnp.bfloat16),
+        ],
         scratch_shapes=[
             pltpu.VMEM((ROWS, ROWS), jnp.float32),
             pltpu.VMEM((2, FRAMES, 3, STEP_TOK, GROUPS, GROUP, E), jnp.bfloat16),
-            pltpu.SemaphoreType.DMA((2,)),
+            pltpu.VMEM((2, FRAMES, STEP_TOK, GROUP, E), jnp.bfloat16),
+            pltpu.VMEM((FRAMES, TOK, GROUPS, GROUP, E), jnp.bfloat16),
+            pltpu.SemaphoreType.DMA((2, 2)),
         ],
         compiler_params=pltpu.CompilerParams(vmem_limit_bytes=VMEM),
         cost_estimate=pl.CostEstimate(flops=7 * 10**9, bytes_accessed=8 * 2**20, transcendentals=0),
@@ -135,8 +148,11 @@
 
 
 def far_kernel(*refs):
-    for part, out in enumerate(refs[4:]):
-        out[...] = partial_sum(2, part, *refs[:4]).astype(jnp.bfloat16)
+    g_ref, gs_ref, raw, raw_swapped, *outs, a_ref, as_ref = refs
+    a_ref[...] = raw[...].reshape(TOKENS, HALF)
+    as_ref[...] = raw_swapped[...].reshape(TOKENS, HALF)
+    for part, out in enumerate(outs):
+        out[...] = partial_sum(2, part, g_ref, gs_ref, a_ref, as_ref).astype(jnp.bfloat16)
 
 
 def direct_kernel(*refs):
@@ -161,13 +177,14 @@
     out[:, QUARTER:] = (own1[...] + came1[...]).astype(jnp.bfloat16)
 
 
-def weight_step(kernel, args, widths, dtype=jnp.bfloat16):
+def weight_step(kernel, args, widths, dtype=jnp.bfloat16, more=()):
     whole = pl.BlockSpec(memory_space=pltpu.VMEM)
     return pl.pallas_call(
         kernel,
         in_specs=[whole] * len(args),
-        out_specs=[whole] * len(widths),
-        out_shape=[jax.ShapeDtypeStruct((YROWS, w), dtype) for w in widths],
+        out_specs=[whole] * (len(widths) + len(more)),
+        out_shape=[jax.ShapeDtypeStruct((YROWS, w), dtype) for w in widths]
+        + [jax.ShapeDtypeStruct(shape, jnp.bfloat16) for shape in more],
         compiler_params=pltpu.CompilerParams(vmem_limit_bytes=VMEM),
         cost_estimate=pl.CostEstimate(flops=2 * 10**10, bytes_accessed=4 * 2**20, transcendentals=0),
     )(*args)
@@ -209,22 +226,23 @@
         .reshape(TOKENS, DM)
     )
     grad_attended = jnp.einsum(
-        "td,dhe->the", g_tok, out_weight, preferred_element_type=jnp.float32
+        "td,dhe->hte", g_tok, out_weight, preferred_element_type=jnp.float32
     ).astype(jnp.bfloat16)
     own, other, grads = attend(
         packed.reshape(FRAMES, 4, TOK, GROUPS, GROUP, E),
-        grad_attended.reshape(FRAMES, TOK, GROUPS, GROUP, E),
+        grad_attended,
     )
 
     back = lax.all_to_all(grads, "tm", split_axis=0, concat_axis=0, tiled=True)
 
-    own = own.reshape(TOKENS, HALF)
+    own = own.reshape(TOKENS, GROUP, E)
     g_swapped = lax.ppermute(g_tok, AXES, core_swap())
-    swapped = lax.ppermute(other.reshape(TOKENS, HALF), AXES, core_swap())
+    swapped = lax.ppermute(other, AXES, core_swap()).reshape(TOKENS, GROUP, E)
 
     ins = [g_tok, g_swapped, own, swapped]
     pair = [QUARTER] * 2
-    left, right = weight_step(far_kernel, ins, pair)
+    left, right, *mats = weight_step(far_kernel, ins, pair, more=[(TOKENS, HALF)] * 2)
+    ins = [g_tok, g_swapped, *mats]
     left = lax.ppermute(left, AXES, y_shift(1))
     right = lax.ppermute(right, AXES, y_shift(-1))
     up1, down0 = weight_step(direct_kernel, ins, pair)

time: 143 us -> 142 us (level)
  local copies, waits for them, and re-layouts: 5.74 us -> 4.09 us
  transfers between devices with their start and end apart: 10 -> 10, of which waited for: 6 -> 6; matrix products, arithmetic and copies ran while one was open for 3% -> 4% of each run, Pallas kernels for 6% -> 6%
where the time goes in v6:
time: 142 us
  blocking collectives  60 us (42%)
  waiting for transfers between devices  41.6 us (29%)
  starting transfers between devices  20.5 us (14%)
  Pallas kernels  9.75 us (7%)
  local copies, waits for them, and re-layouts  4.09 us (3%)
  other arithmetic  2.58 us (2%)
  matrix products  2.37 us (2%)
    all_to_all x1, blocking collectives, shards(): lax.all_to_all(packed, 'tm', split_axis=0, concat_axis=0, tiled=True)  60 us
    all_to_all x1, waiting for transfers between devices, shards(): lax.all_to_all(block, AXES, split_axis=0, concat_axis=0, tiled=True, axis...  13.1 us
    ppermute x1, waiting for transfers between devices, shards(): up0 = lax.ppermute(up0, AXES, y_shift(1))  10.5 us
    ppermute x1, waiting for transfers between devices, shards(): left = lax.ppermute(left, AXES, y_shift(1))  9.58 us
    ppermute x1, waiting for transfers between devices, shards(): down0 = lax.ppermute(down0, AXES, y_shift(-1))  7.34 us
    all_to_all x1, starting transfers between devices, shards(): lax.all_to_all(block, AXES, split_axis=0, concat_axis=0, tiled=True, axis...  7.25 us
    pallas_call x1, Pallas kernels, attend(): pl.pallas_call(attend_kernel, in_specs=[whole, whole], out_specs=[whole]...  4.69 us
    all_to_all x1, starting transfers between devices, shards(): back = lax.all_to_all(grads, 'tm', split_axis=0, concat_axis=0, tiled=True)  4.68 us
  transfers between devices with their start and end apart: 10, of which 6 were waited for; matrix products, arithmetic and copies ran while one was open for 4% of the time, Pallas kernels for 6%

profile of v6, /device:TPU:1, one launch (start us, length us, event | category | flops | bytes accessed | tf_op | source)
XLA Modules:
  0.0 141.6 jit_solution(16080817428610709630)
XLA Ops:
  0.6 0.0 slice-start
  0.6 2.6 %pad_maximum_fusion = bf16[16,128,8,128]{3,2,1,0:T(8,128)(2,1)S(1)} fusion(bf16[16,32,8,128]{3,2,1,0:T(8,128)(2,1)} %bitcast.39, bf16[16,32,8,128]{3,2,1,0:T(8,128)(2,1)} %bitcast.40, bf16[16,32,8,128]{3,2,1,0:T(8,128)(2,1)} %bitcast.41, bf16[16,32,8,128]{3,2,1,0:T(8,128)(2,1)} %bitcast.42), kind=kLoop, calls=%fused_computation.2 | loop fusion | flops 6291456 | bytes 8388608 | tf_op jit(solution)/shard_map/concatenate | solution.py:220
  3.2 0.0 slice-start.1
  3.3 60.0 %all_to_all.19 = bf16[16,128,8,128]{3,2,1,0:T(8,128)(2,1)S(1)} all-to-all(bf16[16,128,8,128]{3,2,1,0:T(8,128)(2,1)S(1)} %pad_maximum_fusion), channel_id=1, replica_groups=mesh['dp'=8,'tm'=16] {'tm'}, dimensions={0} | all-to-all | bytes 8388608 | tf_op jit(solution)/shard_map/all_to_all | solution.py:221
  63.2 0.1 slice.16
  63.3 1.2 collective-permute-start
  64.6 0.0 slice-done
  64.6 0.0 slice-done.1
  64.6 2.4 %fusion.5.mat_ref = bf16[16,256,128]{2,1,0:T(8,128)(2,1)S(1)} fusion(bf16[256,2048,1]{1,0,2:T(8,128)(2,1)S(1)} %bitcast.29, bf16[2048,16,128]{2,1,0:T(8,128)(2,1)S(1)} %bitcast.44), kind=kOutput, calls=%fused_computation.4 | convolution fusion | flops 2148007936 | bytes 10485760 | tf_op jit(solution)/shard_map/td,dhe->hte/dot_general | solution.py:228
  66.9 4.7 %shard_map.84 = (bf16[16,16,8,128]{3,2,1,0:T(8,128)(2,1)S(1)}, bf16[16,16,8,128]{3,2,1,0:T(8,128)(2,1)}, bf16[16,3,16,2,8,128]{5,4,3,2,1,0:T(8,128)(2,1)}) custom-call(bf16[16,4,16,2,8,128]{5,4,3,2,1,0:T(8,128)(2,1)S(1)} %bitcast.26, bf16[16,256,128]{2,1,0:T(8,128)(2,1)S(1)} %fusion.5.mat_ref), custom_call_target="tpu_custom_call" | custom-call | flops 7000000000 | bytes 8388608 | tf_op jit(solution)/shard_map/pallas_call | solution.py:111
  71.6 0.1 collective-permute-start.1
  71.8 4.7 %all-to-all-start.1 = ((bf16[16,3,16,2,8,128]{5,4,3,2,1,0:T(8,128)(2,1)}), bf16[16,3,16,2,8,128]{5,4,3,2,1,0:T(8,128)(2,1)}, u32[]{:S(2)}, u32[]{:S(2)}) async-start(bf16[16,3,16,2,8,128]{5,4,3,2,1,0:T(8,128)(2,1)} %get-tuple-element.31), calls=%async_computation.1 | async-start | bytes 6291456 | tf_op jit(solution)/shard_map/all_to_all | solution.py:236
  76.4 0.0 collective-permute-done.1
  76.4 0.0 collective-permute-done.refs_1_
  76.5 0.8 shard_map.85
  77.2 1.4 collective-permute-start.4
  78.6 1.5 %collective-permute-start.5 = (bf16[512,512]{1,0:T(8,128)(2,1)S(1)}, bf16[512,512]{1,0:T(8,128)(2,1)S(1)}, u32[]{:S(2)}, u32[]{:S(2)}) collective-permute-start(bf16[512,512]{1,0:T(8,128)(2,1)S(1)} %get-tuple-element.28), channel_id=1, source_target_pairs={{0,96},{1,97},{2,98},{3,99},{4,100},{5,101},{6,102},{7,103},{8,104... | collective-permute-start | bytes 1572872 | tf_op jit(solution)/shard_map/ppermute | solution.py:247
  80.1 0.8 shard_map.86
  80.9 1.5 %collective-permute-start.2 = (bf16[512,512]{1,0:T(8,128)(2,1)S(1)}, bf16[512,512]{1,0:T(8,128)(2,1)S(1)}, u32[]{:S(2)}, u32[]{:S(2)}) collective-permute-start(bf16[512,512]{1,0:T(8,128)(2,1)S(1)} %get-tuple-element.23), channel_id=1, source_target_pairs={{0,96},{1,97},{2,98},{3,99},{4,100},{5,101},{6,102},{7,103},{8,104... | collective-permute-start | bytes 1572872 | tf_op jit(solution)/shard_map/ppermute | solution.py:250
  82.3 0.1 collective-permute-start.3
  82.4 9.6 %collective-permute-done.4.refs_4_ = bf16[512,512]{1,0:T(8,128)(2,1)S(1)} collective-permute-done((bf16[512,512]{1,0:T(8,128)(2,1)S(1)}, bf16[512,512]{1,0:T(8,128)(2,1)S(1)}, u32[]{:S(2)}, u32[]{:S(2)}) %collective-permute-start.4) | collective-permute-done | bytes 524320 | tf_op jit(solution)/shard_map/ppermute | solution.py:246
  92.0 0.0 collective-permute-done.5.refs_5_
  92.0 0.8 shard_map.88
  92.8 1.0 collective-permute-start.6
  93.8 1.8 %collective-permute-start.7 = (bf16[512,512]{1,0:T(8,128)(2,1)S(1)}, bf16[512,512]{1,0:T(8,128)(2,1)S(1)}, u32[]{:S(2)}, u32[]{:S(2)}) collective-permute-start(bf16[512,512]{1,0:T(8,128)(2,1)S(1)} %get-tuple-element.30), channel_id=1, source_target_pairs={{0,96},{1,97},{2,98},{3,99},{4,100},{5,101},{6,102},{7,103},{8,104... | collective-permute-start | bytes 1572872 | tf_op jit(solution)/shard_map/ppermute | solution.py:253
  95.5 7.3 %collective-permute-done.2.refs_4_ = bf16[512,512]{1,0:T(8,128)(2,1)S(1)} collective-permute-done((bf16[512,512]{1,0:T(8,128)(2,1)S(1)}, bf16[512,512]{1,0:T(8,128)(2,1)S(1)}, u32[]{:S(2)}, u32[]{:S(2)}) %collective-permute-start.2) | collective-permute-done | bytes 524320 | tf_op jit(solution)/shard_map/ppermute | solution.py:250
  102.9 0.4 collective-permute-done.3.refs_5_
  103.2 0.8 shard_map.87
  104.0 10.5 %collective-permute-done.6.came0 = bf16[512,512]{1,0:T(8,128)(2,1)S(1)} collective-permute-done((bf16[512,512]{1,0:T(8,128)(2,1)S(1)}, bf16[512,512]{1,0:T(8,128)(2,1)S(1)}, u32[]{:S(2)}, u32[]{:S(2)}) %collective-permute-start.6) | collective-permute-done | bytes 524320 | tf_op jit(solution)/shard_map/ppermute | solution.py:252
  114.5 0.0 collective-permute-done.7.came1
  114.5 1.2 shard_map.89
  115.6 0.8 all-to-all-done.1
  116.4 7.3 %all-to-all-start.2 = ((bf16[32,16,1024]{2,1,0:T(8,128)(2,1)}), bf16[32,16,1024]{2,1,0:T(8,128)(2,1)S(1)}, u32[]{:S(2)}, u32[]{:S(2)}) async-start(bf16[32,16,1024]{2,1,0:T(8,128)(2,1)} %bitcast.19), calls=%async_computation.2 | async-start | bytes 2097152 | tf_op jit(solution)/shard_map/all_to_all | solution.py:258
  123.6 4.0 %fusion.8 = (bf16[16,1,16,2,8,128]{5,4,3,2,1,0:T(8,128)(2,1)}, bf16[16,1,16,2,8,128]{5,4,3,2,1,0:T(8,128)(2,1)}, bf16[16,1,16,2,8,128]{5,4,3,2,1,0:T(8,128)(2,1)}) fusion(bf16[16,3,16,2,8,128]{5,4,3,2,1,0:T(8,128)(2,1)} %all-to-all-done.1), kind=kLoop, calls=%fused_computation.5 | loop fusion | bytes 6291456 | tf_op jit(solution)/shard_map/slice | solution.py:262
  127.6 13.1 %all-to-all-done.2 = bf16[32,16,1024]{2,1,0:T(8,128)(2,1)S(1)} async-done(((bf16[32,16,1024]{2,1,0:T(8,128)(2,1)}), bf16[32,16,1024]{2,1,0:T(8,128)(2,1)S(1)}, u32[]{:S(2)}, u32[]{:S(2)}) %all-to-all-start.2) | async-done | bytes 1048608 | tf_op jit(solution)/shard_map/all_to_all | solution.py:258
  140.7 0.9 shard_map.90
  (1 shorter events, 0.0 us)
Async XLA Ops:
  0.6 63.9 %slice-start = ((s8[8388608]{0:T(1024)(128)(4,1)}), s8[4194304]{0:T(1024)(128)(4,1)S(1)}, s32[]{:S(2)}) async-start(s8[8388608]{0:T(1024)(128)(4,1)} %bitcast.43), calls=%async_computation.3 | async-start | bytes 8388608
  3.2 61.3 %slice-start.1 = ((s8[8388608]{0:T(1024)(128)(4,1)}), s8[4194304]{0:T(1024)(128)(4,1)S(1)}, s32[]{:S(2)}) async-start(s8[8388608]{0:T(1024)(128)(4,1)} %bitcast.43), calls=%async_computation.4 | async-start | bytes 8388608
  63.3 13.1 %collective-permute-start = (bf16[256,2048]{1,0:T(8,128)(2,1)S(1)}, bf16[256,2048]{1,0:T(8,128)(2,1)S(1)}, u32[]{:S(2)}, u32[]{:S(2)}) collective-permute-start(bf16[256,2048]{1,0:T(8,128)(2,1)S(1)} %bitcast.28), channel_id=1, source_target_pairs={{0,1},{1,0},{2,3},{3,2},{4,5},{5,4},{6,7},{7,6},{8,9},{9,8},{10,11... | collective-permute-start | bytes 3145736 | tf_op jit(solution)/shard_map/ppermute | solution.py:239
  71.6 4.8 %collective-permute-start.1 = (bf16[16,16,8,128]{3,2,1,0:T(8,128)(2,1)}, bf16[16,16,8,128]{3,2,1,0:T(8,128)(2,1)S(1)}, u32[]{:S(2)}, u32[]{:S(2)}) collective-permute-start(bf16[16,16,8,128]{3,2,1,0:T(8,128)(2,1)} %get-tuple-element.20), channel_id=1, source_target_pairs={{0,1},{1,0},{2,3},{3,2},{4,5},{5,4},{6,7},{7,6},{8,9},{9,8},{10,11... | collective-permute-start | bytes 1572872 | tf_op jit(solution)/shard_map/ppermute | solution.py:240
  71.8 44.6 %all-to-all-start.1 = ((bf16[16,3,16,2,8,128]{5,4,3,2,1,0:T(8,128)(2,1)}), bf16[16,3,16,2,8,128]{5,4,3,2,1,0:T(8,128)(2,1)}, u32[]{:S(2)}, u32[]{:S(2)}) async-start(bf16[16,3,16,2,8,128]{5,4,3,2,1,0:T(8,128)(2,1)} %get-tuple-element.31), calls=%async_computation.1 | async-start | bytes 6291456 | tf_op jit(solution)/shard_map/all_to_all | solution.py:236
  77.2 14.8 %collective-permute-start.4 = (bf16[512,512]{1,0:T(8,128)(2,1)S(1)}, bf16[512,512]{1,0:T(8,128)(2,1)S(1)}, u32[]{:S(2)}, u32[]{:S(2)}) collective-permute-start(bf16[512,512]{1,0:T(8,128)(2,1)S(1)} %get-tuple-element.27), channel_id=1, source_target_pairs={{0,32},{1,33},{2,34},{3,35},{4,36},{5,37},{6,38},{7,39},{8,40},{9,... | collective-permute-start | bytes 1572872 | tf_op jit(solution)/shard_map/ppermute | solution.py:246
  78.6 13.4 %collective-permute-start.5 = (bf16[512,512]{1,0:T(8,128)(2,1)S(1)}, bf16[512,512]{1,0:T(8,128)(2,1)S(1)}, u32[]{:S(2)}, u32[]{:S(2)}) collective-permute-start(bf16[512,512]{1,0:T(8,128)(2,1)S(1)} %get-tuple-element.28), channel_id=1, source_target_pairs={{0,96},{1,97},{2,98},{3,99},{4,100},{5,101},{6,102},{7,103},{8,104... | collective-permute-start | bytes 1572872 | tf_op jit(solution)/shard_map/ppermute | solution.py:247
  80.9 22.0 %collective-permute-start.2 = (bf16[512,512]{1,0:T(8,128)(2,1)S(1)}, bf16[512,512]{1,0:T(8,128)(2,1)S(1)}, u32[]{:S(2)}, u32[]{:S(2)}) collective-permute-start(bf16[512,512]{1,0:T(8,128)(2,1)S(1)} %get-tuple-element.23), channel_id=1, source_target_pairs={{0,96},{1,97},{2,98},{3,99},{4,100},{5,101},{6,102},{7,103},{8,104... | collective-permute-start | bytes 1572872 | tf_op jit(solution)/shard_map/ppermute | solution.py:250
  82.3 20.9 %collective-permute-start.3 = (bf16[512,512]{1,0:T(8,128)(2,1)S(1)}, bf16[512,512]{1,0:T(8,128)(2,1)S(1)}, u32[]{:S(2)}, u32[]{:S(2)}) collective-permute-start(bf16[512,512]{1,0:T(8,128)(2,1)S(1)} %get-tuple-element.24), channel_id=1, source_target_pairs={{0,32},{1,33},{2,34},{3,35},{4,36},{5,37},{6,38},{7,39},{8,40},{9,... | collective-permute-start | bytes 1572872 | tf_op jit(solution)/shard_map/ppermute | solution.py:249
  92.8 21.7 %collective-permute-start.6 = (bf16[512,512]{1,0:T(8,128)(2,1)S(1)}, bf16[512,512]{1,0:T(8,128)(2,1)S(1)}, u32[]{:S(2)}, u32[]{:S(2)}) collective-permute-start(bf16[512,512]{1,0:T(8,128)(2,1)S(1)} %get-tuple-element.29), channel_id=1, source_target_pairs={{0,32},{1,33},{2,34},{3,35},{4,36},{5,37},{6,38},{7,39},{8,40},{9,... | collective-permute-start | bytes 1572872 | tf_op jit(solution)/shard_map/ppermute | solution.py:252
  93.8 20.7 %collective-permute-start.7 = (bf16[512,512]{1,0:T(8,128)(2,1)S(1)}, bf16[512,512]{1,0:T(8,128)(2,1)S(1)}, u32[]{:S(2)}, u32[]{:S(2)}) collective-permute-start(bf16[512,512]{1,0:T(8,128)(2,1)S(1)} %get-tuple-element.30), channel_id=1, source_target_pairs={{0,96},{1,97},{2,98},{3,99},{4,100},{5,101},{6,102},{7,103},{8,104... | collective-permute-start | bytes 1572872 | tf_op jit(solution)/shard_map/ppermute | solution.py:253
  116.4 24.3 %all-to-all-start.2 = ((bf16[32,16,1024]{2,1,0:T(8,128)(2,1)}), bf16[32,16,1024]{2,1,0:T(8,128)(2,1)S(1)}, u32[]{:S(2)}, u32[]{:S(2)}) async-start(bf16[32,16,1024]{2,1,0:T(8,128)(2,1)} %bitcast.19), calls=%async_computation.2 | async-start | bytes 2097152 | tf_op jit(solution)/shard_map/all_to_all | solution.py:258

commit v7 on v6

--- a/solution.py
+++ b/solution.py
@@ -10,7 +10,7 @@
 TOKENS = FRAMES * TOK
 GROUPS, GROUP = 2, 8
 ROWS = FRAMES * GROUP
-STEP_TOK = 4
+STEP_TOK = 8
 STEPS = TOK // STEP_TOK
 AXES = ("dp", "tm")
 SCALE = 1.0 / (E**0.5)
@@ -18,7 +18,7 @@
 Y, PLANE = 4, 32
 YROWS = DM // Y
 HALF = DM // 2
-VMEM = 16 * 1024 * 1024
+VMEM = 24 * 1024 * 1024
 
 
 def y_shift(n):
@@ -172,9 +172,30 @@
         out[...] = partial_sum(0, part, *ins) + add[...]
 
 
-def last_kernel(own0, own1, came0, came1, out):
-    out[:, :QUARTER] = (own0[...] + came0[...]).astype(jnp.bfloat16)
-    out[:, QUARTER:] = (own1[...] + came1[...]).astype(jnp.bfloat16)
+def last_kernel(own0, own1, came0, came1, out, sum_ref, sems):
+    chunk = YROWS // 4
+    copies = []
+    for n in range(4):
+        rows = pl.ds(n * chunk, chunk)
+        sum_ref[rows, :QUARTER] = (own0[rows, :] + came0[rows, :]).astype(jnp.bfloat16)
+        sum_ref[rows, QUARTER:] = (own1[rows, :] + came1[rows, :]).astype(jnp.bfloat16)
+        copies.append(pltpu.make_async_copy(sum_ref.at[rows], out.at[rows], sems.at[n]))
+        copies[-1].start()
+    for copy in copies:
+        copy.wait()
+
+
+def last_step(args):
+    whole = pl.BlockSpec(memory_space=pltpu.VMEM)
+    return pl.pallas_call(
+        last_kernel,
+        in_specs=[whole] * 4,
+        out_specs=pl.BlockSpec(memory_space=pltpu.HBM),
+        out_shape=pltpu.HBM((YROWS, HALF), jnp.bfloat16),
+        scratch_shapes=[pltpu.VMEM((YROWS, HALF), jnp.bfloat16), pltpu.SemaphoreType.DMA((4,))],
+        compiler_params=pltpu.CompilerParams(vmem_limit_bytes=VMEM),
+        cost_estimate=pl.CostEstimate(flops=2 * 10**10, bytes_accessed=2**22, transcendentals=0),
+    )(*args)
 
 
 def weight_step(kernel, args, widths, dtype=jnp.bfloat16, more=()):
@@ -252,7 +273,7 @@
     up0 = lax.ppermute(up0, AXES, y_shift(1))
     down1 = lax.ppermute(down1, AXES, y_shift(-1))
     own0, own1 = weight_step(own_kernel, [*ins, down0, up1], pair, jnp.float32)
-    (block,) = weight_step(last_kernel, [own0, own1, up0, down1], [HALF])
+    block = last_step([own0, own1, up0, down1])
 
     block, back = lax.optimization_barrier((block, back))
     block = lax.all_to_all(

time: 142 us -> 142 us (level)
    pallas_call x5 -> x4, Pallas kernels: 4.2 us -> 3.05 us  [weight_step(): pl.pallas_call(kernel, in_specs=[whole] * len(args), out_specs=[whole] *...]
  transfers between devices with their start and end apart: 10 -> 10, of which waited for: 6 -> 6; matrix products, arithmetic and copies ran while one was open for 4% -> 5% of each run, Pallas kernels for 6% -> 6%
where the time goes in v7:
time: 142 us; the launch traced here: 141 us
  blocking collectives  60 us (42%)
  waiting for transfers between devices  41.7 us (29%)
  starting transfers between devices  20.4 us (14%)
  Pallas kernels  9.36 us (7%)
  local copies, waits for them, and re-layouts  4.09 us (3%)
  other arithmetic  2.58 us (2%)
  matrix products  2.37 us (2%)
    all_to_all x1, blocking collectives, shards(): lax.all_to_all(packed, 'tm', split_axis=0, concat_axis=0, tiled=True)  60 us
    all_to_all x1, waiting for transfers between devices, shards(): lax.all_to_all(block, AXES, split_axis=0, concat_axis=0, tiled=True, axis...  13.1 us
    ppermute x1, waiting for transfers between devices, shards(): up0 = lax.ppermute(up0, AXES, y_shift(1))  10.5 us
    ppermute x1, waiting for transfers between devices, shards(): left = lax.ppermute(left, AXES, y_shift(1))  9.58 us
    ppermute x1, waiting for transfers between devices, shards(): down0 = lax.ppermute(down0, AXES, y_shift(-1))  7.35 us
    all_to_all x1, starting transfers between devices, shards(): lax.all_to_all(block, AXES, split_axis=0, concat_axis=0, tiled=True, axis...  7.2 us
    all_to_all x1, starting transfers between devices, shards(): back = lax.all_to_all(grads, 'tm', split_axis=0, concat_axis=0, tiled=True)  4.66 us
    pallas_call x1, Pallas kernels, attend(): pl.pallas_call(attend_kernel, in_specs=[whole, whole], out_specs=[whole]...  4.39 us
  transfers between devices with their start and end apart: 10, of which 6 were waited for; matrix products, arithmetic and copies ran while one was open for 5% of the time, Pallas kernels for 6%

profile of v7, /device:TPU:1, one launch (start us, length us, event | category | flops | bytes accessed | tf_op | source)
XLA Modules:
  0.0 141.2 jit_solution(3235367518622345945)
XLA Ops:
  0.6 0.0 slice-start
  0.6 2.6 %pad_maximum_fusion = bf16[16,128,8,128]{3,2,1,0:T(8,128)(2,1)S(1)} fusion(bf16[16,32,8,128]{3,2,1,0:T(8,128)(2,1)} %bitcast.40, bf16[16,32,8,128]{3,2,1,0:T(8,128)(2,1)} %bitcast.41, bf16[16,32,8,128]{3,2,1,0:T(8,128)(2,1)} %bitcast.42, bf16[16,32,8,128]{3,2,1,0:T(8,128)(2,1)} %bitcast.43), kind=kLoop, calls=%fused_computation.2 | loop fusion | flops 6291456 | bytes 8388608 | tf_op jit(solution)/shard_map/concatenate | solution.py:241
  3.2 0.0 slice-start.1
  3.3 60.0 %all_to_all.19 = bf16[16,128,8,128]{3,2,1,0:T(8,128)(2,1)S(1)} all-to-all(bf16[16,128,8,128]{3,2,1,0:T(8,128)(2,1)S(1)} %pad_maximum_fusion), channel_id=1, replica_groups=mesh['dp'=8,'tm'=16] {'tm'}, dimensions={0} | all-to-all | bytes 8388608 | tf_op jit(solution)/shard_map/all_to_all | solution.py:242
  63.2 0.1 slice.16
  63.3 1.2 collective-permute-start
  64.6 0.0 slice-done
  64.6 0.0 slice-done.1
  64.6 2.4 %fusion.5.mat_ref = bf16[16,256,128]{2,1,0:T(8,128)(2,1)S(1)} fusion(bf16[256,2048,1]{1,0,2:T(8,128)(2,1)S(1)} %bitcast.29, bf16[2048,16,128]{2,1,0:T(8,128)(2,1)S(1)} %bitcast.45), kind=kOutput, calls=%fused_computation.4 | convolution fusion | flops 2148007936 | bytes 10485760 | tf_op jit(solution)/shard_map/td,dhe->hte/dot_general | solution.py:249
  66.9 4.4 %shard_map.84 = (bf16[16,16,8,128]{3,2,1,0:T(8,128)(2,1)S(1)}, bf16[16,16,8,128]{3,2,1,0:T(8,128)(2,1)}, bf16[16,3,16,2,8,128]{5,4,3,2,1,0:T(8,128)(2,1)}) custom-call(bf16[16,4,16,2,8,128]{5,4,3,2,1,0:T(8,128)(2,1)S(1)} %bitcast.26, bf16[16,256,128]{2,1,0:T(8,128)(2,1)S(1)} %fusion.5.mat_ref), custom_call_target="tpu_custom_call" | custom-call | flops 7000000000 | bytes 8388608 | tf_op jit(solution)/shard_map/pallas_call | solution.py:111
  71.3 0.1 collective-permute-start.1
  71.5 4.7 %all-to-all-start.1 = ((bf16[16,3,16,2,8,128]{5,4,3,2,1,0:T(8,128)(2,1)}), bf16[16,3,16,2,8,128]{5,4,3,2,1,0:T(8,128)(2,1)}, u32[]{:S(2)}, u32[]{:S(2)}) async-start(bf16[16,3,16,2,8,128]{5,4,3,2,1,0:T(8,128)(2,1)} %get-tuple-element.31), calls=%async_computation.1 | async-start | bytes 6291456 | tf_op jit(solution)/shard_map/all_to_all | solution.py:257
  76.1 0.0 collective-permute-done.1
  76.1 0.0 collective-permute-done.refs_1_
  76.2 0.8 shard_map.85
  76.9 1.4 collective-permute-start.4
  78.3 1.5 %collective-permute-start.5 = (bf16[512,512]{1,0:T(8,128)(2,1)S(1)}, bf16[512,512]{1,0:T(8,128)(2,1)S(1)}, u32[]{:S(2)}, u32[]{:S(2)}) collective-permute-start(bf16[512,512]{1,0:T(8,128)(2,1)S(1)} %get-tuple-element.28), channel_id=1, source_target_pairs={{0,96},{1,97},{2,98},{3,99},{4,100},{5,101},{6,102},{7,103},{8,104... | collective-permute-start | bytes 1572872 | tf_op jit(solution)/shard_map/ppermute | solution.py:268
  79.8 0.8 shard_map.86
  80.6 1.5 %collective-permute-start.2 = (bf16[512,512]{1,0:T(8,128)(2,1)S(1)}, bf16[512,512]{1,0:T(8,128)(2,1)S(1)}, u32[]{:S(2)}, u32[]{:S(2)}) collective-permute-start(bf16[512,512]{1,0:T(8,128)(2,1)S(1)} %get-tuple-element.23), channel_id=1, source_target_pairs={{0,96},{1,97},{2,98},{3,99},{4,100},{5,101},{6,102},{7,103},{8,104... | collective-permute-start | bytes 1572872 | tf_op jit(solution)/shard_map/ppermute | solution.py:271
  82.0 0.1 collective-permute-start.3
  82.1 9.6 %collective-permute-done.4.refs_4_ = bf16[512,512]{1,0:T(8,128)(2,1)S(1)} collective-permute-done((bf16[512,512]{1,0:T(8,128)(2,1)S(1)}, bf16[512,512]{1,0:T(8,128)(2,1)S(1)}, u32[]{:S(2)}, u32[]{:S(2)}) %collective-permute-start.4) | collective-permute-done | bytes 524320 | tf_op jit(solution)/shard_map/ppermute | solution.py:267
  91.7 0.0 collective-permute-done.5.refs_5_
  91.7 0.8 shard_map.88
  92.5 1.0 collective-permute-start.6
  93.5 1.8 %collective-permute-start.7 = (bf16[512,512]{1,0:T(8,128)(2,1)S(1)}, bf16[512,512]{1,0:T(8,128)(2,1)S(1)}, u32[]{:S(2)}, u32[]{:S(2)}) collective-permute-start(bf16[512,512]{1,0:T(8,128)(2,1)S(1)} %get-tuple-element.30), channel_id=1, source_target_pairs={{0,96},{1,97},{2,98},{3,99},{4,100},{5,101},{6,102},{7,103},{8,104... | collective-permute-start | bytes 1572872 | tf_op jit(solution)/shard_map/ppermute | solution.py:274
  95.2 7.3 %collective-permute-done.2.refs_4_ = bf16[512,512]{1,0:T(8,128)(2,1)S(1)} collective-permute-done((bf16[512,512]{1,0:T(8,128)(2,1)S(1)}, bf16[512,512]{1,0:T(8,128)(2,1)S(1)}, u32[]{:S(2)}, u32[]{:S(2)}) %collective-permute-start.2) | collective-permute-done | bytes 524320 | tf_op jit(solution)/shard_map/ppermute | solution.py:271
  102.6 0.4 collective-permute-done.3.refs_5_
  102.9 0.8 shard_map.87
  103.7 10.5 %collective-permute-done.6.came0 = bf16[512,512]{1,0:T(8,128)(2,1)S(1)} collective-permute-done((bf16[512,512]{1,0:T(8,128)(2,1)S(1)}, bf16[512,512]{1,0:T(8,128)(2,1)S(1)}, u32[]{:S(2)}, u32[]{:S(2)}) %collective-permute-start.6) | collective-permute-done | bytes 524320 | tf_op jit(solution)/shard_map/ppermute | solution.py:273
  114.2 0.0 collective-permute-done.7.came1
  114.2 1.1 shard_map.89
  115.2 0.8 all-to-all-done.1
  116.1 7.2 %all-to-all-start.2 = ((bf16[32,16,1024]{2,1,0:T(8,128)(2,1)}), bf16[32,16,1024]{2,1,0:T(8,128)(2,1)S(1)}, u32[]{:S(2)}, u32[]{:S(2)}) async-start(bf16[32,16,1024]{2,1,0:T(8,128)(2,1)} %bitcast.36), calls=%async_computation.2 | async-start | bytes 2097152 | tf_op jit(solution)/shard_map/all_to_all | solution.py:279
  123.3 4.0 %fusion.8 = (bf16[16,1,16,2,8,128]{5,4,3,2,1,0:T(8,128)(2,1)}, bf16[16,1,16,2,8,128]{5,4,3,2,1,0:T(8,128)(2,1)}, bf16[16,1,16,2,8,128]{5,4,3,2,1,0:T(8,128)(2,1)}) fusion(bf16[16,3,16,2,8,128]{5,4,3,2,1,0:T(8,128)(2,1)} %all-to-all-done.1), kind=kLoop, calls=%fused_computation.5 | loop fusion | bytes 6291456 | tf_op jit(solution)/shard_map/slice | solution.py:283
  127.3 13.1 %all-to-all-done.2 = bf16[32,16,1024]{2,1,0:T(8,128)(2,1)S(1)} async-done(((bf16[32,16,1024]{2,1,0:T(8,128)(2,1)}), bf16[32,16,1024]{2,1,0:T(8,128)(2,1)S(1)}, u32[]{:S(2)}, u32[]{:S(2)}) %all-to-all-start.2) | async-done | bytes 1048608 | tf_op jit(solution)/shard_map/all_to_all | solution.py:279
  140.4 0.9 shard_map.90
  (1 shorter events, 0.0 us)
Async XLA Ops:
  0.6 63.9 %slice-start = ((s8[8388608]{0:T(1024)(128)(4,1)}), s8[4194304]{0:T(1024)(128)(4,1)S(1)}, s32[]{:S(2)}) async-start(s8[8388608]{0:T(1024)(128)(4,1)} %bitcast.44), calls=%async_computation.3 | async-start | bytes 8388608
  3.2 61.3 %slice-start.1 = ((s8[8388608]{0:T(1024)(128)(4,1)}), s8[4194304]{0:T(1024)(128)(4,1)S(1)}, s32[]{:S(2)}) async-start(s8[8388608]{0:T(1024)(128)(4,1)} %bitcast.44), calls=%async_computation.4 | async-start | bytes 8388608
  63.3 12.8 %collective-permute-start = (bf16[256,2048]{1,0:T(8,128)(2,1)S(1)}, bf16[256,2048]{1,0:T(8,128)(2,1)S(1)}, u32[]{:S(2)}, u32[]{:S(2)}) collective-permute-start(bf16[256,2048]{1,0:T(8,128)(2,1)S(1)} %bitcast.28), channel_id=1, source_target_pairs={{0,1},{1,0},{2,3},{3,2},{4,5},{5,4},{6,7},{7,6},{8,9},{9,8},{10,11... | collective-permute-start | bytes 3145736 | tf_op jit(solution)/shard_map/ppermute | solution.py:260
  71.3 4.8 %collective-permute-start.1 = (bf16[16,16,8,128]{3,2,1,0:T(8,128)(2,1)}, bf16[16,16,8,128]{3,2,1,0:T(8,128)(2,1)S(1)}, u32[]{:S(2)}, u32[]{:S(2)}) collective-permute-start(bf16[16,16,8,128]{3,2,1,0:T(8,128)(2,1)} %get-tuple-element.20), channel_id=1, source_target_pairs={{0,1},{1,0},{2,3},{3,2},{4,5},{5,4},{6,7},{7,6},{8,9},{9,8},{10,11... | collective-permute-start | bytes 1572872 | tf_op jit(solution)/shard_map/ppermute | solution.py:261
  71.5 44.6 %all-to-all-start.1 = ((bf16[16,3,16,2,8,128]{5,4,3,2,1,0:T(8,128)(2,1)}), bf16[16,3,16,2,8,128]{5,4,3,2,1,0:T(8,128)(2,1)}, u32[]{:S(2)}, u32[]{:S(2)}) async-start(bf16[16,3,16,2,8,128]{5,4,3,2,1,0:T(8,128)(2,1)} %get-tuple-element.31), calls=%async_computation.1 | async-start | bytes 6291456 | tf_op jit(solution)/shard_map/all_to_all | solution.py:257
  76.9 14.8 %collective-permute-start.4 = (bf16[512,512]{1,0:T(8,128)(2,1)S(1)}, bf16[512,512]{1,0:T(8,128)(2,1)S(1)}, u32[]{:S(2)}, u32[]{:S(2)}) collective-permute-start(bf16[512,512]{1,0:T(8,128)(2,1)S(1)} %get-tuple-element.27), channel_id=1, source_target_pairs={{0,32},{1,33},{2,34},{3,35},{4,36},{5,37},{6,38},{7,39},{8,40},{9,... | collective-permute-start | bytes 1572872 | tf_op jit(solution)/shard_map/ppermute | solution.py:267
  78.3 13.4 %collective-permute-start.5 = (bf16[512,512]{1,0:T(8,128)(2,1)S(1)}, bf16[512,512]{1,0:T(8,128)(2,1)S(1)}, u32[]{:S(2)}, u32[]{:S(2)}) collective-permute-start(bf16[512,512]{1,0:T(8,128)(2,1)S(1)} %get-tuple-element.28), channel_id=1, source_target_pairs={{0,96},{1,97},{2,98},{3,99},{4,100},{5,101},{6,102},{7,103},{8,104... | collective-permute-start | bytes 1572872 | tf_op jit(solution)/shard_map/ppermute | solution.py:268
  80.6 22.0 %collective-permute-start.2 = (bf16[512,512]{1,0:T(8,128)(2,1)S(1)}, bf16[512,512]{1,0:T(8,128)(2,1)S(1)}, u32[]{:S(2)}, u32[]{:S(2)}) collective-permute-start(bf16[512,512]{1,0:T(8,128)(2,1)S(1)} %get-tuple-element.23), channel_id=1, source_target_pairs={{0,96},{1,97},{2,98},{3,99},{4,100},{5,101},{6,102},{7,103},{8,104... | collective-permute-start | bytes 1572872 | tf_op jit(solution)/shard_map/ppermute | solution.py:271
  82.0 20.9 %collective-permute-start.3 = (bf16[512,512]{1,0:T(8,128)(2,1)S(1)}, bf16[512,512]{1,0:T(8,128)(2,1)S(1)}, u32[]{:S(2)}, u32[]{:S(2)}) collective-permute-start(bf16[512,512]{1,0:T(8,128)(2,1)S(1)} %get-tuple-element.24), channel_id=1, source_target_pairs={{0,32},{1,33},{2,34},{3,35},{4,36},{5,37},{6,38},{7,39},{8,40},{9,... | collective-permute-start | bytes 1572872 | tf_op jit(solution)/shard_map/ppermute | solution.py:270
  92.5 21.7 %collective-permute-start.6 = (bf16[512,512]{1,0:T(8,128)(2,1)S(1)}, bf16[512,512]{1,0:T(8,128)(2,1)S(1)}, u32[]{:S(2)}, u32[]{:S(2)}) collective-permute-start(bf16[512,512]{1,0:T(8,128)(2,1)S(1)} %get-tuple-element.29), channel_id=1, source_target_pairs={{0,32},{1,33},{2,34},{3,35},{4,36},{5,37},{6,38},{7,39},{8,40},{9,... | collective-permute-start | bytes 1572872 | tf_op jit(solution)/shard_map/ppermute | solution.py:273
  93.5 20.7 %collective-permute-start.7 = (bf16[512,512]{1,0:T(8,128)(2,1)S(1)}, bf16[512,512]{1,0:T(8,128)(2,1)S(1)}, u32[]{:S(2)}, u32[]{:S(2)}) collective-permute-start(bf16[512,512]{1,0:T(8,128)(2,1)S(1)} %get-tuple-element.30), channel_id=1, source_target_pairs={{0,96},{1,97},{2,98},{3,99},{4,100},{5,101},{6,102},{7,103},{8,104... | collective-permute-start | bytes 1572872 | tf_op jit(solution)/shard_map/ppermute | solution.py:274
  116.1 24.3 %all-to-all-start.2 = ((bf16[32,16,1024]{2,1,0:T(8,128)(2,1)}), bf16[32,16,1024]{2,1,0:T(8,128)(2,1)S(1)}, u32[]{:S(2)}, u32[]{:S(2)}) async-start(bf16[32,16,1024]{2,1,0:T(8,128)(2,1)} %bitcast.36), calls=%async_computation.2 | async-start | bytes 2097152 | tf_op jit(solution)/shard_map/all_to_all | solution.py:279

commit v8 on v7

--- a/solution.py
+++ b/solution.py
@@ -44,6 +44,31 @@
 
 def dot_nn(a, b):
     return lax.dot_general(a, b, (((1,), (0,)), ((), ())), preferred_element_type=jnp.float32)
+
+
+def pack_kernel(*refs):
+    ins, out, sems = refs[:4], refs[4], refs[5]
+    tiles = TOK * 2
+    copies = [
+        pltpu.make_async_copy(ref, out.at[:, pl.ds(n * tiles, tiles)], sems.at[n])
+        for n, ref in enumerate(ins)
+    ]
+    for copy in copies:
+        copy.start(priority=1)
+    for copy in copies:
+        copy.wait()
+
+
+def pack(pieces):
+    frames, tiles, rows, lanes = pieces[0].shape
+    return pl.pallas_call(
+        pack_kernel,
+        in_specs=[pl.BlockSpec(memory_space=pltpu.HBM)] * 4,
+        out_specs=pl.BlockSpec(memory_space=pltpu.VMEM),
+        out_shape=jax.ShapeDtypeStruct((frames, 4 * tiles, rows, lanes), jnp.bfloat16),
+        scratch_shapes=[pltpu.SemaphoreType.DMA((4,))],
+        compiler_params=pltpu.CompilerParams(vmem_limit_bytes=VMEM),
+    )(*(pltpu.with_memory_space_constraint(p, pltpu.HBM) for p in pieces))
 
 
 def attend_groups(units, bias):
@@ -238,7 +263,7 @@
     pieces.append(
         grad_out.reshape(FRAMES, 2, 8, HEADS, E).transpose(0, 1, 3, 2, 4).reshape(FRAMES, tiles, 8, E)
     )
-    packed = jnp.concatenate(pieces, axis=1)
+    packed = pack(pieces)
     packed = lax.all_to_all(packed, "tm", split_axis=0, concat_axis=0, tiled=True)
     g_tok = (
         packed[:, 3 * tiles :]
@@ -257,7 +282,8 @@
     back = lax.all_to_all(grads, "tm", split_axis=0, concat_axis=0, tiled=True)
 
     own = own.reshape(TOKENS, GROUP, E)
-    g_swapped = lax.ppermute(g_tok, AXES, core_swap())
+    g_sent, other = lax.optimization_barrier((g_tok, other))
+    g_swapped = lax.ppermute(g_sent, AXES, core_swap())
     swapped = lax.ppermute(other, AXES, core_swap()).reshape(TOKENS, GROUP, E)
 
     ins = [g_tok, g_swapped, own, swapped]

time: 142 us -> 141 us (level)
  other arithmetic: 2.58 us -> 0.01 us
  Pallas kernels: 9.36 us -> 11.7 us
    concatenate x1 -> x0, other arithmetic: 2.58 us -> none  [shards(): packed = jnp.concatenate(pieces, axis=1)]
    pallas_call x0 -> x1, Pallas kernels: none -> 2.36 us  [pack(): pl.pallas_call(pack_kernel, in_specs=[pl.BlockSpec(memory_space=pltpu.HBM...]
  transfers between devices with their start and end apart: 10 -> 10, of which waited for: 6 -> 6; matrix products, arithmetic and copies ran while one was open for 5% -> 3% of each run, Pallas kernels for 6% -> 3%
where the time goes in v8:
time: 141 us
  blocking collectives  60 us (43%)
  waiting for transfers between devices  41.7 us (30%)
  starting transfers between devices  20.3 us (14%)
  Pallas kernels  11.7 us (8%)
  local copies, waits for them, and re-layouts  4.09 us (3%)
  matrix products  2.37 us (2%)
    all_to_all x1, blocking collectives, shards(): lax.all_to_all(packed, 'tm', split_axis=0, concat_axis=0, tiled=True)  60 us
    all_to_all x1, waiting for transfers between devices, shards(): lax.all_to_all(block, AXES, split_axis=0, concat_axis=0, tiled=True, axis...  13.1 us
    ppermute x1, waiting for transfers between devices, shards(): up0 = lax.ppermute(up0, AXES, y_shift(1))  10.5 us
    ppermute x1, waiting for transfers between devices, shards(): left = lax.ppermute(left, AXES, y_shift(1))  9.57 us
    ppermute x1, waiting for transfers between devices, shards(): down0 = lax.ppermute(down0, AXES, y_shift(-1))  7.36 us
    all_to_all x1, starting transfers between devices, shards(): lax.all_to_all(block, AXES, split_axis=0, concat_axis=0, tiled=True, axis...  7.18 us
    all_to_all x1, starting transfers between devices, shards(): back = lax.all_to_all(grads, 'tm', split_axis=0, concat_axis=0, tiled=True)  4.62 us
    pallas_call x1, Pallas kernels, attend(): pl.pallas_call(attend_kernel, in_specs=[whole, whole], out_specs=[whole]...  4.39 us
  transfers between devices with their start and end apart: 10, of which 6 were waited for; matrix products, arithmetic and copies ran while one was open for 3% of the time, Pallas kernels for 3%

profile of v8, /device:TPU:1, one launch (start us, length us, event | category | flops | bytes accessed | tf_op | source)
XLA Modules:
  0.0 140.9 jit_solution(4246403969883096419)
XLA Ops:
  0.6 0.0 slice-start
  0.6 2.4 %shard_map.84 = bf16[16,128,8,128]{3,2,1,0:T(8,128)(2,1)S(1)} custom-call(bf16[16,32,8,128]{3,2,1,0:T(8,128)(2,1)} %bitcast.40, bf16[16,32,8,128]{3,2,1,0:T(8,128)(2,1)} %bitcast.41, bf16[16,32,8,128]{3,2,1,0:T(8,128)(2,1)} %bitcast.42, bf16[16,32,8,128]{3,2,1,0:T(8,128)(2,1)} %bitcast.43), custom_call_target="tpu_custom_call" | custom-call | tf_op jit(solution)/shard_map/pallas_call | solution.py:64
  3.0 0.0 slice-start.1
  3.0 60.0 %all_to_all.19 = bf16[16,128,8,128]{3,2,1,0:T(8,128)(2,1)S(1)} all-to-all(bf16[16,128,8,128]{3,2,1,0:T(8,128)(2,1)S(1)} %shard_map.84), channel_id=1, replica_groups=mesh['dp'=8,'tm'=16] {'tm'}, dimensions={0} | all-to-all | bytes 8388608 | tf_op jit(solution)/shard_map/all_to_all | solution.py:267
  63.0 0.1 slice.16
  63.1 0.0 slice-done
  63.1 0.0 slice-done.1
  63.1 2.4 %fusion.5.mat_ref = bf16[16,256,128]{2,1,0:T(8,128)(2,1)S(1)} fusion(bf16[256,2048,1]{1,0,2:T(8,128)(2,1)S(1)} %bitcast.28, bf16[2048,16,128]{2,1,0:T(8,128)(2,1)S(1)} %bitcast.45), kind=kOutput, calls=%fused_computation.3 | convolution fusion | flops 2148007936 | bytes 10485760 | tf_op jit(solution)/shard_map/td,dhe->hte/dot_general | solution.py:274
  65.5 4.4 %shard_map.85 = (bf16[16,16,8,128]{3,2,1,0:T(8,128)(2,1)S(1)}, bf16[16,16,8,128]{3,2,1,0:T(8,128)(2,1)}, bf16[16,3,16,2,8,128]{5,4,3,2,1,0:T(8,128)(2,1)}) custom-call(bf16[16,4,16,2,8,128]{5,4,3,2,1,0:T(8,128)(2,1)S(1)} %bitcast.26, bf16[16,256,128]{2,1,0:T(8,128)(2,1)S(1)} %fusion.5.mat_ref), custom_call_target="tpu_custom_call" | custom-call | flops 7000000000 | bytes 8388608 | tf_op jit(solution)/shard_map/pallas_call | solution.py:136
  69.9 1.2 collective-permute-start
  71.1 0.1 collective-permute-start.1
  71.2 4.6 %all-to-all-start.1 = ((bf16[16,3,16,2,8,128]{5,4,3,2,1,0:T(8,128)(2,1)}), bf16[16,3,16,2,8,128]{5,4,3,2,1,0:T(8,128)(2,1)}, u32[]{:S(2)}, u32[]{:S(2)}) async-start(bf16[16,3,16,2,8,128]{5,4,3,2,1,0:T(8,128)(2,1)} %get-tuple-element.35), calls=%async_computation.1 | async-start | bytes 6291456 | tf_op jit(solution)/shard_map/all_to_all | solution.py:282
  75.8 0.0 collective-permute-done.1
  75.8 0.0 collective-permute-done.refs_1_
  75.9 0.8 shard_map.86
  76.6 1.4 collective-permute-start.4
  78.0 1.5 %collective-permute-start.5 = (bf16[512,512]{1,0:T(8,128)(2,1)S(1)}, bf16[512,512]{1,0:T(8,128)(2,1)S(1)}, u32[]{:S(2)}, u32[]{:S(2)}) collective-permute-start(bf16[512,512]{1,0:T(8,128)(2,1)S(1)} %get-tuple-element.32), channel_id=1, source_target_pairs={{0,96},{1,97},{2,98},{3,99},{4,100},{5,101},{6,102},{7,103},{8,104... | collective-permute-start | bytes 1572872 | tf_op jit(solution)/shard_map/ppermute | solution.py:294
  79.5 0.8 shard_map.87
  80.3 1.5 %collective-permute-start.2 = (bf16[512,512]{1,0:T(8,128)(2,1)S(1)}, bf16[512,512]{1,0:T(8,128)(2,1)S(1)}, u32[]{:S(2)}, u32[]{:S(2)}) collective-permute-start(bf16[512,512]{1,0:T(8,128)(2,1)S(1)} %get-tuple-element.27), channel_id=1, source_target_pairs={{0,96},{1,97},{2,98},{3,99},{4,100},{5,101},{6,102},{7,103},{8,104... | collective-permute-start | bytes 1572872 | tf_op jit(solution)/shard_map/ppermute | solution.py:297
  81.7 0.1 collective-permute-start.3
  81.8 9.6 %collective-permute-done.4.refs_4_ = bf16[512,512]{1,0:T(8,128)(2,1)S(1)} collective-permute-done((bf16[512,512]{1,0:T(8,128)(2,1)S(1)}, bf16[512,512]{1,0:T(8,128)(2,1)S(1)}, u32[]{:S(2)}, u32[]{:S(2)}) %collective-permute-start.4) | collective-permute-done | bytes 524320 | tf_op jit(solution)/shard_map/ppermute | solution.py:293
  91.4 0.0 collective-permute-done.5.refs_5_
  91.4 0.8 shard_map.89
  92.2 1.0 collective-permute-start.6
  93.2 1.8 %collective-permute-start.7 = (bf16[512,512]{1,0:T(8,128)(2,1)S(1)}, bf16[512,512]{1,0:T(8,128)(2,1)S(1)}, u32[]{:S(2)}, u32[]{:S(2)}) collective-permute-start(bf16[512,512]{1,0:T(8,128)(2,1)S(1)} %get-tuple-element.34), channel_id=1, source_target_pairs={{0,96},{1,97},{2,98},{3,99},{4,100},{5,101},{6,102},{7,103},{8,104... | collective-permute-start | bytes 1572872 | tf_op jit(solution)/shard_map/ppermute | solution.py:300
  94.9 7.4 %collective-permute-done.2.refs_4_ = bf16[512,512]{1,0:T(8,128)(2,1)S(1)} collective-permute-done((bf16[512,512]{1,0:T(8,128)(2,1)S(1)}, bf16[512,512]{1,0:T(8,128)(2,1)S(1)}, u32[]{:S(2)}, u32[]{:S(2)}) %collective-permute-start.2) | collective-permute-done | bytes 524320 | tf_op jit(solution)/shard_map/ppermute | solution.py:297
  102.3 0.4 collective-permute-done.3.refs_5_
  102.6 0.8 shard_map.88
  103.4 10.5 %collective-permute-done.6.came0 = bf16[512,512]{1,0:T(8,128)(2,1)S(1)} collective-permute-done((bf16[512,512]{1,0:T(8,128)(2,1)S(1)}, bf16[512,512]{1,0:T(8,128)(2,1)S(1)}, u32[]{:S(2)}, u32[]{:S(2)}) %collective-permute-start.6) | collective-permute-done | bytes 524320 | tf_op jit(solution)/shard_map/ppermute | solution.py:299
  113.9 0.0 collective-permute-done.7.came1
  113.9 1.1 shard_map.90
  114.9 0.9 all-to-all-done.1
  115.8 7.2 %all-to-all-start.2 = ((bf16[32,16,1024]{2,1,0:T(8,128)(2,1)}), bf16[32,16,1024]{2,1,0:T(8,128)(2,1)S(1)}, u32[]{:S(2)}, u32[]{:S(2)}) async-start(bf16[32,16,1024]{2,1,0:T(8,128)(2,1)} %bitcast.36), calls=%async_computation.2 | async-start | bytes 2097152 | tf_op jit(solution)/shard_map/all_to_all | solution.py:305
  123.0 4.0 %fusion.8 = (bf16[16,1,16,2,8,128]{5,4,3,2,1,0:T(8,128)(2,1)}, bf16[16,1,16,2,8,128]{5,4,3,2,1,0:T(8,128)(2,1)}, bf16[16,1,16,2,8,128]{5,4,3,2,1,0:T(8,128)(2,1)}) fusion(bf16[16,3,16,2,8,128]{5,4,3,2,1,0:T(8,128)(2,1)} %all-to-all-done.1), kind=kLoop, calls=%fused_computation.4 | loop fusion | bytes 6291456 | tf_op jit(solution)/shard_map/slice | solution.py:309
  127.0 13.1 %all-to-all-done.2 = bf16[32,16,1024]{2,1,0:T(8,128)(2,1)S(1)} async-done(((bf16[32,16,1024]{2,1,0:T(8,128)(2,1)}), bf16[32,16,1024]{2,1,0:T(8,128)(2,1)S(1)}, u32[]{:S(2)}, u32[]{:S(2)}) %all-to-all-start.2) | async-done | bytes 1048608 | tf_op jit(solution)/shard_map/all_to_all | solution.py:305
  140.0 0.9 shard_map.91
  (1 shorter events, 0.0 us)
Async XLA Ops:
  0.6 62.5 %slice-start = ((s8[8388608]{0:T(1024)(128)(4,1)}), s8[4194304]{0:T(1024)(128)(4,1)S(1)}, s32[]{:S(2)}) async-start(s8[8388608]{0:T(1024)(128)(4,1)} %bitcast.44), calls=%async_computation.3 | async-start | bytes 8388608
  3.0 60.1 %slice-start.1 = ((s8[8388608]{0:T(1024)(128)(4,1)}), s8[4194304]{0:T(1024)(128)(4,1)S(1)}, s32[]{:S(2)}) async-start(s8[8388608]{0:T(1024)(128)(4,1)} %bitcast.44), calls=%async_computation.4 | async-start | bytes 8388608
  69.9 6.0 %collective-permute-start = (bf16[256,2048]{1,0:T(8,128)(2,1)S(1)}, bf16[256,2048]{1,0:T(8,128)(2,1)S(1)}, u32[]{:S(2)}, u32[]{:S(2)}) collective-permute-start(bf16[256,2048]{1,0:T(8,128)(2,1)S(1)} %bitcast.29), channel_id=1, source_target_pairs={{0,1},{1,0},{2,3},{3,2},{4,5},{5,4},{6,7},{7,6},{8,9},{9,8},{10,11... | collective-permute-start | bytes 3145736 | tf_op jit(solution)/shard_map/ppermute | solution.py:286
  71.1 4.7 %collective-permute-start.1 = (bf16[16,16,8,128]{3,2,1,0:T(8,128)(2,1)}, bf16[16,16,8,128]{3,2,1,0:T(8,128)(2,1)S(1)}, u32[]{:S(2)}, u32[]{:S(2)}) collective-permute-start(bf16[16,16,8,128]{3,2,1,0:T(8,128)(2,1)} %get-tuple-element.24), channel_id=1, source_target_pairs={{0,1},{1,0},{2,3},{3,2},{4,5},{5,4},{6,7},{7,6},{8,9},{9,8},{10,11... | collective-permute-start | bytes 1572872 | tf_op jit(solution)/shard_map/ppermute | solution.py:287
  71.2 44.6 %all-to-all-start.1 = ((bf16[16,3,16,2,8,128]{5,4,3,2,1,0:T(8,128)(2,1)}), bf16[16,3,16,2,8,128]{5,4,3,2,1,0:T(8,128)(2,1)}, u32[]{:S(2)}, u32[]{:S(2)}) async-start(bf16[16,3,16,2,8,128]{5,4,3,2,1,0:T(8,128)(2,1)} %get-tuple-element.35), calls=%async_computation.1 | async-start | bytes 6291456 | tf_op jit(solution)/shard_map/all_to_all | solution.py:282
  76.6 14.8 %collective-permute-start.4 = (bf16[512,512]{1,0:T(8,128)(2,1)S(1)}, bf16[512,512]{1,0:T(8,128)(2,1)S(1)}, u32[]{:S(2)}, u32[]{:S(2)}) collective-permute-start(bf16[512,512]{1,0:T(8,128)(2,1)S(1)} %get-tuple-element.31), channel_id=1, source_target_pairs={{0,32},{1,33},{2,34},{3,35},{4,36},{5,37},{6,38},{7,39},{8,40},{9,... | collective-permute-start | bytes 1572872 | tf_op jit(solution)/shard_map/ppermute | solution.py:293
  78.0 13.4 %collective-permute-start.5 = (bf16[512,512]{1,0:T(8,128)(2,1)S(1)}, bf16[512,512]{1,0:T(8,128)(2,1)S(1)}, u32[]{:S(2)}, u32[]{:S(2)}) collective-permute-start(bf16[512,512]{1,0:T(8,128)(2,1)S(1)} %get-tuple-element.32), channel_id=1, source_target_pairs={{0,96},{1,97},{2,98},{3,99},{4,100},{5,101},{6,102},{7,103},{8,104... | collective-permute-start | bytes 1572872 | tf_op jit(solution)/shard_map/ppermute | solution.py:294
  80.3 22.0 %collective-permute-start.2 = (bf16[512,512]{1,0:T(8,128)(2,1)S(1)}, bf16[512,512]{1,0:T(8,128)(2,1)S(1)}, u32[]{:S(2)}, u32[]{:S(2)}) collective-permute-start(bf16[512,512]{1,0:T(8,128)(2,1)S(1)} %get-tuple-element.27), channel_id=1, source_target_pairs={{0,96},{1,97},{2,98},{3,99},{4,100},{5,101},{6,102},{7,103},{8,104... | collective-permute-start | bytes 1572872 | tf_op jit(solution)/shard_map/ppermute | solution.py:297
  81.7 20.9 %collective-permute-start.3 = (bf16[512,512]{1,0:T(8,128)(2,1)S(1)}, bf16[512,512]{1,0:T(8,128)(2,1)S(1)}, u32[]{:S(2)}, u32[]{:S(2)}) collective-permute-start(bf16[512,512]{1,0:T(8,128)(2,1)S(1)} %get-tuple-element.28), channel_id=1, source_target_pairs={{0,32},{1,33},{2,34},{3,35},{4,36},{5,37},{6,38},{7,39},{8,40},{9,... | collective-permute-start | bytes 1572872 | tf_op jit(solution)/shard_map/ppermute | solution.py:296
  92.2 21.7 %collective-permute-start.6 = (bf16[512,512]{1,0:T(8,128)(2,1)S(1)}, bf16[512,512]{1,0:T(8,128)(2,1)S(1)}, u32[]{:S(2)}, u32[]{:S(2)}) collective-permute-start(bf16[512,512]{1,0:T(8,128)(2,1)S(1)} %get-tuple-element.33), channel_id=1, source_target_pairs={{0,32},{1,33},{2,34},{3,35},{4,36},{5,37},{6,38},{7,39},{8,40},{9,... | collective-permute-start | bytes 1572872 | tf_op jit(solution)/shard_map/ppermute | solution.py:299
  93.2 20.7 %collective-permute-start.7 = (bf16[512,512]{1,0:T(8,128)(2,1)S(1)}, bf16[512,512]{1,0:T(8,128)(2,1)S(1)}, u32[]{:S(2)}, u32[]{:S(2)}) collective-permute-start(bf16[512,512]{1,0:T(8,128)(2,1)S(1)} %get-tuple-element.34), channel_id=1, source_target_pairs={{0,96},{1,97},{2,98},{3,99},{4,100},{5,101},{6,102},{7,103},{8,104... | collective-permute-start | bytes 1572872 | tf_op jit(solution)/shard_map/ppermute | solution.py:300
  115.8 24.3 %all-to-all-start.2 = ((bf16[32,16,1024]{2,1,0:T(8,128)(2,1)}), bf16[32,16,1024]{2,1,0:T(8,128)(2,1)S(1)}, u32[]{:S(2)}, u32[]{:S(2)}) async-start(bf16[32,16,1024]{2,1,0:T(8,128)(2,1)} %bitcast.36), calls=%async_computation.2 | async-start | bytes 2097152 | tf_op jit(solution)/shard_map/all_to_all | solution.py:305

commit v9 on v8

--- a/solution.py
+++ b/solution.py
@@ -81,11 +81,10 @@
         (p * (gp - jnp.sum(p * gp, axis=0, keepdims=True))).astype(jnp.bfloat16)
         for p, gp in zip(probs, grad_probs)
     ]
-    gv = [dot_nn(w, u[3]).astype(jnp.bfloat16) for w, u in zip(weights, units)]
-    gk = [(dot_nn(gs, u[0]) * SCALE).astype(jnp.bfloat16) for gs, u in zip(grad_scores, units)]
-    attended = [dot_tn(w, u[2]).astype(jnp.bfloat16) for w, u in zip(weights, units)]
-    gq = [(dot_tn(gs, u[1]) * SCALE).astype(jnp.bfloat16) for gs, u in zip(grad_scores, units)]
-    return attended, zip(gq, gk, gv)
+    yield 2, [dot_nn(w, u[3]).astype(jnp.bfloat16) for w, u in zip(weights, units)]
+    yield 1, [(dot_nn(gs, u[0]) * SCALE).astype(jnp.bfloat16) for gs, u in zip(grad_scores, units)]
+    yield 3, [dot_tn(w, u[2]).astype(jnp.bfloat16) for w, u in zip(weights, units)]
+    yield 0, [(dot_tn(gs, u[1]) * SCALE).astype(jnp.bfloat16) for gs, u in zip(grad_scores, units)]
 
 
 def attend_kernel(packed_ref, mat_ref, own_ref, other_ref, grads_ref, bias_ref, out_ref, half_ref, g_ref, sems):
@@ -98,12 +97,13 @@
     first = lax.rem(lax.axis_index("tm"), 2) == 0
     ids = [(t, h) for t in range(STEP_TOK) for h in range(GROUPS)]
 
-    def out_copies(step):
+    def out_copy(step, n):
         slot, tokens = step % 2, pl.ds(step * STEP_TOK, STEP_TOK)
-        return (
-            pltpu.make_async_copy(half_ref.at[slot], other_ref.at[:, tokens], sems.at[0, slot]),
-            pltpu.make_async_copy(out_ref.at[slot], grads_ref.at[:, :, tokens], sems.at[1, slot]),
-        )
+        if n == 3:
+            here, there = half_ref.at[slot], other_ref.at[:, tokens]
+        else:
+            here, there = out_ref.at[slot, :, n], grads_ref.at[:, n, tokens]
+        return pltpu.make_async_copy(here, there, sems.at[n, slot])
 
     for step in range(STEPS):
         start = step * STEP_TOK
@@ -111,23 +111,22 @@
         for t, h in ids:
             parts = [packed_ref[:, n, start + t, h] for n in range(3)] + [g_ref[:, start + t, h]]
             units.append([part.reshape(ROWS, E) for part in parts])
-        attended, grads = attend_groups(units, bias_ref[...])
-        if step >= 2:
-            for copy in out_copies(step - 2):
-                copy.wait()
-        for (t, h), three in zip(ids, grads):
-            for n, grad in enumerate(three):
-                out_ref[step % 2, :, n, t, h] = grad.reshape(FRAMES, GROUP, E)
-        for t in range(STEP_TOK):
-            pair = attended[GROUPS * t : GROUPS * (t + 1)]
-            low, high = (a.reshape(FRAMES, GROUP, E) for a in pair)
-            own_ref[:, start + t] = jnp.where(first, low, high)
-            half_ref[step % 2, :, t] = jnp.where(first, high, low)
-        for copy in out_copies(step):
-            copy.start()
+        for n, values in attend_groups(units, bias_ref[...]):
+            if step >= 2:
+                out_copy(step - 2, n).wait()
+            blocks = [value.reshape(FRAMES, GROUP, E) for value in values]
+            for t in range(STEP_TOK):
+                low, high = blocks[GROUPS * t : GROUPS * (t + 1)]
+                if n == 3:
+                    own_ref[:, start + t] = jnp.where(first, low, high)
+                    half_ref[step % 2, :, t] = jnp.where(first, high, low)
+                else:
+                    out_ref[step % 2, :, n, t, 0] = low
+                    out_ref[step % 2, :, n, t, 1] = high
+            out_copy(step, n).start()
     for step in range(max(STEPS - 2, 0), STEPS):
-        for copy in out_copies(step):
-            copy.wait()
+        for n in range(4):
+            out_copy(step, n).wait()
 
 
 def attend(packed, grad_attended):
@@ -147,7 +146,7 @@
             pltpu.VMEM((2, FRAMES, 3, STEP_TOK, GROUPS, GROUP, E), jnp.bfloat16),
             pltpu.VMEM((2, FRAMES, STEP_TOK, GROUP, E), jnp.bfloat16),
             pltpu.VMEM((FRAMES, TOK, GROUPS, GROUP, E), jnp.bfloat16),
-            pltpu.SemaphoreType.DMA((2, 2)),
+            pltpu.SemaphoreType.DMA((4, 2)),
         ],
         compiler_params=pltpu.CompilerParams(vmem_limit_bytes=VMEM),
         cost_estimate=pl.CostEstimate(flops=7 * 10**9, bytes_accessed=8 * 2**20, transcendentals=0),

time: 141 us -> 141 us (level)
  no operation moved by 1% of the time
where the time goes in v9:
time: 141 us
  blocking collectives  60 us (43%)
  waiting for transfers between devices  41.7 us (30%)
  starting transfers between devices  20.3 us (14%)
  Pallas kernels  11.4 us (8%)
  local copies, waits for them, and re-layouts  4.09 us (3%)
  matrix products  2.37 us (2%)
    all_to_all x1, blocking collectives, shards(): lax.all_to_all(packed, 'tm', split_axis=0, concat_axis=0, tiled=True)  60 us
    all_to_all x1, waiting for transfers between devices, shards(): lax.all_to_all(block, AXES, split_axis=0, concat_axis=0, tiled=True, axis...  13.1 us
    ppermute x1, waiting for transfers between devices, shards(): up0 = lax.ppermute(up0, AXES, y_shift(1))  10.5 us
    ppermute x1, waiting for transfers between devices, shards(): left = lax.ppermute(left, AXES, y_shift(1))  9.57 us
    ppermute x1, waiting for transfers between devices, shards(): down0 = lax.ppermute(down0, AXES, y_shift(-1))  7.35 us
    all_to_all x1, starting transfers between devices, shards(): lax.all_to_all(block, AXES, split_axis=0, concat_axis=0, tiled=True, axis...  7.17 us
    all_to_all x1, starting transfers between devices, shards(): back = lax.all_to_all(grads, 'tm', split_axis=0, concat_axis=0, tiled=True)  4.62 us
    pallas_call x1, Pallas kernels, attend(): pl.pallas_call(attend_kernel, in_specs=[whole, whole], out_specs=[whole]...  4.09 us
  transfers between devices with their start and end apart: 10, of which 6 were waited for; matrix products, arithmetic and copies ran while one was open for 3% of the time, Pallas kernels for 3%

profile of v9, /device:TPU:1, one launch (start us, length us, event | category | flops | bytes accessed | tf_op | source)
XLA Modules:
  0.0 140.6 jit_solution(6567058114959524891)
XLA Ops:
  0.6 0.0 slice-start
  0.6 2.4 %shard_map.84 = bf16[16,128,8,128]{3,2,1,0:T(8,128)(2,1)S(1)} custom-call(bf16[16,32,8,128]{3,2,1,0:T(8,128)(2,1)} %bitcast.40, bf16[16,32,8,128]{3,2,1,0:T(8,128)(2,1)} %bitcast.41, bf16[16,32,8,128]{3,2,1,0:T(8,128)(2,1)} %bitcast.42, bf16[16,32,8,128]{3,2,1,0:T(8,128)(2,1)} %bitcast.43), custom_call_target="tpu_custom_call" | custom-call | tf_op jit(solution)/shard_map/pallas_call | solution.py:64
  3.0 0.0 slice-start.1
  3.0 60.0 %all_to_all.19 = bf16[16,128,8,128]{3,2,1,0:T(8,128)(2,1)S(1)} all-to-all(bf16[16,128,8,128]{3,2,1,0:T(8,128)(2,1)S(1)} %shard_map.84), channel_id=1, replica_groups=mesh['dp'=8,'tm'=16] {'tm'}, dimensions={0} | all-to-all | bytes 8388608 | tf_op jit(solution)/shard_map/all_to_all | solution.py:266
  63.0 0.1 slice.16
  63.1 0.0 slice-done
  63.1 0.0 slice-done.1
  63.1 2.4 %fusion.5.mat_ref = bf16[16,256,128]{2,1,0:T(8,128)(2,1)S(1)} fusion(bf16[256,2048,1]{1,0,2:T(8,128)(2,1)S(1)} %bitcast.28, bf16[2048,16,128]{2,1,0:T(8,128)(2,1)S(1)} %bitcast.45), kind=kOutput, calls=%fused_computation.3 | convolution fusion | flops 2148007936 | bytes 10485760 | tf_op jit(solution)/shard_map/td,dhe->hte/dot_general | solution.py:273
  65.5 4.1 %shard_map.85 = (bf16[16,16,8,128]{3,2,1,0:T(8,128)(2,1)S(1)}, bf16[16,16,8,128]{3,2,1,0:T(8,128)(2,1)}, bf16[16,3,16,2,8,128]{5,4,3,2,1,0:T(8,128)(2,1)}) custom-call(bf16[16,4,16,2,8,128]{5,4,3,2,1,0:T(8,128)(2,1)S(1)} %bitcast.26, bf16[16,256,128]{2,1,0:T(8,128)(2,1)S(1)} %fusion.5.mat_ref), custom_call_target="tpu_custom_call" | custom-call | flops 7000000000 | bytes 8388608 | tf_op jit(solution)/shard_map/pallas_call | solution.py:135
  69.6 1.2 collective-permute-start
  70.8 0.1 collective-permute-start.1
  70.9 4.6 %all-to-all-start.1 = ((bf16[16,3,16,2,8,128]{5,4,3,2,1,0:T(8,128)(2,1)}), bf16[16,3,16,2,8,128]{5,4,3,2,1,0:T(8,128)(2,1)}, u32[]{:S(2)}, u32[]{:S(2)}) async-start(bf16[16,3,16,2,8,128]{5,4,3,2,1,0:T(8,128)(2,1)} %get-tuple-element.35), calls=%async_computation.1 | async-start | bytes 6291456 | tf_op jit(solution)/shard_map/all_to_all | solution.py:281
  75.6 0.0 collective-permute-done.1
  75.6 0.0 collective-permute-done.refs_1_
  75.6 0.8 shard_map.86
  76.3 1.4 collective-permute-start.4
  77.7 1.5 %collective-permute-start.5 = (bf16[512,512]{1,0:T(8,128)(2,1)S(1)}, bf16[512,512]{1,0:T(8,128)(2,1)S(1)}, u32[]{:S(2)}, u32[]{:S(2)}) collective-permute-start(bf16[512,512]{1,0:T(8,128)(2,1)S(1)} %get-tuple-element.32), channel_id=1, source_target_pairs={{0,96},{1,97},{2,98},{3,99},{4,100},{5,101},{6,102},{7,103},{8,104... | collective-permute-start | bytes 1572872 | tf_op jit(solution)/shard_map/ppermute | solution.py:293
  79.2 0.8 shard_map.87
  80.0 1.5 %collective-permute-start.2 = (bf16[512,512]{1,0:T(8,128)(2,1)S(1)}, bf16[512,512]{1,0:T(8,128)(2,1)S(1)}, u32[]{:S(2)}, u32[]{:S(2)}) collective-permute-start(bf16[512,512]{1,0:T(8,128)(2,1)S(1)} %get-tuple-element.27), channel_id=1, source_target_pairs={{0,96},{1,97},{2,98},{3,99},{4,100},{5,101},{6,102},{7,103},{8,104... | collective-permute-start | bytes 1572872 | tf_op jit(solution)/shard_map/ppermute | solution.py:296
  81.4 0.1 collective-permute-start.3
  81.5 9.6 %collective-permute-done.4.refs_4_ = bf16[512,512]{1,0:T(8,128)(2,1)S(1)} collective-permute-done((bf16[512,512]{1,0:T(8,128)(2,1)S(1)}, bf16[512,512]{1,0:T(8,128)(2,1)S(1)}, u32[]{:S(2)}, u32[]{:S(2)}) %collective-permute-start.4) | collective-permute-done | bytes 524320 | tf_op jit(solution)/shard_map/ppermute | solution.py:292
  91.1 0.0 collective-permute-done.5.refs_5_
  91.1 0.8 shard_map.89
  91.9 1.0 collective-permute-start.6
  92.9 1.8 %collective-permute-start.7 = (bf16[512,512]{1,0:T(8,128)(2,1)S(1)}, bf16[512,512]{1,0:T(8,128)(2,1)S(1)}, u32[]{:S(2)}, u32[]{:S(2)}) collective-permute-start(bf16[512,512]{1,0:T(8,128)(2,1)S(1)} %get-tuple-element.34), channel_id=1, source_target_pairs={{0,96},{1,97},{2,98},{3,99},{4,100},{5,101},{6,102},{7,103},{8,104... | collective-permute-start | bytes 1572872 | tf_op jit(solution)/shard_map/ppermute | solution.py:299
  94.6 7.3 %collective-permute-done.2.refs_4_ = bf16[512,512]{1,0:T(8,128)(2,1)S(1)} collective-permute-done((bf16[512,512]{1,0:T(8,128)(2,1)S(1)}, bf16[512,512]{1,0:T(8,128)(2,1)S(1)}, u32[]{:S(2)}, u32[]{:S(2)}) %collective-permute-start.2) | collective-permute-done | bytes 524320 | tf_op jit(solution)/shard_map/ppermute | solution.py:296
  102.0 0.4 collective-permute-done.3.refs_5_
  102.3 0.8 shard_map.88
  103.1 10.5 %collective-permute-done.6.came0 = bf16[512,512]{1,0:T(8,128)(2,1)S(1)} collective-permute-done((bf16[512,512]{1,0:T(8,128)(2,1)S(1)}, bf16[512,512]{1,0:T(8,128)(2,1)S(1)}, u32[]{:S(2)}, u32[]{:S(2)}) %collective-permute-start.6) | collective-permute-done | bytes 524320 | tf_op jit(solution)/shard_map/ppermute | solution.py:298
  113.6 0.0 collective-permute-done.7.came1
  113.6 1.1 shard_map.90
  114.6 0.9 all-to-all-done.1
  115.5 7.2 %all-to-all-start.2 = ((bf16[32,16,1024]{2,1,0:T(8,128)(2,1)}), bf16[32,16,1024]{2,1,0:T(8,128)(2,1)S(1)}, u32[]{:S(2)}, u32[]{:S(2)}) async-start(bf16[32,16,1024]{2,1,0:T(8,128)(2,1)} %bitcast.36), calls=%async_computation.2 | async-start | bytes 2097152 | tf_op jit(solution)/shard_map/all_to_all | solution.py:304
  122.7 4.0 %fusion.8 = (bf16[16,1,16,2,8,128]{5,4,3,2,1,0:T(8,128)(2,1)}, bf16[16,1,16,2,8,128]{5,4,3,2,1,0:T(8,128)(2,1)}, bf16[16,1,16,2,8,128]{5,4,3,2,1,0:T(8,128)(2,1)}) fusion(bf16[16,3,16,2,8,128]{5,4,3,2,1,0:T(8,128)(2,1)} %all-to-all-done.1), kind=kLoop, calls=%fused_computation.4 | loop fusion | bytes 6291456 | tf_op jit(solution)/shard_map/slice | solution.py:308
  126.7 13.1 %all-to-all-done.2 = bf16[32,16,1024]{2,1,0:T(8,128)(2,1)S(1)} async-done(((bf16[32,16,1024]{2,1,0:T(8,128)(2,1)}), bf16[32,16,1024]{2,1,0:T(8,128)(2,1)S(1)}, u32[]{:S(2)}, u32[]{:S(2)}) %all-to-all-start.2) | async-done | bytes 1048608 | tf_op jit(solution)/shard_map/all_to_all | solution.py:304
  139.8 0.9 shard_map.91
  (1 shorter events, 0.0 us)
Async XLA Ops:
  0.6 62.5 %slice-start = ((s8[8388608]{0:T(1024)(128)(4,1)}), s8[4194304]{0:T(1024)(128)(4,1)S(1)}, s32[]{:S(2)}) async-start(s8[8388608]{0:T(1024)(128)(4,1)} %bitcast.44), calls=%async_computation.3 | async-start | bytes 8388608
  3.0 60.1 %slice-start.1 = ((s8[8388608]{0:T(1024)(128)(4,1)}), s8[4194304]{0:T(1024)(128)(4,1)S(1)}, s32[]{:S(2)}) async-start(s8[8388608]{0:T(1024)(128)(4,1)} %bitcast.44), calls=%async_computation.4 | async-start | bytes 8388608
  69.6 6.0 %collective-permute-start = (bf16[256,2048]{1,0:T(8,128)(2,1)S(1)}, bf16[256,2048]{1,0:T(8,128)(2,1)S(1)}, u32[]{:S(2)}, u32[]{:S(2)}) collective-permute-start(bf16[256,2048]{1,0:T(8,128)(2,1)S(1)} %bitcast.29), channel_id=1, source_target_pairs={{0,1},{1,0},{2,3},{3,2},{4,5},{5,4},{6,7},{7,6},{8,9},{9,8},{10,11... | collective-permute-start | bytes 3145736 | tf_op jit(solution)/shard_map/ppermute | solution.py:285
  70.8 4.7 %collective-permute-start.1 = (bf16[16,16,8,128]{3,2,1,0:T(8,128)(2,1)}, bf16[16,16,8,128]{3,2,1,0:T(8,128)(2,1)S(1)}, u32[]{:S(2)}, u32[]{:S(2)}) collective-permute-start(bf16[16,16,8,128]{3,2,1,0:T(8,128)(2,1)} %get-tuple-element.24), channel_id=1, source_target_pairs={{0,1},{1,0},{2,3},{3,2},{4,5},{5,4},{6,7},{7,6},{8,9},{9,8},{10,11... | collective-permute-start | bytes 1572872 | tf_op jit(solution)/shard_map/ppermute | solution.py:286
  70.9 44.6 %all-to-all-start.1 = ((bf16[16,3,16,2,8,128]{5,4,3,2,1,0:T(8,128)(2,1)}), bf16[16,3,16,2,8,128]{5,4,3,2,1,0:T(8,128)(2,1)}, u32[]{:S(2)}, u32[]{:S(2)}) async-start(bf16[16,3,16,2,8,128]{5,4,3,2,1,0:T(8,128)(2,1)} %get-tuple-element.35), calls=%async_computation.1 | async-start | bytes 6291456 | tf_op jit(solution)/shard_map/all_to_all | solution.py:281
  76.3 14.7 %collective-permute-start.4 = (bf16[512,512]{1,0:T(8,128)(2,1)S(1)}, bf16[512,512]{1,0:T(8,128)(2,1)S(1)}, u32[]{:S(2)}, u32[]{:S(2)}) collective-permute-start(bf16[512,512]{1,0:T(8,128)(2,1)S(1)} %get-tuple-element.31), channel_id=1, source_target_pairs={{0,32},{1,33},{2,34},{3,35},{4,36},{5,37},{6,38},{7,39},{8,40},{9,... | collective-permute-start | bytes 1572872 | tf_op jit(solution)/shard_map/ppermute | solution.py:292
  77.7 13.4 %collective-permute-start.5 = (bf16[512,512]{1,0:T(8,128)(2,1)S(1)}, bf16[512,512]{1,0:T(8,128)(2,1)S(1)}, u32[]{:S(2)}, u32[]{:S(2)}) collective-permute-start(bf16[512,512]{1,0:T(8,128)(2,1)S(1)} %get-tuple-element.32), channel_id=1, source_target_pairs={{0,96},{1,97},{2,98},{3,99},{4,100},{5,101},{6,102},{7,103},{8,104... | collective-permute-start | bytes 1572872 | tf_op jit(solution)/shard_map/ppermute | solution.py:293
  80.0 22.0 %collective-permute-start.2 = (bf16[512,512]{1,0:T(8,128)(2,1)S(1)}, bf16[512,512]{1,0:T(8,128)(2,1)S(1)}, u32[]{:S(2)}, u32[]{:S(2)}) collective-permute-start(bf16[512,512]{1,0:T(8,128)(2,1)S(1)} %get-tuple-element.27), channel_id=1, source_target_pairs={{0,96},{1,97},{2,98},{3,99},{4,100},{5,101},{6,102},{7,103},{8,104... | collective-permute-start | bytes 1572872 | tf_op jit(solution)/shard_map/ppermute | solution.py:296
  81.4 20.9 %collective-permute-start.3 = (bf16[512,512]{1,0:T(8,128)(2,1)S(1)}, bf16[512,512]{1,0:T(8,128)(2,1)S(1)}, u32[]{:S(2)}, u32[]{:S(2)}) collective-permute-start(bf16[512,512]{1,0:T(8,128)(2,1)S(1)} %get-tuple-element.28), channel_id=1, source_target_pairs={{0,32},{1,33},{2,34},{3,35},{4,36},{5,37},{6,38},{7,39},{8,40},{9,... | collective-permute-start | bytes 1572872 | tf_op jit(solution)/shard_map/ppermute | solution.py:295
  91.9 21.7 %collective-permute-start.6 = (bf16[512,512]{1,0:T(8,128)(2,1)S(1)}, bf16[512,512]{1,0:T(8,128)(2,1)S(1)}, u32[]{:S(2)}, u32[]{:S(2)}) collective-permute-start(bf16[512,512]{1,0:T(8,128)(2,1)S(1)} %get-tuple-element.33), channel_id=1, source_target_pairs={{0,32},{1,33},{2,34},{3,35},{4,36},{5,37},{6,38},{7,39},{8,40},{9,... | collective-permute-start | bytes 1572872 | tf_op jit(solution)/shard_map/ppermute | solution.py:298
  92.9 20.7 %collective-permute-start.7 = (bf16[512,512]{1,0:T(8,128)(2,1)S(1)}, bf16[512,512]{1,0:T(8,128)(2,1)S(1)}, u32[]{:S(2)}, u32[]{:S(2)}) collective-permute-start(bf16[512,512]{1,0:T(8,128)(2,1)S(1)} %get-tuple-element.34), channel_id=1, source_target_pairs={{0,96},{1,97},{2,98},{3,99},{4,100},{5,101},{6,102},{7,103},{8,104... | collective-permute-start | bytes 1572872 | tf_op jit(solution)/shard_map/ppermute | solution.py:299
  115.5 24.3 %all-to-all-start.2 = ((bf16[32,16,1024]{2,1,0:T(8,128)(2,1)}), bf16[32,16,1024]{2,1,0:T(8,128)(2,1)S(1)}, u32[]{:S(2)}, u32[]{:S(2)}) async-start(bf16[32,16,1024]{2,1,0:T(8,128)(2,1)} %bitcast.36), calls=%async_computation.2 | async-start | bytes 2097152 | tf_op jit(solution)/shard_map/all_to_all | solution.py:304
